TPU v7x, 32 devices: a whole 2x2x4 slice. The times are simulated.
32 devices in a mesh: dp: 8 (over z, y), tier: 2 (over core), head: 2 (over x).
Axes of the slice: x: 2, y: 2, z: 4, core: 2. Of those that a mesh axis runs over, the one named last changes fastest.
Arguments:
- segment_input: bfloat16 [24, 512, 1024], P('dp', 'tier'), may hold values from -6 to 6
- memory: bfloat16 [24, 512, 1024], P('dp', 'tier'), may hold values from -6 to 6
- compressed: bfloat16 [24, 384, 1024], P('dp', 'tier'), may hold values from -6 to 6
- evicted: bfloat16 [24, 384, 1024], P('dp', 'tier'), may hold values from -6 to 6
- cotangent: bfloat16 [24, 512, 1024], P('dp', 'tier'), may hold values from -6 to 6
- seg_lengths: int32 [24], P('dp'), may hold values from 128 to 512, as said below
- memory_fills: int32 [24], P('dp'), may hold values from 0 to 512, as said below
- compressed_fills: int32 [24], P('dp'), may hold values from 1 to 512, as said below
- conv_weight: bfloat16 [3, 1024, 1024], P(None, ('dp', 'tier'), 'head'), may hold values from -0.109375 to 0.109375
- conv_bias: float32 [1024], P('head'), may hold values from -1.75 to 1.75
- norm1_gain: float32 [1024], replicated, may hold values from 0.5 to 1.5
- norm1_bias: float32 [1024], replicated, may hold values from -1.25 to 1.25
- query_weight: bfloat16 [1024, 1024], P(('dp', 'tier'), 'head'), may hold values from -0.1875 to 0.1875
- key_weight: bfloat16 [1024, 1024], P(('dp', 'tier'), 'head'), may hold values from -0.1875 to 0.1875
- value_weight: bfloat16 [1024, 1024], P(('dp', 'tier'), 'head'), may hold values from -0.1875 to 0.1875
- position_weight: bfloat16 [1024, 1024], P(('dp', 'tier'), 'head'), may hold values from -0.1875 to 0.1875
- content_bias: float32 [8, 128], P('head'), may hold values from -3 to 3
- position_bias: float32 [8, 128], P('head'), may hold values from -3 to 3
- out_weight: bfloat16 [1024, 1024], P('head', ('dp', 'tier')), may hold values from -2 to 2
- norm2_gain: float32 [1024], replicated, may hold values from 0.5 to 1.5
- norm2_bias: float32 [1024], replicated, may hold values from -1.25 to 1.25
- up_weight: bfloat16 [1024, 4096], P(('dp', 'tier'), 'head'), may hold values from -0.1875 to 0.1875
- up_bias: float32 [4096], P('head'), may hold values from -1.75 to 1.75
- down_weight: bfloat16 [4096, 1024], P('head', ('dp', 'tier')), may hold values from -0.09375 to 0.09375
- down_bias: float32 [1024], replicated, may hold values from -1.75 to 1.75
Outputs:
- output: bfloat16 [24, 512, 1024], P('dp', 'tier')
- grad_input: float32 [24, 512, 1024], P('dp', 'tier')
- grad_compressed: float32 [24, 384, 1024], P('dp', 'tier')
- grad_conv_weight: float32 [3, 1024, 1024], P(None, ('dp', 'tier'), 'head')
- grad_conv_bias: float32 [1024], P('head')
- grad_norm1_gain: float32 [1024], replicated
- grad_norm1_bias: float32 [1024], replicated
- grad_query_weight: float32 [1024, 1024], P(('dp', 'tier'), 'head')
- grad_key_weight: float32 [1024, 1024], P(('dp', 'tier'), 'head')
- grad_value_weight: float32 [1024, 1024], P(('dp', 'tier'), 'head')
- grad_position_weight: float32 [1024, 1024], P(('dp', 'tier'), 'head')
- grad_content_bias: float32 [8, 128], P('head')
- grad_position_bias: float32 [8, 128], P('head')
- grad_out_weight: float32 [1024, 1024], P('head', ('dp', 'tier'))
- grad_norm2_gain: float32 [1024], replicated
- grad_norm2_bias: float32 [1024], replicated
- grad_up_weight: float32 [1024, 4096], P(('dp', 'tier'), 'head')
- grad_up_bias: float32 [4096], P('head')
- grad_down_weight: float32 [4096, 1024], P('head', ('dp', 'tier'))
- grad_down_bias: float32 [1024], replicated
Inputs may be any that keep to these rules, and one draw needn't show every extreme that they name: `seg_lengths`: tokens of a stream's segment that are real; later positions are padding. `memory_fills`: how many of a stream's newest memory rows hold data; older ones are empty. `compressed_fills`: how many of a stream's newest compressed rows (the 128 fresh ones last) hold data.
All inputs are finite; a program needn't handle non-finite values.
Results may differ from a plain program's by a relative error of at most 0.035.
Values may be sent and summed in bfloat16 or wider, within the bound.
No kernel may reach another device: no remote copies, remote signals or barrier semaphores. Data moves between devices by JAX's collectives and lax.ppermute only.
A program may use at most 160 MiB of HBM per device.

v0:
```python
import math

import jax
import jax.numpy as jnp
from jax import lax
from jax.sharding import PartitionSpec as P

D = 1024
MEM = 512
CMEM = 512
KW = 3
MB = 3
OLDC = 384


norm_eps = 1e-05
neg_fill = -1e30


def combined_all(array, axis, combine):
    everything = lax.all_gather(array, axis)
    leading = everything[0]

    def step(k, so_far):
        return combine(so_far, everything[k])

    return lax.fori_loop(1, lax.axis_size(axis), step, leading)


def smooth_gate(values_in):
    return jax.nn.gelu(values_in, approximate=True)


def layer_norm(row_vals, gain_vec, shift_vec):
    row_mean = jnp.mean(row_vals, axis=-1, keepdims=True)
    centred = row_vals - row_mean
    row_var = jnp.mean(centred * centred, axis=-1, keepdims=True)
    return centred * lax.rsqrt(row_var + norm_eps) * gain_vec + shift_vec


def sin_cos(positions):
    half_width = D // 2
    frequency = jnp.exp(jnp.arange(half_width, dtype=jnp.float32) * (-2.0 * math.log(10000.0) / D))
    turned = positions.astype(jnp.float32)[:, None] * frequency[None, :]
    return (jnp.sin(turned), jnp.cos(turned))


def rotate(amplitude, sin_rows, cos_rows):
    half_width = amplitude.shape[-1] // 2
    sin_part = amplitude[..., :half_width]
    cos_part = amplitude[..., half_width:]
    return jnp.concatenate(
        [sin_part * sin_rows + cos_part * cos_rows, cos_part * sin_rows - sin_part * cos_rows],
        axis=-1,
    )


def unrotate(grad_rot, sin_rows, cos_rows):
    half_width = grad_rot.shape[-1] // 2
    grad_first = grad_rot[..., :half_width]
    grad_second = grad_rot[..., half_width:]
    return jnp.concatenate(
        [
            grad_first * sin_rows - grad_second * cos_rows,
            grad_first * cos_rows + grad_second * sin_rows,
        ],
        axis=-1,
    )


def key_valid(key_pos, query_pos, seg_len, mem_fill, comp_fill):
    query_start = CMEM + MEM
    in_comp = key_pos < CMEM
    in_memory = key_pos < query_start
    comp_ok = key_pos >= CMEM - comp_fill
    memory_ok = key_pos >= query_start - mem_fill
    seg_index = key_pos - query_start
    seg_ok = (seg_index < seg_len) & (seg_index <= query_pos[:, None])
    return jnp.where(in_comp, comp_ok, jnp.where(in_memory, memory_ok, seg_ok))


def merge_lse(left_lse, right_lse):
    larger = jnp.maximum(left_lse, right_lse)
    return larger + jnp.log(jnp.exp(left_lse - larger) + jnp.exp(right_lse - larger))


def add_tuples(left_set, right_set):
    return tuple((left_item + right_item for left_item, right_item in zip(left_set, right_set)))


def fetch_weights(conv_w, query_w, key_matrix, value_matrix, pos_w, out_w, up_w, down_w):
    return (
        lax.all_gather(conv_w, ("dp", "tier"), axis=1, tiled=True),
        lax.all_gather(query_w, ("dp", "tier"), axis=0, tiled=True),
        lax.all_gather(key_matrix, ("dp", "tier"), axis=0, tiled=True),
        lax.all_gather(value_matrix, ("dp", "tier"), axis=0, tiled=True),
        lax.all_gather(pos_w, ("dp", "tier"), axis=0, tiled=True),
        lax.all_gather(out_w, ("dp", "tier"), axis=1, tiled=True),
        lax.all_gather(up_w, ("dp", "tier"), axis=0, tiled=True),
        lax.all_gather(down_w, ("dp", "tier"), axis=1, tiled=True),
    )


def return_grads(grads):
    return (
        lax.psum_scatter(
            grads[0].astype(jnp.bfloat16), ("dp", "tier"), scatter_dimension=1, tiled=True
        ).astype(jnp.float32),
        lax.psum_scatter(
            grads[1].astype(jnp.bfloat16), ("dp", "tier"), scatter_dimension=0, tiled=True
        ).astype(jnp.float32),
        lax.psum_scatter(
            grads[2].astype(jnp.bfloat16), ("dp", "tier"), scatter_dimension=0, tiled=True
        ).astype(jnp.float32),
        lax.psum_scatter(
            grads[3].astype(jnp.bfloat16), ("dp", "tier"), scatter_dimension=0, tiled=True
        ).astype(jnp.float32),
        lax.psum_scatter(
            grads[4].astype(jnp.bfloat16), ("dp", "tier"), scatter_dimension=0, tiled=True
        ).astype(jnp.float32),
        lax.psum_scatter(
            grads[5].astype(jnp.bfloat16), ("dp", "tier"), scatter_dimension=1, tiled=True
        ).astype(jnp.float32),
        lax.psum_scatter(
            grads[6].astype(jnp.bfloat16), ("dp", "tier"), scatter_dimension=0, tiled=True
        ).astype(jnp.float32),
        lax.psum_scatter(
            grads[7].astype(jnp.bfloat16), ("dp", "tier"), scatter_dimension=1, tiled=True
        ).astype(jnp.float32),
    )


def micro_batch(gathered, small_params, batch_data, tier_index, head_index):
    conv_w, query_w, key_matrix, value_matrix, pos_w, out_w, up_w, down_w = gathered
    conv_b, gain_one, shift_one, content_b, pos_b, gain_two, shift_two, up_b, down_b = small_params
    input_rows, memory_rows, comp_rows, evicted_rows, cot_rows, seg_len, mem_fill, comp_fill = (
        batch_data
    )
    single_sequence = jnp.float32
    brain = jnp.bfloat16
    highest = lax.Precision.HIGHEST
    streams = input_rows.shape[0]
    seg_half = input_rows.shape[1]
    mem_half = memory_rows.shape[1]
    comp_half = comp_rows.shape[1]
    group_count = evicted_rows.shape[1] // KW
    width_local = conv_w.shape[2]
    local_heads = content_b.shape[0]
    head_dim = content_b.shape[1]
    proj_width = local_heads * head_dim
    scale_factor = 1.0 / math.sqrt(head_dim)
    tier_count = lax.axis_size("tier")
    query_full = seg_half * tier_count
    query_start = CMEM + MEM
    comp_pos = tier_index * comp_half + jnp.arange(comp_half, dtype=jnp.int32)
    fresh_pos = OLDC + tier_index * group_count + jnp.arange(group_count, dtype=jnp.int32)
    memory_pos = CMEM + tier_index * mem_half + jnp.arange(mem_half, dtype=jnp.int32)
    own_seg = tier_index * seg_half + jnp.arange(seg_half, dtype=jnp.int32)
    key_pos = jnp.concatenate([comp_pos, fresh_pos, memory_pos, query_start + own_seg])
    query_pos = jnp.arange(query_full, dtype=jnp.int32)
    grouped = evicted_rows.reshape(streams, group_count, KW * D)
    conv_flat = conv_w.reshape(KW * D, width_local)
    fresh_cols = (
        jnp.einsum("bgc,cd->bgd", grouped, conv_flat, preferred_element_type=single_sequence)
        + conv_b
    ).astype(brain)
    fresh_full = lax.all_gather(fresh_cols, "head", axis=2, tiled=True)
    context = jnp.concatenate([comp_rows, fresh_full, memory_rows, input_rows], axis=1).astype(
        single_sequence
    )
    key_count = context.shape[1]
    normed, norm_pull_one = jax.vjp(layer_norm, context, gain_one, shift_one)
    normed_lowprec = normed.astype(brain)
    own_queries = normed_lowprec[:, key_count - seg_half :]
    query_part = jnp.einsum(
        "brd,de->bre", own_queries, query_w, preferred_element_type=single_sequence
    ).astype(brain)
    query_all = lax.all_gather(query_part, "tier", axis=1, tiled=True)
    key_projection = jnp.einsum(
        "ary,yn->arn", normed_lowprec, key_matrix, preferred_element_type=single_sequence
    ).astype(brain)
    value_proj = jnp.einsum(
        "ary,yn->arn", normed_lowprec, value_matrix, preferred_element_type=single_sequence
    ).astype(brain)
    query_float = query_all.astype(single_sequence)
    with_content = (query_float + content_b.reshape(proj_width)).astype(brain)
    with_pos = (query_float + pos_b.reshape(proj_width)).astype(brain)
    content_heads = with_content.reshape(streams, query_full, local_heads, head_dim)
    position_heads = with_pos.reshape(streams, query_full, local_heads, head_dim)
    key_heads = key_projection.reshape(streams, key_count, local_heads, head_dim)
    value_heads = value_proj.reshape(streams, key_count, local_heads, head_dim)
    pos_matrix = pos_w.reshape(D, local_heads, head_dim)
    amplitude = jnp.einsum(
        "bihe,fhe->bhif", position_heads, pos_matrix, preferred_element_type=single_sequence
    )
    sin_query, cos_query = sin_cos(query_pos + query_start)
    sin_key, cos_key = sin_cos(key_pos)
    rotated = rotate(amplitude, sin_query, cos_query).astype(brain)
    key_table = jnp.concatenate([cos_key, sin_key], axis=-1).astype(brain)
    allowed = key_valid(
        key_pos,
        query_pos,
        seg_len[:, None, None],
        mem_fill[:, None, None],
        comp_fill[:, None, None],
    )

    def score_block():
        content = jnp.einsum(
            "bihe,bjhe->bhij", content_heads, key_heads, preferred_element_type=single_sequence
        )
        relative = jnp.einsum(
            "bhif,jf->bhij", rotated, key_table, preferred_element_type=single_sequence
        )
        raw_scores = (content + relative) * scale_factor
        return jnp.where(allowed[:, None], raw_scores, neg_fill)

    masked = score_block()
    row_peak = jnp.max(masked, axis=-1)
    row_total = jnp.sum(jnp.exp(masked - row_peak[..., None]), axis=-1)
    local_lse = row_peak + jnp.log(row_total)
    global_lse = combined_all(local_lse, "tier", merge_lse)
    probs_now = jnp.exp(masked - global_lse[..., None])
    attended_part = jnp.einsum(
        "bhij,bjhe->bihe",
        probs_now.astype(brain),
        value_heads,
        preferred_element_type=single_sequence,
    ).reshape(streams, query_full, proj_width)
    attended = lax.psum(attended_part.astype(jnp.bfloat16), "tier").astype(jnp.float32)
    row_start = tier_index * seg_half
    attended_low = attended.astype(brain)
    own_attended = lax.dynamic_slice_in_dim(attended_low, row_start, seg_half, 1)
    branch_part = jnp.einsum(
        "bre,ed->brd", own_attended, out_w, preferred_element_type=single_sequence
    )
    branch = lax.psum(branch_part.astype(jnp.bfloat16), "head").astype(jnp.float32)
    hidden_one = input_rows.astype(single_sequence) + branch
    normed_two, norm_pull_two = jax.vjp(layer_norm, hidden_one, gain_two, shift_two)
    normed_two_low = normed_two.astype(brain)
    pre_act = (
        jnp.einsum("brd,df->brf", normed_two_low, up_w, preferred_element_type=single_sequence)
        + up_b
    )
    activated_float, gate_pull = jax.vjp(smooth_gate, pre_act)
    activated = activated_float.astype(brain)
    ffn_part = jnp.einsum("brf,fd->brd", activated, down_w, preferred_element_type=single_sequence)
    ffn_out = lax.psum(ffn_part.astype(jnp.bfloat16), "head").astype(jnp.float32) + down_b
    output = (hidden_one + ffn_out).astype(brain)
    live_rows = (own_seg[None, :] < seg_len[:, None]).astype(single_sequence)
    grad_out = (cot_rows.astype(single_sequence) * live_rows[:, :, None]).astype(brain)
    grad_down_b = jnp.sum(grad_out.astype(single_sequence), axis=(0, 1))
    grad_down_w = jnp.einsum(
        "brf,brd->fd", activated, grad_out, preferred_element_type=single_sequence
    )
    grad_act = jnp.einsum("brd,fd->brf", grad_out, down_w, preferred_element_type=single_sequence)
    grad_pre = gate_pull(grad_act)[0].astype(brain)
    grad_up_b = jnp.sum(grad_pre.astype(single_sequence), axis=(0, 1))
    grad_up_w = jnp.einsum(
        "brd,brf->df", normed_two_low, grad_pre, preferred_element_type=single_sequence
    )
    grad_norm_part = jnp.einsum(
        "brf,df->brd", grad_pre, up_w, preferred_element_type=single_sequence
    )
    grad_norm_two = lax.psum(grad_norm_part.astype(jnp.bfloat16), "head").astype(jnp.float32)
    grad_hidden_ln, grad_gain_two, grad_shift_two = norm_pull_two(grad_norm_two)
    grad_hidden = grad_out.astype(single_sequence) + grad_hidden_ln
    grad_branch = grad_hidden.astype(brain)
    grad_out_w = jnp.einsum(
        "bre,brd->ed", own_attended, grad_branch, preferred_element_type=single_sequence
    )
    grad_att_own = jnp.einsum(
        "brd,ed->bre", grad_branch, out_w, preferred_element_type=single_sequence
    ).astype(brain)
    grad_att = lax.all_gather(grad_att_own, "tier", axis=1, tiled=True)
    grad_att_heads = grad_att.reshape(streams, query_full, local_heads, head_dim)
    attended_heads = attended.reshape(streams, query_full, local_heads, head_dim)
    row_dot = jnp.transpose(
        jnp.sum(grad_att_heads.astype(single_sequence) * attended_heads, axis=-1), (0, 2, 1)
    )
    masked_again = score_block()
    probs_again = jnp.exp(masked_again - global_lse[..., None])
    grad_probs = jnp.einsum(
        "bihe,bjhe->bhij", grad_att_heads, value_heads, preferred_element_type=single_sequence
    )
    grad_scores = (probs_again * (grad_probs - row_dot[..., None])).astype(brain)
    grad_values = jnp.einsum(
        "bhij,bihe->bjhe",
        probs_again.astype(brain),
        grad_att_heads,
        preferred_element_type=single_sequence,
    )
    grad_keys = (
        jnp.einsum(
            "bhij,bihe->bjhe", grad_scores, content_heads, preferred_element_type=single_sequence
        )
        * scale_factor
    )
    grad_content_part = (
        jnp.einsum(
            "bhij,bjhe->bihe", grad_scores, key_heads, preferred_element_type=single_sequence
        )
        * scale_factor
    )
    grad_rotated = (
        jnp.einsum("bhij,jf->bhif", grad_scores, key_table, preferred_element_type=single_sequence)
        * scale_factor
    )
    grad_amp_part = unrotate(grad_rotated, sin_query, cos_query)
    pos_float = pos_matrix.astype(single_sequence)
    grad_content_own, grad_amp_own = (
        lax.psum_scatter(
            grad_content_part.reshape(streams, query_full, proj_width).astype(jnp.bfloat16),
            "tier",
            scatter_dimension=1,
            tiled=True,
        ).astype(jnp.float32),
        lax.psum_scatter(
            grad_amp_part.astype(jnp.bfloat16), "tier", scatter_dimension=2, tiled=True
        ).astype(jnp.float32),
    )
    own_pos_heads = lax.dynamic_slice_in_dim(position_heads, row_start, seg_half, 1).astype(
        single_sequence
    )
    grad_pos_w = jnp.einsum(
        "bhif,bihe->fhe",
        grad_amp_own,
        own_pos_heads,
        precision=highest,
        preferred_element_type=single_sequence,
    ).reshape(D, proj_width)
    grad_with_pos = jnp.einsum(
        "bhif,fhe->bihe",
        grad_amp_own,
        pos_float,
        precision=highest,
        preferred_element_type=single_sequence,
    ).reshape(streams, seg_half, proj_width)
    grad_content_b = jnp.sum(grad_content_own, axis=(0, 1)).reshape(local_heads, head_dim)
    grad_pos_b = jnp.sum(grad_with_pos, axis=(0, 1)).reshape(local_heads, head_dim)
    grad_queries = (grad_content_own + grad_with_pos).astype(brain)
    grad_query_w = jnp.einsum(
        "brd,bre->de", own_queries, grad_queries, preferred_element_type=single_sequence
    )
    grad_own_norm = jnp.einsum(
        "bre,de->brd", grad_queries, query_w, preferred_element_type=single_sequence
    )
    keys_gradient_lowprec = grad_keys.reshape(streams, key_count, proj_width).astype(brain)
    values_gradient_lowprec = grad_values.reshape(streams, key_count, proj_width).astype(brain)
    key_matrix_grad = jnp.einsum(
        "grm,grs->ms", normed_lowprec, keys_gradient_lowprec, preferred_element_type=single_sequence
    )
    grad_value_w = jnp.einsum(
        "grm,grs->ms",
        normed_lowprec,
        values_gradient_lowprec,
        preferred_element_type=single_sequence,
    )
    grad_normed_part = jnp.einsum(
        "mxv,lv->mxl", keys_gradient_lowprec, key_matrix, preferred_element_type=single_sequence
    ) + jnp.einsum(
        "mxv,lv->mxl", values_gradient_lowprec, value_matrix, preferred_element_type=single_sequence
    )
    split_at = key_count - seg_half
    grad_normed_part = jnp.concatenate(
        [grad_normed_part[:, :split_at], grad_normed_part[:, split_at:] + grad_own_norm], axis=1
    )
    grad_normed = lax.psum(grad_normed_part.astype(jnp.bfloat16), "head").astype(jnp.float32)
    grad_context, grad_gain_one, grad_shift_one = norm_pull_one(grad_normed)
    grad_comp = grad_context[:, :comp_half]
    grad_fresh = grad_context[:, comp_half : comp_half + group_count]
    grad_in = grad_hidden + grad_context[:, split_at:]
    fresh_own = lax.dynamic_slice_in_dim(
        grad_fresh, head_index * width_local, width_local, 2
    ).astype(brain)
    grad_conv_b = jnp.sum(fresh_own.astype(single_sequence), axis=(0, 1))
    grad_conv_w = jnp.einsum(
        "bgc,bgd->cd", grouped, fresh_own, preferred_element_type=single_sequence
    ).reshape(KW, D, width_local)
    full_grads = (
        grad_conv_w,
        grad_query_w,
        key_matrix_grad,
        grad_value_w,
        grad_pos_w,
        grad_out_w,
        grad_up_w,
        grad_down_w,
    )
    small_grads = (
        grad_conv_b,
        grad_gain_one,
        grad_shift_one,
        grad_content_b,
        grad_pos_b,
        grad_gain_two,
        grad_shift_two,
        grad_up_b,
        grad_down_b,
    )
    return (full_grads, small_grads, (output, grad_in, grad_comp))


def shards(
    segment_input,
    memory,
    compressed,
    evicted,
    cotangent,
    seg_lengths,
    memory_fills,
    compressed_fills,
    conv_weight,
    conv_bias,
    norm1_gain,
    norm1_bias,
    query_weight,
    key_weight,
    value_weight,
    position_weight,
    content_bias,
    position_bias,
    out_weight,
    norm2_gain,
    norm2_bias,
    up_weight,
    up_bias,
    down_weight,
    down_bias,
):
    tier_index = lax.axis_index("tier")
    head_index = lax.axis_index("head")
    per_batch = segment_input.shape[0] // MB
    small_params = (
        conv_bias,
        norm1_gain,
        norm1_bias,
        content_bias,
        position_bias,
        norm2_gain,
        norm2_bias,
        up_bias,
        down_bias,
    )
    small_total = tuple((jnp.zeros(param_item.shape, jnp.float32) for param_item in small_params))
    out_rows = []
    grad_in_rows = []
    grad_comp_rows = []
    shard_total = tuple(
        (
            jnp.zeros(param_item.shape, jnp.float32)
            for param_item in (
                conv_weight,
                query_weight,
                key_weight,
                value_weight,
                position_weight,
                out_weight,
                up_weight,
                down_weight,
            )
        )
    )
    for batch_index in range(MB):
        gathered = fetch_weights(
            conv_weight,
            query_weight,
            key_weight,
            value_weight,
            position_weight,
            out_weight,
            up_weight,
            down_weight,
        )
        low_end = batch_index * per_batch
        high_end = low_end + per_batch
        batch_data = (
            segment_input[low_end:high_end],
            memory[low_end:high_end],
            compressed[low_end:high_end],
            evicted[low_end:high_end],
            cotangent[low_end:high_end],
            seg_lengths[low_end:high_end],
            memory_fills[low_end:high_end],
            compressed_fills[low_end:high_end],
        )
        full_grads, small_grads, results = micro_batch(
            gathered, small_params, batch_data, tier_index, head_index
        )
        shard_total = add_tuples(shard_total, return_grads(full_grads))
        small_total = add_tuples(small_total, small_grads)
        out_rows.append(results[0])
        grad_in_rows.append(results[1])
        grad_comp_rows.append(results[2])
    small_sums = lax.psum(
        (
            small_total[0],
            small_total[1],
            small_total[2],
            small_total[3],
            small_total[4],
            small_total[5],
            small_total[6],
            small_total[7],
            small_total[8],
        ),
        ("dp", "tier"),
    )
    return (
        jnp.concatenate(out_rows, axis=0),
        jnp.concatenate(grad_in_rows, axis=0),
        jnp.concatenate(grad_comp_rows, axis=0),
        shard_total[0],
        small_sums[0],
        small_sums[1],
        small_sums[2],
        shard_total[1],
        shard_total[2],
        shard_total[3],
        shard_total[4],
        small_sums[3],
        small_sums[4],
        shard_total[5],
        small_sums[5],
        small_sums[6],
        shard_total[6],
        small_sums[7],
        shard_total[7],
        small_sums[8],
    )


def solution(mesh):
    placed = (
        P("dp", "tier", None),
        P("dp", "tier", None),
        P("dp", "tier", None),
        P("dp", "tier", None),
        P("dp", "tier", None),
        P("dp"),
        P("dp"),
        P("dp"),
        P(None, ("dp", "tier"), "head"),
        P("head"),
        P(),
        P(),
        P(("dp", "tier"), "head"),
        P(("dp", "tier"), "head"),
        P(("dp", "tier"), "head"),
        P(("dp", "tier"), "head"),
        P("head", None),
        P("head", None),
        P("head", ("dp", "tier")),
        P(),
        P(),
        P(("dp", "tier"), "head"),
        P("head"),
        P("head", ("dp", "tier")),
        P(),
    )
    return jax.shard_map(
        shards,
        mesh=mesh,
        in_specs=placed,
        out_specs=(
            P("dp", "tier", None),
            P("dp", "tier", None),
            P("dp", "tier", None),
            P(None, ("dp", "tier"), "head"),
            P("head"),
            P(),
            P(),
            P(("dp", "tier"), "head"),
            P(("dp", "tier"), "head"),
            P(("dp", "tier"), "head"),
            P(("dp", "tier"), "head"),
            P("head", None),
            P("head", None),
            P("head", ("dp", "tier")),
            P(),
            P(),
            P(("dp", "tier"), "head"),
            P("head"),
            P("head", ("dp", "tier")),
            P(),
        ),
        check_vma=False,
    )
```

profile of v0, /device:TPU:0, one launch (start us, length us, event | category | flops | bytes accessed | tf_op | source)
XLA Modules:
  0.0 2450.8 jit_solution(14031743501614325233)
XLA Ops:
  52.4 44.9 %all-gather.24.cloned.1.call-done = bf16[3,1024,512]{2,1,0:T(8,128)(2,1)} async-done(((bf16[3,64,512]{2,1,0:T(8,128)(2,1)}), bf16[3,1024,512]{2,1,0:T(8,128)(2,1)}) %all-gather.24.cloned.1.call-update) | async-done | bytes 3145744 | tf_op jit(solution)/shard_map/all_gather | solution.py:93
  123.5 12.7 all-gather.28.cloned.1.call-done
  172.6 11.1 fusion.60
  259.5 19.5 all-reduce.23.cloned.1.call-done
  289.4 49.4 %all-reduce.21.cloned.1.call-done = (bf16[1,256,1024]{2,1,0:T(8,128)(2,1)}, bf16[1,256,1024]{2,1,0:T(8,128)(2,1)}, bf16[1,256,1024]{2,1,0:T(8,128)(2,1)}) async-done(((bf16[1,256,1024]{2,1,0:T(8,128)(2,1)}, bf16[1,256,1024]{2,1,0:T(8,128)(2,1)}, bf16[1,256,1024]{2,1,0:T(8,128)(2,1)}), (bf16[1,256,1024]{2,1,0:T(8,128)(2,1)}, bf16[1,256,1024]{2,1,0:T(8,128)(2,1)}, ...) | async-done | bytes 1572880 | tf_op jit(solution)/shard_map/psum | solution.py:237
  342.7 48.9 %all-gather.36.cloned.1.call-done = bf16[1024,2048]{1,0:T(8,128)(2,1)} async-done(((bf16[64,2048]{1,0:T(8,128)(2,1)}), bf16[1024,2048]{1,0:T(8,128)(2,1)}) %all-gather.36.cloned.1.call-update) | async-done | bytes 4194320 | tf_op jit(solution)/shard_map/all_gather | solution.py:99
  396.5 46.2 %all-gather.38.cloned.1.call-done = bf16[2048,1024]{0,1:T(8,128)(2,1)} async-done(((bf16[2048,64]{0,1:T(8,128)(2,1)}), bf16[2048,1024]{0,1:T(8,128)(2,1)}) %all-gather.38.cloned.1.call-update) | async-done | bytes 4194320 | tf_op jit(solution)/shard_map/all_gather | solution.py:100
  467.6 50.4 %all-reduce.19.cloned.1.call-done = (bf16[1,256,1024]{2,1,0:T(8,128)(2,1)}, bf16[1,256,1024]{2,1,0:T(8,128)(2,1)}, bf16[1,256,1024]{2,1,0:T(8,128)(2,1)}) async-done(((bf16[1,256,1024]{2,1,0:T(8,128)(2,1)}, bf16[1,256,1024]{2,1,0:T(8,128)(2,1)}, bf16[1,256,1024]{2,1,0:T(8,128)(2,1)}), (bf16[1,256,1024]{2,1,0:T(8,128)(2,1)}, bf16[1,256,1024]{2,1,0:T(8,128)(2,1)}, ...) | async-done | bytes 1572880 | tf_op jit(solution)/shard_map/psum | solution.py:265
  584.9 10.8 subtract_convert_fusion.2
  776.6 67.2 %all-reduce.17.cloned.1.call-done = (bf16[1,256,1024]{2,1,0:T(8,128)(2,1)}, bf16[1,256,1024]{2,1,0:T(8,128)(2,1)}, bf16[1,256,1024]{2,1,0:T(8,128)(2,1)}, bf16[1...) async-done(((bf16[1,256,1024]{2,1,0:T(8,128)(2,1)}, bf16[1,256,1024]{2,1,0:T(8,128)(2,1)}, bf16[1,256,1024]{2,1,0:T(8,128)(2,1)}, ...) | async-done | bytes 6291472 | tf_op jit(solution)/shard_map/psum | solution.py:248
  904.8 60.3 %reduce-scatter.66.cloned.1.call-done = bf16[512,64]{0,1:T(8,128)(2,1)} async-done(((bf16[512,1024]{0,1:T(8,128)(2,1)}), bf16[512,64]{0,1:T(8,128)(2,1)}) %reduce-scatter.66.cloned.1.call-update) | async-done | bytes 65552 | tf_op jit(solution)/shard_map/reduce_scatter | solution.py:121
  965.1 60.2 %reduce-scatter.64.cloned.1.call-done = bf16[512,64]{0,1:T(8,128)(2,1)} async-done(((bf16[512,1024]{0,1:T(8,128)(2,1)}), bf16[512,64]{0,1:T(8,128)(2,1)}) %reduce-scatter.64.cloned.1.call-update) | async-done | bytes 65552 | tf_op jit(solution)/shard_map/reduce_scatter | solution.py:121
  1026.9 58.8 %reduce-scatter.56.cloned.1.call-done = bf16[64,512]{1,0:T(8,128)(2,1)} async-done(((bf16[1024,512]{1,0:T(8,128)(2,1)}), bf16[64,512]{1,0:T(8,128)(2,1)}) %reduce-scatter.56.cloned.1.call-update) | async-done | bytes 65552 | tf_op jit(solution)/shard_map/reduce_scatter | solution.py:115
  1085.8 60.2 %reduce-scatter.54.cloned.1.call-done = bf16[64,512]{1,0:T(8,128)(2,1)} async-done(((bf16[1024,512]{1,0:T(8,128)(2,1)}), bf16[64,512]{1,0:T(8,128)(2,1)}) %reduce-scatter.54.cloned.1.call-update) | async-done | bytes 65552 | tf_op jit(solution)/shard_map/reduce_scatter | solution.py:115
  1146.0 60.3 %reduce-scatter.52.cloned.1.call-done = bf16[64,512]{1,0:T(8,128)(2,1)} async-done(((bf16[1024,512]{1,0:T(8,128)(2,1)}), bf16[64,512]{1,0:T(8,128)(2,1)}) %reduce-scatter.52.cloned.1.call-update) | async-done | bytes 65552 | tf_op jit(solution)/shard_map/reduce_scatter | solution.py:115
  1207.8 58.6 %reduce-scatter.50.cloned.1.call-done = bf16[64,512]{1,0:T(8,128)(2,1)} async-done(((bf16[1024,512]{1,0:T(8,128)(2,1)}), bf16[64,512]{1,0:T(8,128)(2,1)}) %reduce-scatter.50.cloned.1.call-update) | async-done | bytes 65552 | tf_op jit(solution)/shard_map/reduce_scatter | solution.py:112
  1266.4 60.3 %reduce-scatter.48.cloned.1.call-done = bf16[64,512]{1,0:T(8,128)(2,1)} async-done(((bf16[1024,512]{1,0:T(8,128)(2,1)}), bf16[64,512]{1,0:T(8,128)(2,1)}) %reduce-scatter.48.cloned.1.call-update) | async-done | bytes 65552 | tf_op jit(solution)/shard_map/reduce_scatter | solution.py:112
  1326.7 60.0 %reduce-scatter.46.cloned.1.call-done = bf16[64,512]{1,0:T(8,128)(2,1)} async-done(((bf16[1024,512]{1,0:T(8,128)(2,1)}), bf16[64,512]{1,0:T(8,128)(2,1)}) %reduce-scatter.46.cloned.1.call-update) | async-done | bytes 65552 | tf_op jit(solution)/shard_map/reduce_scatter | solution.py:112
  1388.2 74.2 %reduce-scatter.76.cloned.1.call-done = bf16[2048,64]{0,1:T(8,128)(2,1)} async-done(((bf16[2048,1024]{0,1:T(8,128)(2,1)}), bf16[2048,64]{0,1:T(8,128)(2,1)}) %reduce-scatter.76.cloned.1.call-update) | async-done | bytes 262160 | tf_op jit(solution)/shard_map/reduce_scatter | solution.py:127
  1462.4 75.2 %reduce-scatter.78.cloned.1.call-done = bf16[2048,64]{0,1:T(8,128)(2,1)} async-done(((bf16[2048,1024]{0,1:T(8,128)(2,1)}), bf16[2048,64]{0,1:T(8,128)(2,1)}) %reduce-scatter.78.cloned.1.call-update) | async-done | bytes 262160 | tf_op jit(solution)/shard_map/reduce_scatter | solution.py:127
  1537.7 75.8 %reduce-scatter.80.cloned.1.call-done = bf16[2048,64]{0,1:T(8,128)(2,1)} async-done(((bf16[2048,1024]{0,1:T(8,128)(2,1)}), bf16[2048,64]{0,1:T(8,128)(2,1)}) %reduce-scatter.80.cloned.1.call-update) | async-done | bytes 262160 | tf_op jit(solution)/shard_map/reduce_scatter | solution.py:127
  1615.5 73.6 %reduce-scatter.72.cloned.1.call-done = bf16[64,2048]{1,0:T(8,128)(2,1)} async-done(((bf16[1024,2048]{1,0:T(8,128)(2,1)}), bf16[64,2048]{1,0:T(8,128)(2,1)}) %reduce-scatter.72.cloned.1.call-update) | async-done | bytes 262160 | tf_op jit(solution)/shard_map/reduce_scatter | solution.py:124
  1689.1 75.8 %reduce-scatter.70.cloned.1.call-done = bf16[64,2048]{1,0:T(8,128)(2,1)} async-done(((bf16[1024,2048]{1,0:T(8,128)(2,1)}), bf16[64,2048]{1,0:T(8,128)(2,1)}) %reduce-scatter.70.cloned.1.call-update) | async-done | bytes 262160 | tf_op jit(solution)/shard_map/reduce_scatter | solution.py:124
  1764.9 75.2 %reduce-scatter.74.cloned.1.call-done = bf16[64,2048]{1,0:T(8,128)(2,1)} async-done(((bf16[1024,2048]{1,0:T(8,128)(2,1)}), bf16[64,2048]{1,0:T(8,128)(2,1)}) %reduce-scatter.74.cloned.1.call-update) | async-done | bytes 262160 | tf_op jit(solution)/shard_map/reduce_scatter | solution.py:124
  1842.2 58.5 %reduce-scatter.40.cloned.1.call-done = bf16[64,512]{1,0:T(8,128)(2,1)} async-done(((bf16[1024,512]{1,0:T(8,128)(2,1)}), bf16[64,512]{1,0:T(8,128)(2,1)}) %reduce-scatter.40.cloned.1.call-update) | async-done | bytes 65552 | tf_op jit(solution)/shard_map/reduce_scatter | solution.py:109
  1900.7 60.7 %reduce-scatter.42.cloned.1.call-done = bf16[64,512]{1,0:T(8,128)(2,1)} async-done(((bf16[1024,512]{1,0:T(8,128)(2,1)}), bf16[64,512]{1,0:T(8,128)(2,1)}) %reduce-scatter.42.cloned.1.call-update) | async-done | bytes 65552 | tf_op jit(solution)/shard_map/reduce_scatter | solution.py:109
  1961.3 60.9 %reduce-scatter.44.cloned.1.call-done = bf16[64,512]{1,0:T(8,128)(2,1)} async-done(((bf16[1024,512]{1,0:T(8,128)(2,1)}), bf16[64,512]{1,0:T(8,128)(2,1)}) %reduce-scatter.44.cloned.1.call-update) | async-done | bytes 65552 | tf_op jit(solution)/shard_map/reduce_scatter | solution.py:109
  2023.8 58.4 %reduce-scatter.58.cloned.1.call-done = bf16[64,512]{1,0:T(8,128)(2,1)} async-done(((bf16[1024,512]{1,0:T(8,128)(2,1)}), bf16[64,512]{1,0:T(8,128)(2,1)}) %reduce-scatter.58.cloned.1.call-update) | async-done | bytes 65552 | tf_op jit(solution)/shard_map/reduce_scatter | solution.py:118
  2082.2 60.4 %reduce-scatter.60.cloned.1.call-done = bf16[64,512]{1,0:T(8,128)(2,1)} async-done(((bf16[1024,512]{1,0:T(8,128)(2,1)}), bf16[64,512]{1,0:T(8,128)(2,1)}) %reduce-scatter.60.cloned.1.call-update) | async-done | bytes 65552 | tf_op jit(solution)/shard_map/reduce_scatter | solution.py:118
  2142.7 60.0 %reduce-scatter.62.cloned.1.call-done = bf16[64,512]{1,0:T(8,128)(2,1)} async-done(((bf16[1024,512]{1,0:T(8,128)(2,1)}), bf16[64,512]{1,0:T(8,128)(2,1)}) %reduce-scatter.62.cloned.1.call-update) | async-done | bytes 65552 | tf_op jit(solution)/shard_map/reduce_scatter | solution.py:118
  2216.1 62.1 %all-reduce.3 = (f32[512]{0:T(512)}, f32[1024]{0:T(1024)}, f32[1024]{0:T(1024)}, f32[4,128]{1,0:T(4,128)}, f32[4,128]{1,0:T(4,128)}, /*index=5*/f32[1024]{0:T(10...) all-reduce(f32[512]{0:T(512)S(1)} %add_add_fusion.13, ...), channel_id=1, replica_groups=mesh['dp'=8,'tier'=2,'head'=2] {'dp','tier'}, use_global_device_ids=true, to_apply=%region_60.61 | all-reduce | flops 8704 | bytes 69632 | tf_op jit(solution)/shard_map/psum | solution.py:495
  2287.5 153.8 %all-reduce.15.cloned.1.call-done = (bf16[3,1024,512]{2,0,1:T(4,128)(2,1)}, bf16[3,1024,512]{2,0,1:T(4,128)(2,1)}, bf16[3,1024,512]{2,0,1:T(4,128)(2,1)}) async-done(((bf16[3,1024,512]{2,0,1:T(4,128)(2,1)}, bf16[3,1024,512]{2,0,1:T(4,128)(2,1)}, bf16[3,1024,512]{2,0,1:T(4,128)(2,1)}), (bf16[3,1024,512]{2,0,1:T(4,128)(2,1)}, bf16[3,1024,512]{2,0,1:T(4,128)(2,1)}, ...) | async-done | bytes 9437200
  (911 shorter events, 563.2 us)
Async XLA Ops:
  8.7 127.6 %all-gather.28.cloned.1.call-start = ((), (), s32[]{:S(2)}) async-start(), calls=%async_computation.29 | async-start | bytes 1114112 | tf_op jit(solution)/shard_map/all_gather | solution.py:94
  9.4 187.7 %all-gather.30.cloned.1.call-start = ((), (), s32[]{:S(2)}) async-start(), calls=%async_computation.30 | async-start | bytes 1114112 | tf_op jit(solution)/shard_map/all_gather | solution.py:95
  10.0 204.1 %all-gather.26.cloned.1.call-start = ((), (), s32[]{:S(2)}) async-start(), calls=%async_computation.28 | async-start | bytes 1114112 | tf_op jit(solution)/shard_map/all_gather | solution.py:96
  10.6 249.0 %all-gather.34.cloned.1.call-start = ((), (), s32[]{:S(2)}) async-start(), calls=%async_computation.32 | async-start | bytes 1114112 | tf_op jit(solution)/shard_map/all_gather | solution.py:98
  11.1 267.9 %all-reduce.23.cloned.1.call-start = ((), (), s32[]{:S(2)}) async-start(), calls=%async_computation.66 | async-start | bytes 3145728 | tf_op jit(solution)/shard_map/psum | solution.py:230
  285.6 106.0 %all-gather.36.cloned.1.call-start = ((), (), s32[]{:S(2)}) async-start(), calls=%async_computation.33 | async-start | bytes 4456448 | tf_op jit(solution)/shard_map/all_gather | solution.py:99
  286.3 156.3 %all-gather.38.cloned.1.call-start = ((), (), s32[]{:S(2)}) async-start(), calls=%async_computation.34 | async-start | bytes 4456448 | tf_op jit(solution)/shard_map/all_gather | solution.py:100
  286.9 231.2 %all-reduce.19.cloned.1.call-start = ((), (), s32[]{:S(2)}) async-start(), calls=%async_computation.64 | async-start | bytes 3145728 | tf_op jit(solution)/shard_map/psum | solution.py:265
  467.6 190.1 %reduce-scatter.30.cloned.1.call-start = ((), (), s32[]{:S(2)}) async-start(), calls=%async_computation.36 | async-start | bytes 6291456 | tf_op jit(solution)/shard_map/reduce_scatter | solution.py:318
  657.6 186.2 %all-reduce.17.cloned.1.call-start = ((), (), s32[]{:S(2)}) async-start(), calls=%async_computation.63 | async-start | bytes 12582912 | tf_op jit(solution)/shard_map/psum | solution.py:248
  688.4 216.4 %reduce-scatter.68.cloned.1.call-start = ((), (), s32[]{:S(2)}) async-start(), calls=%async_computation.55 | async-start | bytes 1114112 | tf_op jit(solution)/shard_map/reduce_scatter | solution.py:121
  691.2 274.0 %reduce-scatter.66.cloned.1.call-start = ((), (), s32[]{:S(2)}) async-start(), calls=%async_computation.54 | async-start | bytes 1114112 | tf_op jit(solution)/shard_map/reduce_scatter | solution.py:121
  693.7 331.7 %reduce-scatter.64.cloned.1.call-start = ((), (), s32[]{:S(2)}) async-start(), calls=%async_computation.53 | async-start | bytes 1114112 | tf_op jit(solution)/shard_map/reduce_scatter | solution.py:121
  696.3 389.5 %reduce-scatter.56.cloned.1.call-start = ((), (), s32[]{:S(2)}) async-start(), calls=%async_computation.49 | async-start | bytes 1114112 | tf_op jit(solution)/shard_map/reduce_scatter | solution.py:115
  700.0 445.9 %reduce-scatter.54.cloned.1.call-start = ((), (), s32[]{:S(2)}) async-start(), calls=%async_computation.48 | async-start | bytes 1114112 | tf_op jit(solution)/shard_map/reduce_scatter | solution.py:115
  703.6 502.7 %reduce-scatter.52.cloned.1.call-start = ((), (), s32[]{:S(2)}) async-start(), calls=%async_computation.47 | async-start | bytes 1114112 | tf_op jit(solution)/shard_map/reduce_scatter | solution.py:115
  707.6 558.7 %reduce-scatter.50.cloned.1.call-start = ((), (), s32[]{:S(2)}) async-start(), calls=%async_computation.46 | async-start | bytes 1114112 | tf_op jit(solution)/shard_map/reduce_scatter | solution.py:112
  711.2 615.5 %reduce-scatter.48.cloned.1.call-start = ((), (), s32[]{:S(2)}) async-start(), calls=%async_computation.45 | async-start | bytes 1114112 | tf_op jit(solution)/shard_map/reduce_scatter | solution.py:112
  714.7 672.0 %reduce-scatter.46.cloned.1.call-start = ((), (), s32[]{:S(2)}) async-start(), calls=%async_computation.44 | async-start | bytes 1114112 | tf_op jit(solution)/shard_map/reduce_scatter | solution.py:112
  718.6 743.8 %reduce-scatter.76.cloned.1.call-start = ((), (), s32[]{:S(2)}) async-start(), calls=%async_computation.59 | async-start | bytes 4456448 | tf_op jit(solution)/shard_map/reduce_scatter | solution.py:127
  723.8 813.8 %reduce-scatter.78.cloned.1.call-start = ((), (), s32[]{:S(2)}) async-start(), calls=%async_computation.60 | async-start | bytes 4456448 | tf_op jit(solution)/shard_map/reduce_scatter | solution.py:127
  729.1 884.4 %reduce-scatter.80.cloned.1.call-start = ((), (), s32[]{:S(2)}) async-start(), calls=%async_computation.61 | async-start | bytes 4456448 | tf_op jit(solution)/shard_map/reduce_scatter | solution.py:127
  734.2 954.8 %reduce-scatter.72.cloned.1.call-start = ((), (), s32[]{:S(2)}) async-start(), calls=%async_computation.57 | async-start | bytes 4456448 | tf_op jit(solution)/shard_map/reduce_scatter | solution.py:124
  739.1 1025.7 %reduce-scatter.70.cloned.1.call-start = ((), (), s32[]{:S(2)}) async-start(), calls=%async_computation.56 | async-start | bytes 4456448 | tf_op jit(solution)/shard_map/reduce_scatter | solution.py:124
  744.1 1096.0 %reduce-scatter.74.cloned.1.call-start = ((), (), s32[]{:S(2)}) async-start(), calls=%async_computation.58 | async-start | bytes 4456448 | tf_op jit(solution)/shard_map/reduce_scatter | solution.py:124
  749.0 1151.7 %reduce-scatter.40.cloned.1.call-start = ((), (), s32[]{:S(2)}) async-start(), calls=%async_computation.41 | async-start | bytes 1114112 | tf_op jit(solution)/shard_map/reduce_scatter | solution.py:109
  752.6 1208.7 %reduce-scatter.42.cloned.1.call-start = ((), (), s32[]{:S(2)}) async-start(), calls=%async_computation.42 | async-start | bytes 1114112 | tf_op jit(solution)/shard_map/reduce_scatter | solution.py:109
  755.5 1266.8 %reduce-scatter.44.cloned.1.call-start = ((), (), s32[]{:S(2)}) async-start(), calls=%async_computation.43 | async-start | bytes 1114112 | tf_op jit(solution)/shard_map/reduce_scatter | solution.py:109
  758.2 1324.0 %reduce-scatter.58.cloned.1.call-start = ((), (), s32[]{:S(2)}) async-start(), calls=%async_computation.50 | async-start | bytes 1114112 | tf_op jit(solution)/shard_map/reduce_scatter | solution.py:118
  762.2 1380.5 %reduce-scatter.60.cloned.1.call-start = ((), (), s32[]{:S(2)}) async-start(), calls=%async_computation.51 | async-start | bytes 1114112 | tf_op jit(solution)/shard_map/reduce_scatter | solution.py:118
  766.2 1436.4 %reduce-scatter.62.cloned.1.call-start = ((), (), s32[]{:S(2)}) async-start(), calls=%async_computation.52 | async-start | bytes 1114112 | tf_op jit(solution)/shard_map/reduce_scatter | solution.py:118
  776.3 1665.0 %all-reduce.15.cloned.1.call-start = ((), (), s32[]{:S(2)}) async-start(), calls=%async_computation.62 | async-start | bytes 25165824
  (280 other events, 15479.6 us)
Sparse Core Ops, SparseCore 0:
  10.2 40.6 all-gather.31
  53.1 44.1 all-gather.23
  138.3 36.8 all-gather.29
  177.2 36.8 all-gather.25
  216.1 36.8 all-gather.33
  285.7 53.0 all-reduce.20
  341.0 50.5 all-gather.35
  393.6 49.0 all-gather.37
  467.7 50.3 all-reduce.18
  688.5 155.1 all-reduce.16
  847.4 57.3 reduce-scatter.67
  908.7 56.3 reduce-scatter.65
  968.8 56.5 reduce-scatter.63
  1029.4 56.3 reduce-scatter.55
  1089.4 56.5 reduce-scatter.53
  1149.9 56.3 reduce-scatter.51
  1209.8 56.4 reduce-scatter.49
  1270.3 56.3 reduce-scatter.47
  1330.1 56.4 reduce-scatter.45
  1391.0 71.3 reduce-scatter.75
  1466.3 71.3 reduce-scatter.77
  1541.9 71.5 reduce-scatter.79
  1617.3 71.6 reduce-scatter.71
  1693.4 71.4 reduce-scatter.69
  1768.6 71.4 reduce-scatter.73
  1844.1 56.4 reduce-scatter.39
  1904.8 56.4 reduce-scatter.41
  1965.8 56.3 reduce-scatter.43
  2025.7 56.4 reduce-scatter.57
  2086.3 56.3 reduce-scatter.59
  2146.1 56.4 reduce-scatter.61
  2207.7 233.6 all-reduce.14
  (8 shorter events, 121.9 us)
where the time goes:
time: 2460 us; the launch traced here: 2450 us
  waiting for transfers between devices  1800 us (73%)
  matrix products  254 us (10%)
  other arithmetic  163 us (7%)
  local copies, waits for them, and re-layouts  113 us (5%)
  blocking collectives  96.6 us (4%)
    reduce_scatter x3, waiting for transfers between devices, return_grads(): lax.psum_scatter(grads[7].astype(jnp.bfloat16), ('dp', 'tier'), scatter_d...  225 us
    reduce_scatter x3, waiting for transfers between devices, return_grads(): lax.psum_scatter(grads[6].astype(jnp.bfloat16), ('dp', 'tier'), scatter_d...  225 us
    reduce_scatter x3, waiting for transfers between devices, return_grads(): lax.psum_scatter(grads[1].astype(jnp.bfloat16), ('dp', 'tier'), scatter_d...  180 us
    reduce_scatter x3, waiting for transfers between devices, return_grads(): lax.psum_scatter(grads[3].astype(jnp.bfloat16), ('dp', 'tier'), scatter_d...  179 us
    reduce_scatter x3, waiting for transfers between devices, return_grads(): lax.psum_scatter(grads[2].astype(jnp.bfloat16), ('dp', 'tier'), scatter_d...  179 us
    reduce_scatter x3, waiting for transfers between devices, return_grads(): lax.psum_scatter(grads[4].astype(jnp.bfloat16), ('dp', 'tier'), scatter_d...  179 us
    unnamed x41, waiting for transfers between devices  159 us
    reduce_scatter x3, waiting for transfers between devices, return_grads(): lax.psum_scatter(grads[5].astype(jnp.bfloat16), ('dp', 'tier'), scatter_d...  121 us
  transfers between devices with their start and end apart: 40, of which 32 were waited for; matrix products, arithmetic and copies ran while one was open for 16% of the time, Pallas kernels for 0%

commit v1 on v0

v1 whole, which is shorter than its diff:
```python
import functools
import math

import jax
import jax.numpy as jnp
import ml_dtypes
import numpy as np
from jax import lax
from jax.experimental import pallas as pl
from jax.experimental.pallas import tpu as pltpu
from jax.sharding import PartitionSpec as P

D = 1024
MEM = 512
CMEM = 512
KW = 3
OLDC = 384
EPS = 1e-05
NEG = -1e30
F32 = jnp.float32
BF16 = jnp.bfloat16


def swap(x, axis, step=1):
    n = lax.axis_size(axis)
    return lax.ppermute(x, axis, [(i, i ^ step) for i in range(n)])


def turn(x, steps):
    n = lax.axis_size("dp")
    zn = n // 2
    return lax.ppermute(
        x, "dp", [(i, ((i // 2 + steps) % zn) * 2 + i % 2) for i in range(n)]
    )


def head_sum(x):
    if lax.axis_size("head") == 2:
        return x.astype(F32) + swap(x, "head").astype(F32)
    return lax.psum(x, "head").astype(F32)


def head_gather(x):
    if lax.axis_size("head") == 2:
        other = swap(x, "head")
        first = lax.axis_index("head") == 0
        return jnp.concatenate(
            [jnp.where(first, x, other), jnp.where(first, other, x)], axis=-1
        )
    return lax.all_gather(x, "head", axis=x.ndim - 1, tiled=True)


def place_kernel(zn, rows, at_ref, *refs):
    count = zn * 4
    blocks, out, sems = refs[:count], refs[count], refs[count + 1]
    z, y, t = at_ref[0], at_ref[1], at_ref[2]
    copies = []
    for k in range(count):
        turned, flip_y, flip_t = k % zn, (k // zn) % 2, k // (2 * zn)
        zz = lax.rem(z + zn - turned, zn)
        yy = y + flip_y - 2 * y * flip_y
        tt = t + flip_t - 2 * t * flip_t
        row = pl.multiple_of(((zz * 2 + yy) * 2 + tt) * rows, rows)
        copies.append(
            pltpu.make_async_copy(blocks[k], out.at[pl.ds(row, rows)], sems.at[k])
        )
    for copy in copies:
        copy.start()
    for copy in copies:
        copy.wait()


def gather_rows(x):
    n = lax.axis_size("dp")
    rows, cols = x.shape
    zn = n // 2
    ring = [x] + [turn(x, s) for s in range(1, zn)]
    own = ring + [swap(r, "dp") for r in ring]
    blocks = own + [swap(r, "tier") for r in own]
    dp = lax.axis_index("dp")
    at = jnp.stack([dp // 2, dp % 2, lax.axis_index("tier")]).astype(jnp.int32)
    return pl.pallas_call(
        functools.partial(place_kernel, zn, rows),
        grid_spec=pltpu.PrefetchScalarGridSpec(
            num_scalar_prefetch=1,
            grid=(1,),
            in_specs=[pl.BlockSpec(memory_space=pl.ANY)] * len(blocks),
            out_specs=pl.BlockSpec((n * 2 * rows, cols), lambda i, s: (0, 0)),
            scratch_shapes=[pltpu.SemaphoreType.DMA((len(blocks),))],
        ),
        out_shape=jax.ShapeDtypeStruct((n * 2 * rows, cols), x.dtype),
        compiler_params=pltpu.CompilerParams(vmem_limit_bytes=48 << 20),
        name="place",
    )(at, *blocks)


def reduce_rows(g):
    n = lax.axis_size("dp")
    zn = n // 2
    dp = lax.axis_index("dp")
    z, y, t = dp // 2, dp % 2, lax.axis_index("tier")
    rows = g.shape[0] // (n * 2)

    def pick(v, k, axis):
        return lax.dynamic_index_in_dim(v, k, axis, keepdims=False)

    v = g.reshape(zn, 2, 2, rows, -1)
    v = (
        pick(v, t, 2).astype(F32) + swap(pick(v, 1 - t, 2), "tier").astype(F32)
    ).astype(BF16)
    v = (pick(v, y, 1).astype(F32) + swap(pick(v, 1 - y, 1), "dp").astype(F32)).astype(
        BF16
    )
    total = pick(v, z, 0).astype(F32)
    for s in range(1, zn):
        total = total + turn(pick(v, lax.rem(z + s, zn), 0), s).astype(F32)
    return total


def small_sum(parts):
    flat = jnp.concatenate([p.reshape(-1) for p in parts])
    pad = -flat.shape[0] % 1024
    flat = jnp.pad(flat, (0, pad)).reshape(-1, 128)
    n = lax.axis_size("dp")
    if n & (n - 1):
        flat = lax.psum(flat, ("dp", "tier"))
    else:
        flat = flat + swap(flat, "tier")
        step = 1
        while step < n:
            flat = flat + swap(flat, "dp", step)
            step *= 2
    flat = flat.reshape(-1)
    out, at = [], 0
    for p in parts:
        out.append(flat[at : at + p.size].reshape(p.shape))
        at += p.size
    return out


def dot(a, b, contract):
    return lax.dot_general(a, b, (contract, ((), ())), preferred_element_type=F32)


def key_pieces(sizes):
    comp, fresh, mem, seg = sizes
    return (
        (0, 0, comp),
        (comp, OLDC, fresh),
        (comp + fresh, CMEM, mem),
        (comp + fresh + mem, CMEM + MEM, seg),
    )


def in_order(full, own, other, tier, sizes):
    for row, pos, rows in key_pieces(sizes):
        mine = pl.multiple_of(pos + tier * rows, rows)
        theirs = pl.multiple_of(pos + (1 - tier) * rows, rows)
        full[pl.ds(mine, rows)] = own[0, row : row + rows]
        full[pl.ds(theirs, rows)] = other[0, row : row + rows]


def forward_kernel(
    sizes, at, q, k_own, k_other, v_own, v_other, table, cb, pb, att, probs, kf, vf
):
    b = pl.program_id(0)
    tier = at[0]
    comp_fill, mem_fill, seg_len = at[1 + 3 * b], at[2 + 3 * b], at[3 + 3 * b]
    rows = q.shape[1]
    keys = kf.shape[0]
    in_order(kf, k_own, k_other, tier, sizes)
    in_order(vf, v_own, v_other, tier, sizes)
    query = q[0].astype(F32)
    content_q = (query + cb[0]).astype(BF16)
    position_q = (query + pb[0]).astype(BF16)
    scale = 1.0 / math.sqrt(q.shape[2])
    relative = dot(position_q, table[...], ((1,), (1,)))
    relative = pltpu.roll(relative, keys - rows + 1, 1, stride=1, stride_axis=0)
    scores = (dot(content_q, kf[...], ((1,), (1,))) + relative) * scale
    start = CMEM + MEM
    j = lax.broadcasted_iota(jnp.int32, (1, keys), 1)
    lowest = jnp.where(
        j < CMEM, CMEM - comp_fill, jnp.where(j < start, start - mem_fill, start)
    )
    beyond = jnp.where(j < start, start, start + seg_len)
    open_col = (j >= lowest) & (j < beyond)
    bias = jnp.where(open_col, 0.0, NEG)
    i = lax.broadcasted_iota(jnp.int32, (rows, keys), 0) + tier * rows
    jj = lax.broadcasted_iota(jnp.int32, (rows, keys), 1) - start
    masked = jnp.where(jj <= i, scores + bias, NEG)
    peak = jnp.max(masked, axis=-1, keepdims=True)
    e = jnp.exp(masked - peak)
    total = jnp.sum(e, axis=-1, keepdims=True)
    p = (e * (1.0 / total)).astype(BF16)
    probs[0, 0] = p
    att[0] = dot(p, vf[...], ((1,), (0,))).astype(BF16)


def attend(at, q, kv, kv_other, table, cb, pb, sizes):
    batch, rows, width = q.shape
    heads = cb.shape[0]
    hd = width // heads
    keys_local = kv.shape[1]
    keys = 2 * keys_local

    def col(off):
        return pl.BlockSpec((1, keys_local, hd), lambda b, h, s: (b, 0, h + off))

    return pl.pallas_call(
        functools.partial(forward_kernel, sizes),
        grid_spec=pltpu.PrefetchScalarGridSpec(
            num_scalar_prefetch=1,
            grid=(batch, heads),
            in_specs=[
                pl.BlockSpec((1, rows, hd), lambda b, h, s: (b, 0, h)),
                col(0),
                col(0),
                col(heads),
                col(heads),
                pl.BlockSpec((keys, hd), lambda b, h, s: (0, h)),
                pl.BlockSpec((1, 1, hd), lambda b, h, s: (h, 0, 0)),
                pl.BlockSpec((1, 1, hd), lambda b, h, s: (h, 0, 0)),
            ],
            out_specs=[
                pl.BlockSpec((1, rows, hd), lambda b, h, s: (b, 0, h)),
                pl.BlockSpec((1, 1, rows, keys), lambda b, h, s: (b, h, 0, 0)),
            ],
            scratch_shapes=[pltpu.VMEM((keys, hd), BF16), pltpu.VMEM((keys, hd), BF16)],
        ),
        out_shape=[
            jax.ShapeDtypeStruct((batch, rows, width), BF16),
            jax.ShapeDtypeStruct((batch, heads, rows, keys), BF16),
        ],
        compiler_params=pltpu.CompilerParams(vmem_limit_bytes=48 << 20),
        cost_estimate=pl.CostEstimate(
            flops=batch * heads * 6 * rows * keys * hd,
            bytes_accessed=batch * heads * rows * keys * 2,
            transcendentals=batch * heads * rows * keys,
        ),
        name="attend",
    )(at, q, kv, kv_other, kv, kv_other, table, cb[:, None], pb[:, None])


def backward_kernel(
    sizes,
    at,
    probs,
    gatt,
    q,
    k_own,
    k_other,
    v_own,
    v_other,
    table,
    cb,
    pb,
    gq,
    keep,
    send,
    gtable,
    gbias,
    kf,
    vf,
    gk,
):
    first = pl.program_id(1) == 0
    tier = at[0]
    rows = q.shape[1]
    in_order(kf, k_own, k_other, tier, sizes)
    in_order(vf, v_own, v_other, tier, sizes)
    query = q[0].astype(F32)
    content_q = (query + cb[0]).astype(BF16)
    position_q = (query + pb[0]).astype(BF16)
    scale = 1.0 / math.sqrt(q.shape[2])
    ga = gatt[0]
    p_low = probs[0, 0]
    p = p_low.astype(F32)
    gp = dot(ga, vf[...], ((1,), (1,)))
    row_dot = jnp.sum(p * gp, axis=-1, keepdims=True)
    ds = (p * (gp - row_dot)).astype(BF16)

    def hand_out(which, value):
        gk[...] = value.astype(BF16)
        for row, pos, size in key_pieces(sizes):
            mine = pl.multiple_of(pos + tier * size, size)
            theirs = pl.multiple_of(pos + (1 - tier) * size, size)
            keep[which, 0, row : row + size] = gk[pl.ds(mine, size)]
            send[which, 0, row : row + size] = gk[pl.ds(theirs, size)]

    hand_out(0, dot(ds, content_q, ((0,), (0,))) * scale)
    hand_out(1, dot(p_low, ga, ((0,), (0,))))
    g_content = dot(ds, kf[...], ((1,), (0,))) * scale
    r = lax.broadcasted_iota(jnp.int32, (rows, rows), 0)
    c = lax.broadcasted_iota(jnp.int32, (rows, rows), 1)
    flip = jnp.where(r + c == rows - 1, 1.0, 0.0).astype(BF16)
    ds_flip = dot(flip, ds, ((1,), (0,)))
    skewed = pltpu.roll(ds_flip, 0, 1, stride=1, stride_axis=0).astype(BF16)
    position_flip = dot(flip, position_q, ((1,), (0,))).astype(BF16)
    g_table = dot(skewed, position_flip, ((0,), (0,))) * scale
    g_flip = dot(skewed, table[...], ((1,), (0,))) * scale
    high = g_flip.astype(BF16)
    low = (g_flip - high.astype(F32)).astype(BF16)
    g_position = dot(flip, high, ((1,), (0,))) + dot(flip, low, ((1,), (0,)))
    gq[0] = (g_content + g_position).astype(BF16)
    sums = jnp.concatenate(
        [
            jnp.sum(g_content, axis=0, keepdims=True),
            jnp.sum(g_position, axis=0, keepdims=True),
            jnp.zeros((6, g_content.shape[1]), F32),
        ],
        axis=0,
    )

    @pl.when(first)
    def _():
        gtable[...] = g_table
        gbias[0] = sums

    @pl.when(jnp.logical_not(first))
    def _():
        gtable[...] += g_table
        gbias[0] += sums


def attend_back(at, probs, gatt, q, kv, kv_other, table, cb, pb, sizes):
    batch, rows, width = q.shape
    heads = cb.shape[0]
    hd = width // heads
    keys_local = kv.shape[1]
    keys = 2 * keys_local

    def col(off):
        return pl.BlockSpec((1, keys_local, hd), lambda h, b, s: (b, 0, h + off))

    def row_block():
        return pl.BlockSpec((1, rows, hd), lambda h, b, s: (b, 0, h))

    def half():
        return pl.BlockSpec((2, 1, keys_local, hd), lambda h, b, s: (0, b, 0, h))

    return pl.pallas_call(
        functools.partial(backward_kernel, sizes),
        grid_spec=pltpu.PrefetchScalarGridSpec(
            num_scalar_prefetch=1,
            grid=(heads, batch),
            in_specs=[
                pl.BlockSpec((1, 1, rows, keys), lambda h, b, s: (b, h, 0, 0)),
                row_block(),
                row_block(),
                col(0),
                col(0),
                col(heads),
                col(heads),
                pl.BlockSpec((keys, hd), lambda h, b, s: (0, h)),
                pl.BlockSpec((1, 1, hd), lambda h, b, s: (h, 0, 0)),
                pl.BlockSpec((1, 1, hd), lambda h, b, s: (h, 0, 0)),
            ],
            out_specs=[
                row_block(),
                half(),
                half(),
                pl.BlockSpec((keys, hd), lambda h, b, s: (0, h)),
                pl.BlockSpec((1, 8, hd), lambda h, b, s: (h, 0, 0)),
            ],
            scratch_shapes=[pltpu.VMEM((keys, hd), BF16)] * 3,
        ),
        out_shape=[
            jax.ShapeDtypeStruct((batch, rows, width), BF16),
            jax.ShapeDtypeStruct((2, batch, keys_local, width), BF16),
            jax.ShapeDtypeStruct((2, batch, keys_local, width), BF16),
            jax.ShapeDtypeStruct((keys, width), F32),
            jax.ShapeDtypeStruct((heads, 8, hd), F32),
        ],
        compiler_params=pltpu.CompilerParams(vmem_limit_bytes=48 << 20),
        cost_estimate=pl.CostEstimate(
            flops=batch * heads * 14 * rows * keys * hd,
            bytes_accessed=batch * heads * rows * keys * 2,
            transcendentals=0,
        ),
        name="attend_back",
    )(at, probs, gatt, q, kv, kv_other, kv, kv_other, table, cb[:, None], pb[:, None])


def distance_rows(first, count):
    half = D // 2
    freq = np.exp(np.arange(half) * (-2.0 * math.log(10000.0) / D))
    turned = (first - np.arange(count))[:, None] * freq[None, :]
    return np.concatenate([np.sin(turned), np.cos(turned)], axis=1).astype(
        ml_dtypes.bfloat16
    )


def standardize(rows):
    mean = jnp.mean(rows, axis=-1, keepdims=True)
    centred = rows - mean
    var = jnp.mean(centred * centred, axis=-1, keepdims=True)
    r = lax.rsqrt(var + EPS)
    return centred * r, r


def norm_back(grad, xhat, r, gain):
    g = grad * gain
    return r * (
        g
        - jnp.mean(g, axis=-1, keepdims=True)
        - xhat * jnp.mean(g * xhat, axis=-1, keepdims=True)
    )


def col_sum(x):
    return jnp.sum(x, axis=tuple(range(x.ndim - 1)))


def ein(spec, a, b):
    return jnp.einsum(spec, a, b, preferred_element_type=F32)


def shards(
    segment_input,
    memory,
    compressed,
    evicted,
    cotangent,
    seg_lengths,
    memory_fills,
    compressed_fills,
    conv_weight,
    conv_bias,
    norm1_gain,
    norm1_bias,
    query_weight,
    key_weight,
    value_weight,
    position_weight,
    content_bias,
    position_bias,
    out_weight,
    norm2_gain,
    norm2_bias,
    up_weight,
    up_bias,
    down_weight,
    down_bias,
):
    tier = lax.axis_index("tier")
    head = lax.axis_index("head")
    batch, seg, _ = segment_input.shape
    mem = memory.shape[1]
    comp = compressed.shape[1]
    fresh = evicted.shape[1] // KW
    sizes = (comp, fresh, mem, seg)
    width = query_weight.shape[1]
    wide = conv_weight.shape[2]
    hidden = up_weight.shape[1]
    keys = 2 * (comp + fresh + mem + seg)

    attn_w = gather_rows(
        jnp.concatenate([key_weight, value_weight, query_weight, position_weight], 1)
    )
    conv_w = gather_rows(jnp.concatenate([conv_weight[k] for k in range(KW)], 1))
    out_t = head_gather(out_weight.T)
    ffn_w = gather_rows(jnp.concatenate([out_t, up_weight, down_weight.T], 1))
    kv_w = attn_w[:, : 2 * width]
    q_w = attn_w[:, 2 * width : 3 * width]
    pos_w = attn_w[:, 3 * width :]
    full_width = out_t.shape[1]
    out_wt = ffn_w[:, :full_width]
    up_w = ffn_w[:, full_width : full_width + hidden]
    down_wt = ffn_w[:, full_width + hidden :]

    grouped = evicted.reshape(batch, fresh, KW, D)
    fresh_part = conv_bias
    for k in range(KW):
        fresh_part = fresh_part + ein(
            "bgc,cd->bgd", grouped[:, :, k], conv_w[:, k * wide : (k + 1) * wide]
        )
    fresh_rows = head_gather(fresh_part.astype(BF16))
    context = jnp.concatenate([compressed, fresh_rows, memory, segment_input], axis=1)
    xhat, r_one = standardize(context.astype(F32))
    normed = (xhat * norm1_gain + norm1_bias).astype(BF16)
    split = comp + fresh + mem
    kv = ein("brd,de->bre", normed, kv_w).astype(BF16)
    own_normed = normed[:, split:]
    q = ein("brd,de->bre", own_normed, q_w).astype(BF16)
    kv_other = swap(kv, "tier")
    far = keys - 1
    steps = jnp.asarray(distance_rows(far, keys + seg))
    steps = lax.dynamic_slice_in_dim(steps, (1 - tier) * seg, keys, 0)
    table = ein("nf,fe->ne", steps, pos_w).astype(BF16)
    at = jnp.concatenate(
        [
            tier[None].astype(jnp.int32),
            jnp.stack([compressed_fills, memory_fills, seg_lengths], 1).reshape(-1),
        ]
    )
    att, probs = attend(at, q, kv, kv_other, table, content_bias, position_bias, sizes)
    att_full = head_gather(att)
    branch = ein("bre,de->brd", att_full, out_wt)
    hidden_one = segment_input.astype(F32) + branch

    xhat_two, r_two = standardize(hidden_one)
    normed_two = (xhat_two * norm2_gain + norm2_bias).astype(BF16)
    pre = ein("brd,df->brf", normed_two, up_w) + up_bias
    activated_f, gate_pull = jax.vjp(
        lambda v: jax.nn.gelu(v, approximate=True), pre
    )
    activated = activated_f.astype(BF16)
    live = (tier * seg + jnp.arange(seg))[None, :] < seg_lengths[:, None]
    grad_out = jnp.where(live[:, :, None], cotangent, jnp.zeros((), BF16))
    grad_act = ein("brd,df->brf", grad_out, down_wt)
    grad_pre = gate_pull(grad_act)[0].astype(BF16)
    grad_two = head_sum(ein("brf,df->brd", grad_pre, up_w).astype(BF16))
    ffn = head_sum(ein("brf,df->brd", activated, down_wt).astype(BF16))
    output = (hidden_one + ffn + down_bias).astype(BF16)

    grad_up = ein("brd,brf->df", normed_two, grad_pre).astype(BF16)
    grad_down_t = ein("brd,brf->df", grad_out, activated).astype(BF16)
    grad_hidden = grad_out.astype(F32) + norm_back(grad_two, xhat_two, r_two, norm2_gain)
    grad_branch = grad_hidden.astype(BF16)
    grad_out_t = ein("brd,bre->de", grad_branch, att).astype(BF16)
    mid_sums = small_sum(
        [
            col_sum(grad_two * xhat_two),
            col_sum(grad_two),
            col_sum(grad_pre.astype(F32)),
            col_sum(grad_out.astype(F32)),
        ]
    )
    grad_up_s = reduce_rows(grad_up)
    grad_down_s = reduce_rows(grad_down_t).T
    grad_out_s = reduce_rows(grad_out_t).T

    own_cols = lax.dynamic_slice_in_dim(out_wt, head * width, width, 1)
    gatt = ein("brd,de->bre", grad_branch, own_cols).astype(BF16)
    gq, keep, send, gtable, gbias = attend_back(
        at, probs, gatt, q, kv, kv_other, table, content_bias, position_bias, sizes
    )
    gkv = (keep.astype(F32) + swap(send, "tier").astype(F32)).astype(BF16)
    gk, gv = gkv[0], gkv[1]
    grad_k = ein("brd,bre->de", normed, gk).astype(BF16)
    grad_v = ein("brd,bre->de", normed, gv).astype(BF16)
    grad_q = ein("brd,bre->de", own_normed, gq).astype(BF16)
    grad_pos = ein("nf,ne->fe", steps, gtable.astype(BF16)).astype(BF16)

    grad_n = ein("bre,de->brd", gk, kv_w[:, :width]) + ein(
        "bre,de->brd", gv, kv_w[:, width:]
    )
    grad_q_rows = ein("bre,de->brd", gq, q_w)
    low = comp + fresh
    part = jnp.concatenate(
        [grad_n[:, :low], grad_n[:, split:] + grad_q_rows], axis=1
    ).astype(BF16)
    grad_mem = grad_n[:, low:split]
    mem_sums = jnp.stack([col_sum(grad_mem * xhat[:, low:split]), col_sum(grad_mem)])
    grad_rows = head_sum(part)
    xhat_kept = jnp.concatenate([xhat[:, :low], xhat[:, split:]], axis=1)
    r_kept = jnp.concatenate([r_one[:, :low], r_one[:, split:]], axis=1)
    grad_context = norm_back(grad_rows, xhat_kept, r_kept, norm1_gain)
    grad_comp = grad_context[:, :comp]
    grad_in = grad_hidden + grad_context[:, low:]
    fresh_own = lax.dynamic_slice_in_dim(
        grad_context[:, comp:low], head * wide, wide, 2
    ).astype(BF16)
    grad_conv = jnp.concatenate(
        [ein("bgc,bgd->cd", grouped[:, :, k], fresh_own) for k in range(KW)], axis=1
    ).astype(BF16)
    if lax.axis_size("head") == 2:
        mem_sums = mem_sums + swap(mem_sums, "head")
    else:
        mem_sums = lax.psum(mem_sums, "head")
    end_sums = small_sum(
        [
            col_sum(fresh_own.astype(F32)),
            col_sum(grad_rows * xhat_kept) + mem_sums[0],
            col_sum(grad_rows) + mem_sums[1],
            gbias[:, 0],
            gbias[:, 1],
        ]
    )
    grad_conv_s = reduce_rows(grad_conv)
    grad_conv_s = jnp.stack(
        [grad_conv_s[:, k * wide : (k + 1) * wide] for k in range(KW)]
    )
    return (
        output,
        grad_in,
        grad_comp,
        grad_conv_s,
        end_sums[0],
        end_sums[1],
        end_sums[2],
        reduce_rows(grad_q),
        reduce_rows(grad_k),
        reduce_rows(grad_v),
        reduce_rows(grad_pos),
        end_sums[3],
        end_sums[4],
        grad_out_s,
        mid_sums[0],
        mid_sums[1],
        grad_up_s,
        mid_sums[2],
        grad_down_s,
        mid_sums[3],
    )


def solution(mesh):
    rows = P("dp", "tier", None)
    by_row = P(("dp", "tier"), "head")
    by_col = P("head", ("dp", "tier"))
    conv = P(None, ("dp", "tier"), "head")
    heads = P("head", None)
    placed = (
        (rows,) * 5
        + (P("dp"),) * 3
        + (conv, P("head"), P(), P())
        + (by_row,) * 4
        + (heads, heads, by_col, P(), P(), by_row, P("head"), by_col, P())
    )
    results = (
        (rows,) * 3
        + (conv, P("head"), P(), P())
        + (by_row,) * 4
        + (heads, heads, by_col, P(), P(), by_row, P("head"), by_col, P())
    )
    return jax.shard_map(
        shards, mesh=mesh, in_specs=placed, out_specs=results, check_vma=False
    )
```

time: 2460 us -> 706 us (0.29)
  waiting for transfers between devices: 1800 us -> 331 us
  matrix products: 254 us -> 90.6 us
  other arithmetic: 163 us -> 52.4 us
  blocking collectives: 96.6 us -> 0 us
  starting transfers between devices: 3.07 us -> 91.3 us
  Pallas kernels: 0 us -> 80 us
  local copies, waits for them, and re-layouts: 113 us -> 48.5 us
    reduce_scatter x27 -> x0, waiting for transfers between devices: 1290 us -> none  [the longest x3 225 us: return_grads(): lax.psum_scatter(grads[7].astype(jnp.bfloat16), ('dp', 'tier'), scatter_d...]
    ppermute x0 -> x102, waiting for transfers between devices: none -> 331 us  [the longest x69 227 us: swap(): return lax.ppermute(x, axis, [(i, i ^ step) for i in range(n)])]
    psum x4 -> x0, waiting for transfers between devices: 187 us -> none  [the longest x1 67.2 us: micro_batch(): lax.psum(ffn_part.astype(jnp.bfloat16), 'head').astype(jnp.float32) + down_b]
    all_gather x8 -> x0, waiting for transfers between devices: 165 us -> none  [the longest x1 48.9 us: fetch_weights(): lax.all_gather(up_w, ('dp', 'tier'), axis=0, tiled=True)]
    dot_general x93 -> x25, matrix products: 254 us -> 90.6 us  [ein(): return jnp.einsum(spec, a, b, preferred_element_type=F32)]
    unnamed x41 -> x0, waiting for transfers between devices: 159 us -> none
    ppermute x0 -> x102, starting transfers between devices: none -> 91.3 us  [the longest x33 49.6 us: turn(): lax.ppermute(x, 'dp', [(i, (i // 2 + steps) % zn * 2 + i % 2) for i in ra...]
    pallas_call x0 -> x5, Pallas kernels: none -> 80 us  [the longest x1 37.4 us: attend_back(): pl.pallas_call(functools.partial(backward_kernel, sizes), grid_spec=pltpu...]
  transfers between devices with their start and end apart: 40 -> 102, of which waited for: 32 -> 40; matrix products, arithmetic and copies ran while one was open for 16% -> 16% of each run, Pallas kernels for 0% -> 11%
where the time goes in v1:
time: 706 us; the launch traced here: 696 us
  waiting for transfers between devices  331 us (47%)
  starting transfers between devices  91.3 us (13%)
  matrix products  90.6 us (13%)
  Pallas kernels  80 us (11%)
  other arithmetic  52.4 us (7%)
  local copies, waits for them, and re-layouts  48.5 us (7%)
    ppermute x69, waiting for transfers between devices, swap(): return lax.ppermute(x, axis, [(i, i ^ step) for i in range(n)])  227 us
    ppermute x33, waiting for transfers between devices, turn(): lax.ppermute(x, 'dp', [(i, (i // 2 + steps) % zn * 2 + i % 2) for i in ra...  104 us
    dot_general x25, matrix products, ein(): return jnp.einsum(spec, a, b, preferred_element_type=F32)  90.6 us
    ppermute x33, starting transfers between devices, turn(): lax.ppermute(x, 'dp', [(i, (i // 2 + steps) % zn * 2 + i % 2) for i in ra...  49.6 us
    ppermute x69, starting transfers between devices, swap(): return lax.ppermute(x, axis, [(i, i ^ step) for i in range(n)])  41.7 us
    pallas_call x1, Pallas kernels, attend_back(): pl.pallas_call(functools.partial(backward_kernel, sizes), grid_spec=pltpu...  37.4 us
    pallas_call x1, Pallas kernels, attend(): pl.pallas_call(functools.partial(forward_kernel, sizes), grid_spec=pltpu....  22.2 us
    pallas_call x3, Pallas kernels, gather_rows(): pl.pallas_call(functools.partial(place_kernel, zn, rows), grid_spec=pltpu...  20.3 us
  transfers between devices with their start and end apart: 102, of which 40 were waited for; matrix products, arithmetic and copies ran while one was open for 16% of the time, Pallas kernels for 11%

profile of v1, /device:TPU:0, one launch (start us, length us, event | category | flops | bytes accessed | tf_op | source)
XLA Modules:
  0.0 696.1 jit_solution(7613769061091352791)
XLA Ops:
  21.0 12.0 %collective-permute-done.1.refs_2_ = bf16[64,1536]{1,0:T(8,128)(2,1)S(1)} collective-permute-done((bf16[64,1536]{1,0:T(8,128)(2,1)S(1)}, bf16[64,1536]{1,0:T(8,128)(2,1)S(1)}, u32[]{:S(2)}, u32[]{:S(2)}) %collective-permute-start.1) | collective-permute-done | bytes 196640 | tf_op jit(solution)/shard_map/ppermute | solution.py:32
  62.3 7.4 %place.3 = bf16[1024,1536]{1,0:T(8,128)(2,1)} custom-call(s32[3]{0:T(128)S(1)} %pad_add_fusion.2.at_ref, bf16[64,1536]{1,0:T(8,128)(2,1)S(1)} %pad_maximum_fusion.6.refs_0_, bf16[64,1536]{1,0:T(8,128)(2,1)S(1)} %collective-permute-done.refs_1_, bf16[64,1536]{1,0:T(8,128)(2,1)S(1)} %collective-permute-done.1.refs_2_, ...), custom_call_target="tpu_custom_call" | custom-call | tf_op jit(solution)/shard_map/place/pallas_call | solution.py:82
  80.6 5.6 collective-permute-done.21.refs_6_
  86.2 5.2 collective-permute-done.20.refs_5_
  110.1 7.0 %convolution_convert_fusion.k_own.v_own = bf16[3,768,1024]{2,1,0:T(8,128)(2,1)} fusion(bf16[3,768,1024]{2,1,0:T(8,128)(2,1)S(1)} %get-tuple-element.51, bf16[1024,2048]{1,0:T(8,128)(2,1)S(1)} %copy-done.23), kind=kOutput, calls=%fused_computation.65 | convolution fusion | flops 4834197504 | bytes 11534336 | tf_op jit(solution)/shard_map/brd,de->bre/dot_general | solution.py:415
  129.5 9.4 %collective-permute-done.37.refs_4_ = bf16[64,5120]{1,0:T(8,128)(2,1)S(1)} collective-permute-done((bf16[64,5120]{1,0:T(8,128)(2,1)S(1)}, bf16[64,5120]{1,0:T(8,128)(2,1)S(1)}, u32[]{:S(2)}, u32[]{:S(2)}) %collective-permute-start.37) | collective-permute-done | bytes 655392 | tf_op jit(solution)/shard_map/ppermute | solution.py:26
  143.8 39.4 %collective-permute-done.35.refs_2_ = bf16[64,5120]{1,0:T(8,128)(2,1)} collective-permute-done((bf16[64,5120]{1,0:T(8,128)(2,1)S(1)}, bf16[64,5120]{1,0:T(8,128)(2,1)}, u32[]{:S(2)}, u32[]{:S(2)}) %collective-permute-start.35) | collective-permute-done | bytes 655392 | tf_op jit(solution)/shard_map/ppermute | solution.py:32
  189.6 22.2 %attend.1 = (bf16[3,256,512]{2,1,0:T(8,128)(2,1)S(1)}, bf16[3,4,256,1536]{3,2,1,0:T(8,128)(2,1)}) custom-call(s32[10]{0:T(128)S(1)} %pad_add_fusion.1.at, bf16[3,256,512]{2,1,0:T(8,128)(2,1)S(1)} %convolution_convert_fusion.2.q, bf16[3,768,1024]{2,1,0:T(8,128)(2,1)} %convolution_convert_fusion.k_own.v_own, ...), custom_call_target="tpu_custom_call" | custom-call | flops 3623878656 | bytes 9437184 | tf_op jit(solution)/shard_map/attend/pallas_call | solution.py:209
  215.2 12.3 %collective-permute-done.38.refs_5_ = bf16[64,5120]{1,0:T(8,128)(2,1)} collective-permute-done((bf16[64,5120]{1,0:T(8,128)(2,1)}, bf16[64,5120]{1,0:T(8,128)(2,1)}, u32[]{:S(2)}, u32[]{:S(2)}) %collective-permute-start.38) | collective-permute-done | bytes 655392 | tf_op jit(solution)/shard_map/ppermute | solution.py:26
  234.1 8.4 %place.5 = bf16[1024,5120]{1,0:T(8,128)(2,1)} custom-call(s32[3]{0:T(128)S(1)} %pad_add_fusion.2.at_ref, bf16[64,5120]{1,0:T(8,128)(2,1)S(1)} %copy-done.1, bf16[64,5120]{1,0:T(8,128)(2,1)} %collective-permute-done.34.refs_1_, bf16[64,5120]{1,0:T(8,128)(2,1)} %collective-permute-done.35.refs_2_, bf16[64,5120]{1,0:T(8,128)(2,1)} %collective-permute-done.36.refs_3_, ...), custom_call_target="tpu_custom_call" | custom-call | tf_op jit(solution)/shard_map/place/pallas_call | solution.py:82
  252.4 5.3 fusion.40
  257.7 7.3 %convert_reduce_fusion.1 = (f32[2048]{0:T(1024)S(1)}, bf16[3,256,2048]{2,1,0:T(8,128)(2,1)S(1)}) fusion(f32[3,256,2048]{2,1,0:T(8,128)S(1)} %fusion.20, f32[2048]{0:T(1024)S(1)} %copy-done.66, bf16[1024,5120]{1,0:T(8,128)(2,1)S(1)} %bitcast.369, bf16[3,256,1024]{2,1,0:T(8,128)(2,1)S(1)} %copy-done.32, pred[3,256]{1,0:T(4,128)(4,1)S(1)} %broadcast_compare_fusion), kind=kOutput, calls=%fused_computation.19 | convolution fusion | flops 3258185728 | bytes 15221760 | tf_op jit(solution)/shard_map/brd,df->brf/dot_general | solution.py:415
  270.2 5.8 bitcast_convert_fusion
  276.4 5.6 bitcast_convert_fusion.1
  289.8 16.1 %collective-permute-done.50 = bf16[3,256,1024]{2,1,0:T(8,128)(2,1)S(1)} collective-permute-done((bf16[3,256,1024]{2,1,0:T(8,128)(2,1)S(1)}, bf16[3,256,1024]{2,1,0:T(8,128)(2,1)S(1)}, u32[]{:S(2)}, u32[]{:S(2)}) %collective-permute-start.50) | collective-permute-done | bytes 1572896 | tf_op jit(solution)/shard_map/ppermute | solution.py:26
  307.6 31.3 %collective-permute-done.49 = bf16[3,256,1024]{2,1,0:T(8,128)(2,1)} collective-permute-done((bf16[3,256,1024]{2,1,0:T(8,128)(2,1)}, bf16[3,256,1024]{2,1,0:T(8,128)(2,1)}, u32[]{:S(2)}, u32[]{:S(2)}) %collective-permute-start.49) | collective-permute-done | bytes 1572896 | tf_op jit(solution)/shard_map/ppermute | solution.py:26
  338.9 5.6 convert_add_fusion.3
  345.6 37.4 %attend_back.1 = (bf16[3,256,512]{2,1,0:T(8,128)(2,1)S(1)}, bf16[2,3,768,512]{3,2,1,0:T(8,128)(2,1)}, bf16[2,3,768,512]{3,2,1,0:T(8,128)(2,1)}, f32[1536,512]{1,0:T(8,128)}, f32[4,8,128]{2,1,0:T(8,128)S(1)}) custom-call(s32[10]{0:T(128)S(1)} %pad_add_fusion.1.at, bf16[3,4,256,1536]{3,2,1,0:T(8,128)(2,1)} %get-tuple-element.28.probs, ...), custom_call_target="tpu_custom_call" | custom-call | flops 8455716864 | bytes 9437184 | tf_op jit(solution)/shard_map/attend_back/pallas_call | solution.py:341
  415.9 24.4 %collective-permute-done.84 = bf16[4,64,512]{2,1,0:T(8,128)(2,1)S(1)} collective-permute-done((bf16[4,64,512]{2,1,0:T(8,128)(2,1)S(1)}, bf16[4,64,512]{2,1,0:T(8,128)(2,1)S(1)}, u32[]{:S(2)}, u32[]{:S(2)}) %collective-permute-start.84) | collective-permute-done | bytes 262176 | tf_op jit(solution)/shard_map/ppermute | solution.py:26
  440.5 5.4 collective-permute-done.79
  485.9 8.1 %collective-permute-start.100 = (bf16[64,2048]{1,0:T(8,128)(2,1)S(1)}, bf16[64,2048]{1,0:T(8,128)(2,1)S(1)}, u32[]{:S(2)}, u32[]{:S(2)}) collective-permute-start(bf16[64,2048]{1,0:T(8,128)(2,1)S(1)} %get-tuple-element.66), channel_id=1, source_target_pairs={{0,16},{4,20},{8,24},{12,28},{16,0},{20,4},{24,8},{28,12},{1,17},{... | collective-permute-start | bytes 786440 | tf_op jit(solution)/shard_map/ppermute | solution.py:32
  494.0 14.3 %collective-permute-done.95 = bf16[64,2048]{1,0:T(8,128)(2,1)S(1)} collective-permute-done((bf16[64,2048]{1,0:T(8,128)(2,1)S(1)}, bf16[64,2048]{1,0:T(8,128)(2,1)S(1)}, u32[]{:S(2)}, u32[]{:S(2)}) %collective-permute-start.95) | collective-permute-done | bytes 262176 | tf_op jit(solution)/shard_map/ppermute | solution.py:32
  509.2 6.6 collective-permute-done.100
  518.1 6.7 bitcast_convert_fusion.3
  524.9 5.1 fusion.37
  530.0 5.5 convolution_add_fusion
  547.3 5.7 bitcast_convert_fusion.4
  553.3 59.4 %collective-permute-done.58 = f32[2,1024]{1,0:T(2,128)S(1)} collective-permute-done((f32[2,1024]{1,0:T(2,128)S(1)}, f32[2,1024]{1,0:T(2,128)S(1)}, u32[]{:S(2)}, u32[]{:S(2)}) %collective-permute-start.58) | collective-permute-done | bytes 8224 | tf_op jit(solution)/shard_map/ppermute | solution.py:26
  616.3 6.9 collective-permute-done.74
  668.2 8.0 %collective-permute-done.54 = bf16[4,64,1536]{2,1,0:T(8,128)(2,1)S(1)} collective-permute-done((bf16[4,64,1536]{2,1,0:T(8,128)(2,1)S(1)}, bf16[4,64,1536]{2,1,0:T(8,128)(2,1)S(1)}, u32[]{:S(2)}, u32[]{:S(2)}) %collective-permute-start.54) | collective-permute-done | bytes 786464 | tf_op jit(solution)/shard_map/ppermute | solution.py:26
  680.9 5.3 collective-permute-done.55
  686.2 8.8 %collective-permute-done.56 = bf16[64,1536]{1,0:T(8,128)(2,1)S(1)} collective-permute-done((bf16[64,1536]{1,0:T(8,128)(2,1)S(1)}, bf16[64,1536]{1,0:T(8,128)(2,1)S(1)}, u32[]{:S(2)}, u32[]{:S(2)}) %collective-permute-start.56) | collective-permute-done | bytes 196640 | tf_op jit(solution)/shard_map/ppermute | solution.py:32
  (508 shorter events, 279.8 us)
Async XLA Ops:
  5.5 29.6 %collective-permute-start.18 = (bf16[64,2048]{1,0:T(8,128)(2,1)S(1)}, bf16[64,2048]{1,0:T(8,128)(2,1)S(1)}, u32[]{:S(2)}, u32[]{:S(2)}) collective-permute-start(bf16[64,2048]{1,0:T(8,128)(2,1)S(1)} %constant_dynamic-update-slice_fusion.refs_0_), channel_id=1, source_target_pairs={{0,24},{4,28},{8,0},{12,4},{16,8},{20,12},{24,16},{28,20},{1,25},{... | collective-permute-start | bytes 786440 | tf_op jit(solution)/shard_map/ppermute | solution.py:32
  117.1 68.3 %collective-permute-start.31 = (bf16[3,768,1024]{2,1,0:T(8,128)(2,1)}, bf16[3,768,1024]{2,1,0:T(8,128)(2,1)}, u32[]{:S(2)}, u32[]{:S(2)}) collective-permute-start(bf16[3,768,1024]{2,1,0:T(8,128)(2,1)} %convolution_convert_fusion.k_own.v_own), channel_id=1, source_target_pairs={{0,2},{2,0},{1,3},{3,1},{4,6},{6,4},{5,7},{7,5},{8,10},{10,8},{9,1... | collective-permute-start | bytes 14155784 | tf_op jit(solution)/shard_map/ppermute | solution.py:26
  125.1 58.1 %collective-permute-start.35 = (bf16[64,5120]{1,0:T(8,128)(2,1)S(1)}, bf16[64,5120]{1,0:T(8,128)(2,1)}, u32[]{:S(2)}, u32[]{:S(2)}) collective-permute-start(bf16[64,5120]{1,0:T(8,128)(2,1)S(1)} %pad_maximum_fusion.4.refs_0_), channel_id=1, source_target_pairs={{0,16},{4,20},{8,24},{12,28},{16,0},{20,4},{24,8},{28,12},{1,17},{... | collective-permute-start | bytes 1966088 | tf_op jit(solution)/shard_map/ppermute | solution.py:32
  127.0 57.7 %collective-permute-start.34 = (bf16[64,5120]{1,0:T(8,128)(2,1)S(1)}, bf16[64,5120]{1,0:T(8,128)(2,1)}, u32[]{:S(2)}, u32[]{:S(2)}) collective-permute-start(bf16[64,5120]{1,0:T(8,128)(2,1)S(1)} %pad_maximum_fusion.4.refs_0_), channel_id=1, source_target_pairs={{0,8},{4,12},{8,16},{12,20},{16,24},{20,28},{24,0},{28,4},{1,9},{5... | collective-permute-start | bytes 1966088 | tf_op jit(solution)/shard_map/ppermute | solution.py:32
  138.9 45.8 %collective-permute-start.45 = (bf16[64,5120]{1,0:T(8,128)(2,1)S(1)}, bf16[64,5120]{1,0:T(8,128)(2,1)S(1)}, u32[]{:S(2)}, u32[]{:S(2)}) collective-permute-start(bf16[64,5120]{1,0:T(8,128)(2,1)S(1)} %collective-permute-done.37.refs_4_), channel_id=1, source_target_pairs={{0,2},{2,0},{1,3},{3,1},{4,6},{6,4},{5,7},{7,5},{8,10},{10,8},{9,1... | collective-permute-start | bytes 1966088 | tf_op jit(solution)/shard_map/ppermute | solution.py:26
  143.2 68.6 %collective-permute-start.44 = (bf16[64,5120]{1,0:T(8,128)(2,1)}, bf16[64,5120]{1,0:T(8,128)(2,1)S(1)}, u32[]{:S(2)}, u32[]{:S(2)}) collective-permute-start(bf16[64,5120]{1,0:T(8,128)(2,1)} %collective-permute-done.36.refs_3_), channel_id=1, source_target_pairs={{0,2},{2,0},{1,3},{3,1},{4,6},{6,4},{5,7},{7,5},{8,10},{10,8},{9,1... | collective-permute-start | bytes 1966088 | tf_op jit(solution)/shard_map/ppermute | solution.py:26
  183.2 31.0 %collective-permute-start.40 = (bf16[64,5120]{1,0:T(8,128)(2,1)}, bf16[64,5120]{1,0:T(8,128)(2,1)}, u32[]{:S(2)}, u32[]{:S(2)}) collective-permute-start(bf16[64,5120]{1,0:T(8,128)(2,1)} %collective-permute-done.36.refs_3_), channel_id=1, source_target_pairs={{0,4},{4,0},{8,12},{12,8},{16,20},{20,16},{24,28},{28,24},{1,5},{5... | collective-permute-start | bytes 1966088 | tf_op jit(solution)/shard_map/ppermute | solution.py:26
  184.7 29.5 %collective-permute-start.43 = (bf16[64,5120]{1,0:T(8,128)(2,1)}, bf16[64,5120]{1,0:T(8,128)(2,1)}, u32[]{:S(2)}, u32[]{:S(2)}) collective-permute-start(bf16[64,5120]{1,0:T(8,128)(2,1)} %collective-permute-done.35.refs_2_), channel_id=1, source_target_pairs={{0,2},{2,0},{1,3},{3,1},{4,6},{6,4},{5,7},{7,5},{8,10},{10,8},{9,1... | collective-permute-start | bytes 1966088 | tf_op jit(solution)/shard_map/ppermute | solution.py:26
  184.8 30.5 %collective-permute-start.39 = (bf16[64,5120]{1,0:T(8,128)(2,1)}, bf16[64,5120]{1,0:T(8,128)(2,1)}, u32[]{:S(2)}, u32[]{:S(2)}) collective-permute-start(bf16[64,5120]{1,0:T(8,128)(2,1)} %collective-permute-done.35.refs_2_), channel_id=1, source_target_pairs={{0,4},{4,0},{8,12},{12,8},{16,20},{20,16},{24,28},{28,24},{1,5},{5... | collective-permute-start | bytes 1966088 | tf_op jit(solution)/shard_map/ppermute | solution.py:26
  185.6 42.0 %collective-permute-start.38 = (bf16[64,5120]{1,0:T(8,128)(2,1)}, bf16[64,5120]{1,0:T(8,128)(2,1)}, u32[]{:S(2)}, u32[]{:S(2)}) collective-permute-start(bf16[64,5120]{1,0:T(8,128)(2,1)} %collective-permute-done.34.refs_1_), channel_id=1, source_target_pairs={{0,4},{4,0},{8,12},{12,8},{16,20},{20,16},{24,28},{28,24},{1,5},{5... | collective-permute-start | bytes 1966088 | tf_op jit(solution)/shard_map/ppermute | solution.py:26
  212.7 29.8 %collective-permute-start.32 = (bf16[3,256,512]{2,1,0:T(8,128)(2,1)S(1)}, bf16[3,256,512]{2,1,0:T(8,128)(2,1)}, u32[]{:S(2)}, u32[]{:S(2)}) collective-permute-start(bf16[3,256,512]{2,1,0:T(8,128)(2,1)S(1)} %get-tuple-element.27), channel_id=1, source_target_pairs={{0,1},{1,0},{2,3},{3,2},{4,5},{5,4},{6,7},{7,6},{8,9},{9,8},{10,11... | collective-permute-start | bytes 2359304 | tf_op jit(solution)/shard_map/ppermute | solution.py:26
  268.6 37.3 %collective-permute-start.50 = (bf16[3,256,1024]{2,1,0:T(8,128)(2,1)S(1)}, bf16[3,256,1024]{2,1,0:T(8,128)(2,1)S(1)}, u32[]{:S(2)}, u32[]{:S(2)}) collective-permute-start(bf16[3,256,1024]{2,1,0:T(8,128)(2,1)S(1)} %fusion.41), channel_id=1, source_target_pairs={{0,1},{1,0},{2,3},{3,2},{4,5},{5,4},{6,7},{7,6},{8,9},{9,8},{10,11... | collective-permute-start | bytes 4718600 | tf_op jit(solution)/shard_map/ppermute | solution.py:26
  275.9 63.0 %collective-permute-start.49 = (bf16[3,256,1024]{2,1,0:T(8,128)(2,1)}, bf16[3,256,1024]{2,1,0:T(8,128)(2,1)}, u32[]{:S(2)}, u32[]{:S(2)}) collective-permute-start(bf16[3,256,1024]{2,1,0:T(8,128)(2,1)} %fusion.40), channel_id=1, source_target_pairs={{0,1},{1,0},{2,3},{3,2},{4,5},{5,4},{6,7},{7,6},{8,9},{9,8},{10,11... | collective-permute-start | bytes 4718600 | tf_op jit(solution)/shard_map/ppermute | solution.py:26
  289.3 115.0 %collective-permute-start.92 = (bf16[4,2,64,2048]{3,2,0,1:T(8,128)(2,1)}, bf16[4,2,64,2048]{3,2,0,1:T(8,128)(2,1)S(1)}, u32[]{:S(2)}, u32[]{:S(2)}) collective-permute-start(bf16[4,2,64,2048]{3,2,0,1:T(8,128)(2,1)} %bitcast.354), channel_id=1, source_target_pairs={{0,2},{2,0},{1,3},{3,1},{4,6},{6,4},{5,7},{7,5},{8,10},{10,8},{9,1... | collective-permute-start | bytes 6291464 | tf_op jit(solution)/shard_map/ppermute | solution.py:26
  289.3 119.3 %collective-permute-start.97 = (bf16[4,2,64,2048]{3,2,0,1:T(8,128)(2,1)}, bf16[4,2,64,2048]{3,2,0,1:T(8,128)(2,1)}, u32[]{:S(2)}, u32[]{:S(2)}) collective-permute-start(bf16[4,2,64,2048]{3,2,0,1:T(8,128)(2,1)} %bitcast.353), channel_id=1, source_target_pairs={{0,2},{2,0},{1,3},{3,1},{4,6},{6,4},{5,7},{7,5},{8,10},{10,8},{9,1... | collective-permute-start | bytes 6291464 | tf_op jit(solution)/shard_map/ppermute | solution.py:26
  344.5 46.1 %collective-permute-start.88 = (f32[40,128]{1,0:T(8,128)S(1)}, f32[40,128]{1,0:T(8,128)S(1)}, u32[]{:S(2)}, u32[]{:S(2)}) collective-permute-start(f32[40,128]{1,0:T(8,128)S(1)} %maximum_bitcast_fusion), channel_id=1, source_target_pairs={{0,2},{2,0},{1,3},{3,1},{4,6},{6,4},{5,7},{7,5},{8,10},{10,8},{9,1... | collective-permute-start | bytes 61448 | tf_op jit(solution)/shard_map/ppermute | solution.py:26
  388.0 25.4 %collective-permute-start.78 = (bf16[4,2,64,512]{3,2,0,1:T(8,128)(2,1)S(1)}, bf16[4,2,64,512]{3,2,0,1:T(8,128)(2,1)S(1)}, u32[]{:S(2)}, u32[]{:S(2)}) collective-permute-start(bf16[4,2,64,512]{3,2,0,1:T(8,128)(2,1)S(1)} %bitcast.384), channel_id=1, source_target_pairs={{0,2},{2,0},{1,3},{3,1},{4,6},{6,4},{5,7},{7,5},{8,10},{10,8},{9,1... | collective-permute-start | bytes 1572872 | tf_op jit(solution)/shard_map/ppermute | solution.py:26
  405.6 111.1 %collective-permute-start.51 = (bf16[2,3,768,512]{3,2,1,0:T(8,128)(2,1)S(1)}, bf16[2,3,768,512]{3,2,1,0:T(8,128)(2,1)S(1)}, u32[]{:S(2)}, u32[]{:S(2)}) collective-permute-start(bf16[2,3,768,512]{3,2,1,0:T(8,128)(2,1)S(1)} %bitcast.402), channel_id=1, source_target_pairs={{0,2},{2,0},{1,3},{3,1},{4,6},{6,4},{5,7},{7,5},{8,10},{10,8},{9,1... | collective-permute-start | bytes 14155784 | tf_op jit(solution)/shard_map/ppermute | solution.py:26
  408.6 63.5 %collective-permute-start.93 = (bf16[4,64,2048]{2,1,0:T(8,128)(2,1)S(1)}, bf16[4,64,2048]{2,1,0:T(8,128)(2,1)S(1)}, u32[]{:S(2)}, u32[]{:S(2)}) collective-permute-start(bf16[4,64,2048]{2,1,0:T(8,128)(2,1)S(1)} %dynamic-slice_bitcast_fusion.2), channel_id=1, source_target_pairs={{0,4},{4,0},{8,12},{12,8},{16,20},{20,16},{24,28},{28,24},{1,5},{5... | collective-permute-start | bytes 3145736 | tf_op jit(solution)/shard_map/ppermute | solution.py:26
  412.8 27.5 %collective-permute-start.84 = (bf16[4,64,512]{2,1,0:T(8,128)(2,1)S(1)}, bf16[4,64,512]{2,1,0:T(8,128)(2,1)S(1)}, u32[]{:S(2)}, u32[]{:S(2)}) collective-permute-start(bf16[4,64,512]{2,1,0:T(8,128)(2,1)S(1)} %dynamic-slice_bitcast_fusion.10), channel_id=1, source_target_pairs={{0,4},{4,0},{8,12},{12,8},{16,20},{20,16},{24,28},{28,24},{1,5},{5... | collective-permute-start | bytes 786440 | tf_op jit(solution)/shard_map/ppermute | solution.py:26
  413.6 32.3 %collective-permute-start.79 = (bf16[4,64,512]{2,1,0:T(8,128)(2,1)S(1)}, bf16[4,64,512]{2,1,0:T(8,128)(2,1)S(1)}, u32[]{:S(2)}, u32[]{:S(2)}) collective-permute-start(bf16[4,64,512]{2,1,0:T(8,128)(2,1)S(1)} %dynamic-slice_bitcast_fusion.11), channel_id=1, source_target_pairs={{0,4},{4,0},{8,12},{12,8},{16,20},{20,16},{24,28},{28,24},{1,5},{5... | collective-permute-start | bytes 786440 | tf_op jit(solution)/shard_map/ppermute | solution.py:26
  415.4 35.2 %collective-permute-start.64 = (bf16[4,64,512]{2,1,0:T(8,128)(2,1)S(1)}, bf16[4,64,512]{2,1,0:T(8,128)(2,1)S(1)}, u32[]{:S(2)}, u32[]{:S(2)}) collective-permute-start(bf16[4,64,512]{2,1,0:T(8,128)(2,1)S(1)} %dynamic-slice_bitcast_fusion.14), channel_id=1, source_target_pairs={{0,4},{4,0},{8,12},{12,8},{16,20},{20,16},{24,28},{28,24},{1,5},{5... | collective-permute-start | bytes 786440 | tf_op jit(solution)/shard_map/ppermute | solution.py:26
  476.5 31.8 %collective-permute-start.95 = (bf16[64,2048]{1,0:T(8,128)(2,1)S(1)}, bf16[64,2048]{1,0:T(8,128)(2,1)S(1)}, u32[]{:S(2)}, u32[]{:S(2)}) collective-permute-start(bf16[64,2048]{1,0:T(8,128)(2,1)S(1)} %get-tuple-element.69), channel_id=1, source_target_pairs={{0,16},{4,20},{8,24},{12,28},{16,0},{20,4},{24,8},{28,12},{1,17},{... | collective-permute-start | bytes 786440 | tf_op jit(solution)/shard_map/ppermute | solution.py:32
  482.0 27.2 %collective-permute-start.99 = (bf16[64,2048]{1,0:T(8,128)(2,1)S(1)}, bf16[64,2048]{1,0:T(8,128)(2,1)S(1)}, u32[]{:S(2)}, u32[]{:S(2)}) collective-permute-start(bf16[64,2048]{1,0:T(8,128)(2,1)S(1)} %get-tuple-element.64), channel_id=1, source_target_pairs={{0,8},{4,12},{8,16},{12,20},{16,24},{20,28},{24,0},{28,4},{1,9},{5... | collective-permute-start | bytes 786440 | tf_op jit(solution)/shard_map/ppermute | solution.py:32
  485.9 29.9 %collective-permute-start.100 = (bf16[64,2048]{1,0:T(8,128)(2,1)S(1)}, bf16[64,2048]{1,0:T(8,128)(2,1)S(1)}, u32[]{:S(2)}, u32[]{:S(2)}) collective-permute-start(bf16[64,2048]{1,0:T(8,128)(2,1)S(1)} %get-tuple-element.66), channel_id=1, source_target_pairs={{0,16},{4,20},{8,24},{12,28},{16,0},{20,4},{24,8},{28,12},{1,17},{... | collective-permute-start | bytes 786440 | tf_op jit(solution)/shard_map/ppermute | solution.py:32
  539.8 72.9 %collective-permute-start.73 = (bf16[4,2,64,512]{3,2,0,1:T(8,128)(2,1)}, bf16[4,2,64,512]{3,2,0,1:T(8,128)(2,1)}, u32[]{:S(2)}, u32[]{:S(2)}) collective-permute-start(bf16[4,2,64,512]{3,2,0,1:T(8,128)(2,1)} %bitcast.357), channel_id=1, source_target_pairs={{0,2},{2,0},{1,3},{3,1},{4,6},{6,4},{5,7},{7,5},{8,10},{10,8},{9,1... | collective-permute-start | bytes 1572872 | tf_op jit(solution)/shard_map/ppermute | solution.py:26
  541.8 86.4 %collective-permute-start.52 = (bf16[3,512,1024]{2,1,0:T(8,128)(2,1)}, bf16[3,512,1024]{2,1,0:T(8,128)(2,1)}, u32[]{:S(2)}, u32[]{:S(2)}) collective-permute-start(bf16[3,512,1024]{2,1,0:T(8,128)(2,1)} %pad_maximum_fusion.2), channel_id=1, source_target_pairs={{0,1},{1,0},{2,3},{3,2},{4,5},{5,4},{6,7},{7,6},{8,9},{9,8},{10,11... | collective-permute-start | bytes 9437192 | tf_op jit(solution)/shard_map/ppermute | solution.py:26
  546.7 66.0 %collective-permute-start.58 = (f32[2,1024]{1,0:T(2,128)S(1)}, f32[2,1024]{1,0:T(2,128)S(1)}, u32[]{:S(2)}, u32[]{:S(2)}) collective-permute-start(f32[2,1024]{1,0:T(2,128)S(1)} %pad_maximum_fusion.7), channel_id=1, source_target_pairs={{0,1},{1,0},{2,3},{3,2},{4,5},{5,4},{6,7},{7,6},{8,9},{9,8},{10,11... | collective-permute-start | bytes 24584 | tf_op jit(solution)/shard_map/ppermute | solution.py:26
  553.2 62.2 %collective-permute-start.68 = (bf16[4,2,64,512]{3,2,0,1:T(8,128)(2,1)S(1)}, bf16[4,2,64,512]{3,2,0,1:T(8,128)(2,1)S(1)}, u32[]{:S(2)}, u32[]{:S(2)}) collective-permute-start(bf16[4,2,64,512]{3,2,0,1:T(8,128)(2,1)S(1)} %bitcast.387), channel_id=1, source_target_pairs={{0,2},{2,0},{1,3},{3,1},{4,6},{6,4},{5,7},{7,5},{8,10},{10,8},{9,1... | collective-permute-start | bytes 1572872 | tf_op jit(solution)/shard_map/ppermute | solution.py:26
  624.1 25.4 %collective-permute-start.75 = (bf16[64,512]{1,0:T(8,128)(2,1)}, bf16[64,512]{1,0:T(8,128)(2,1)S(1)}, u32[]{:S(2)}, u32[]{:S(2)}) collective-permute-start(bf16[64,512]{1,0:T(8,128)(2,1)} %get-tuple-element.94), channel_id=1, source_target_pairs={{0,8},{4,12},{8,16},{12,20},{16,24},{20,28},{24,0},{28,4},{1,9},{5... | collective-permute-start | bytes 196616 | tf_op jit(solution)/shard_map/ppermute | solution.py:32
  624.1 28.7 %collective-permute-start.77 = (bf16[64,512]{1,0:T(8,128)(2,1)}, bf16[64,512]{1,0:T(8,128)(2,1)S(1)}, u32[]{:S(2)}, u32[]{:S(2)}) collective-permute-start(bf16[64,512]{1,0:T(8,128)(2,1)} %get-tuple-element.95), channel_id=1, source_target_pairs={{0,24},{4,28},{8,0},{12,4},{16,8},{20,12},{24,16},{28,20},{1,25},{... | collective-permute-start | bytes 196616 | tf_op jit(solution)/shard_map/ppermute | solution.py:32
  628.1 25.8 %collective-permute-start.76 = (bf16[64,512]{1,0:T(8,128)(2,1)}, bf16[64,512]{1,0:T(8,128)(2,1)}, u32[]{:S(2)}, u32[]{:S(2)}) collective-permute-start(bf16[64,512]{1,0:T(8,128)(2,1)} %get-tuple-element.96), channel_id=1, source_target_pairs={{0,16},{4,20},{8,24},{12,28},{16,0},{20,4},{24,8},{28,12},{1,17},{... | collective-permute-start | bytes 196616 | tf_op jit(solution)/shard_map/ppermute | solution.py:32
  (156 other events, 1833.4 us)

commit v2 on v1

v2 whole, which is shorter than its diff:
```python
import functools
import math

import jax
import jax.numpy as jnp
import ml_dtypes
import numpy as np
from jax import lax
from jax.experimental import pallas as pl
from jax.experimental.pallas import tpu as pltpu
from jax.sharding import PartitionSpec as P

D = 1024
MEM = 512
CMEM = 512
KW = 3
OLDC = 384
EPS = 1e-05
NEG = -1e30
F32 = jnp.float32
BF16 = jnp.bfloat16


def swap(x, axis, step=1):
    n = lax.axis_size(axis)
    return lax.ppermute(x, axis, [(i, i ^ step) for i in range(n)])


def after(x, *others):
    return lax.optimization_barrier((x, *others))[0]


def z_exchange(x):
    n = lax.axis_size("dp")
    groups = [[z * 2 + y for z in range(n // 2)] for y in range(2)]
    return lax.all_to_all(x, "dp", 0, 0, axis_index_groups=groups, tiled=True)


def head_gather(x):
    if lax.axis_size("head") == 2:
        other = swap(x, "head")
        first = lax.axis_index("head") == 0
        return jnp.concatenate(
            [jnp.where(first, x, other), jnp.where(first, other, x)], axis=-1
        )
    return lax.all_gather(x, "head", axis=x.ndim - 1, tiled=True)


def place_kernel(at_ref, b0, b1, b2, b3, out, sems):
    y, t = at_ref[0], at_ref[1]
    copies = []
    for k, block in enumerate((b0, b1, b2, b3)):
        yy = 1 - y if k % 2 else y
        tt = 1 - t if k // 2 else t
        copies.append(pltpu.make_async_copy(block, out.at[:, yy, tt], sems.at[k]))
    for copy in copies:
        copy.start()
    for copy in copies:
        copy.wait()


def gather_z(x):
    zn = lax.axis_size("dp") // 2
    return z_exchange(jnp.broadcast_to(x[None], (zn,) + x.shape))


def gather_yt(over_z):
    other = swap(over_z, "dp")
    return [over_z, other, swap(over_z, "tier"), swap(other, "tier")]


def place(blocks):
    zn, rows, cols = blocks[0].shape
    shape = (zn, 2, 2, rows, cols)
    at = jnp.stack([lax.axis_index("dp") % 2, lax.axis_index("tier")])
    out = pl.pallas_call(
        place_kernel,
        grid_spec=pltpu.PrefetchScalarGridSpec(
            num_scalar_prefetch=1,
            grid=(1,),
            in_specs=[pl.BlockSpec(memory_space=pl.ANY)] * 4,
            out_specs=pl.BlockSpec(shape, lambda i, s: (0, 0, 0, 0, 0)),
            scratch_shapes=[pltpu.SemaphoreType.DMA((4,))],
        ),
        out_shape=jax.ShapeDtypeStruct(shape, blocks[0].dtype),
        compiler_params=pltpu.CompilerParams(vmem_limit_bytes=60 << 20),
        cost_estimate=cost(3),
        name="place",
    )(at.astype(jnp.int32), *blocks)
    return out.reshape(zn * 4 * rows, cols)


def small_sum(parts):
    flat = jnp.concatenate([p.reshape(-1) for p in parts])
    pad = -flat.shape[0] % 1024
    flat = jnp.pad(flat, (0, pad)).reshape(-1, 128)
    n = lax.axis_size("dp")
    if n & (n - 1):
        flat = lax.psum(flat, ("dp", "tier"))
    else:
        flat = flat + swap(flat, "tier")
        step = 1
        while step < n:
            flat = flat + swap(flat, "dp", step)
            step *= 2
    flat = flat.reshape(-1)
    out, at = [], 0
    for p in parts:
        out.append(flat[at : at + p.size].reshape(p.shape))
        at += p.size
    return out


def dot(a, b, contract):
    return lax.dot_general(a, b, (contract, ((), ())), preferred_element_type=F32)


NN = ((1,), (0,))
NT = ((1,), (1,))
TN = ((0,), (0,))


def params(mib=60):
    return pltpu.CompilerParams(vmem_limit_bytes=mib << 20)


def cost(us):
    return pl.CostEstimate(
        flops=int(us * 1.15e9), bytes_accessed=1024, transcendentals=0
    )


def whole(shape):
    return pl.BlockSpec(shape, lambda *i: (0,) * len(shape))


def stream(b, rows, cols=D):
    return pl.BlockSpec((1, rows, cols), lambda *i: (b, 0, 0))


def key_pieces(sizes):
    comp, fresh, mem, seg = sizes
    return (
        (0, 0, comp),
        (comp, OLDC, fresh),
        (comp + fresh, CMEM, mem),
        (comp + fresh + mem, CMEM + MEM, seg),
    )


def in_order(full, own, other, tier, sizes):
    for row, pos, rows in key_pieces(sizes):
        mine = pl.multiple_of(pos + tier * rows, rows)
        theirs = pl.multiple_of(pos + (1 - tier) * rows, rows)
        full[pl.ds(mine, rows)] = own[0, row : row + rows]
        full[pl.ds(theirs, rows)] = other[0, row : row + rows]


def project_kernel(comp, fresh, mem, seg, w, normed, kv, q):
    at = 0
    for piece in (comp, fresh, mem, seg):
        rows = piece.shape[1]
        normed[0, at : at + rows] = piece[0]
        at += rows
    width = q.shape[2]
    kv[0] = dot(normed[0], w[:, : 2 * width], NN).astype(BF16)
    first = at - seg.shape[1]
    q[0] = dot(normed[0, first:], w[:, 2 * width : 3 * width], NN).astype(BF16)


def project(comp, fresh, mem, seg, w):
    batch = comp.shape[0]
    width = w.shape[1] // 4
    pieces = (comp, fresh, mem, seg)
    rows = sum(p.shape[1] for p in pieces)

    def block(n, cols=D):
        return pl.BlockSpec((1, n, cols), lambda b: (b, 0, 0))

    shapes = ((rows, D), (rows, 2 * width), (seg.shape[1], width))
    return pl.pallas_call(
        project_kernel,
        grid=(batch,),
        in_specs=[block(p.shape[1]) for p in pieces] + [whole(w.shape)],
        out_specs=[block(*shape) for shape in shapes],
        out_shape=[jax.ShapeDtypeStruct((batch,) + shape, BF16) for shape in shapes],
        compiler_params=params(),
        cost_estimate=cost(50),
        name="project",
    )(*pieces, w)


def forward_kernel(
    b, sizes, at, q, k_own, k_other, v_own, v_other, table, cb, pb, att, probs, kf, vf
):
    tier = at[0]
    comp_fill, mem_fill, seg_len = at[2 + 3 * b], at[3 + 3 * b], at[4 + 3 * b]
    rows = q.shape[1]
    keys = kf.shape[0]
    in_order(kf, k_own, k_other, tier, sizes)
    in_order(vf, v_own, v_other, tier, sizes)
    query = q[0].astype(F32)
    content_q = (query + cb[0]).astype(BF16)
    position_q = (query + pb[0]).astype(BF16)
    scale = 1.0 / math.sqrt(q.shape[2])
    relative = dot(position_q, table[...], NT)
    relative = pltpu.roll(relative, keys - rows + 1, 1, stride=1, stride_axis=0)
    scores = (dot(content_q, kf[...], NT) + relative) * scale
    start = CMEM + MEM
    j = lax.broadcasted_iota(jnp.int32, (1, keys), 1)
    lowest = jnp.where(
        j < CMEM, CMEM - comp_fill, jnp.where(j < start, start - mem_fill, start)
    )
    beyond = jnp.where(j < start, start, start + seg_len)
    open_col = (j >= lowest) & (j < beyond)
    bias = jnp.where(open_col, 0.0, NEG)
    i = lax.broadcasted_iota(jnp.int32, (rows, keys), 0) + tier * rows
    jj = lax.broadcasted_iota(jnp.int32, (rows, keys), 1) - start
    masked = jnp.where(jj <= i, scores + bias, NEG)
    peak = jnp.max(masked, axis=-1, keepdims=True)
    e = jnp.exp(masked - peak)
    total = jnp.sum(e, axis=-1, keepdims=True)
    p = (e * (1.0 / total)).astype(BF16)
    probs[0] = p
    att[...] = dot(p, vf[...], NN).astype(BF16)


def attend(b, at, q, kv, kv_other, table, cb, pb, sizes):
    _, rows, width = q.shape
    heads = cb.shape[0]
    hd = width // heads
    keys_local = kv.shape[1]
    keys = 2 * keys_local

    def col(off):
        return pl.BlockSpec((1, keys_local, hd), lambda h, s: (b, 0, h + off))

    def bias():
        return pl.BlockSpec((1, 1, hd), lambda h, s: (h, 0, 0))

    return pl.pallas_call(
        functools.partial(forward_kernel, b, sizes),
        grid_spec=pltpu.PrefetchScalarGridSpec(
            num_scalar_prefetch=1,
            grid=(heads,),
            in_specs=[
                pl.BlockSpec((1, rows, hd), lambda h, s: (b, 0, h)),
                col(0),
                col(0),
                col(heads),
                col(heads),
                pl.BlockSpec((keys, hd), lambda h, s: (0, h)),
                bias(),
                bias(),
            ],
            out_specs=[
                pl.BlockSpec((rows, hd), lambda h, s: (0, h)),
                pl.BlockSpec((1, rows, keys), lambda h, s: (h, 0, 0)),
            ],
            scratch_shapes=[pltpu.VMEM((keys, hd), BF16), pltpu.VMEM((keys, hd), BF16)],
        ),
        out_shape=[
            jax.ShapeDtypeStruct((rows, width), BF16),
            jax.ShapeDtypeStruct((heads, rows, keys), BF16),
        ],
        compiler_params=params(),
        cost_estimate=cost(20),
        name="attend",
    )(at, q, kv, kv_other, kv, kv_other, table, cb[:, None], pb[:, None])


def standardize(rows):
    mean = jnp.mean(rows, axis=-1, keepdims=True)
    centred = rows - mean
    var = jnp.mean(centred * centred, axis=-1, keepdims=True)
    r = lax.rsqrt(var + EPS)
    return centred * r, r


def norm_back(grad, xhat, r, gain):
    g = grad * gain
    return r * (
        g
        - jnp.mean(g, axis=-1, keepdims=True)
        - xhat * jnp.mean(g * xhat, axis=-1, keepdims=True)
    )


def row_sums(values, width):
    sums = [jnp.sum(v, axis=0, keepdims=True) for v in values]
    return jnp.concatenate(sums + [jnp.zeros((8 - len(sums), width), F32)], axis=0)


def ffn_kernel(batch, parts, full, at, *refs):
    count = batch * parts
    atts = refs[:count]
    x, cot, gain, shift, up_b, w = refs[count : count + 6]
    outs = refs[count + 6 :]
    kept_out, (sums_up, sums_out) = outs[:5], outs[5:7]
    twos, ffns = outs[7 : 7 + batch], outs[7 + batch : 7 + 2 * batch]
    kept, (wv, w_sem, sem) = outs[7 + 2 * batch : -3], outs[-3:]
    hidden, n2, go, act, gpre = kept
    hid = act.shape[1]
    hb = min(512, hid)
    steps = hid // hb
    tier, head = at[0], at[1]
    rows = x.shape[1]

    def fetch(k, first, cols):
        part = slice(first, first + cols)
        return pltpu.make_async_copy(w.at[:, part], wv.at[:, part], w_sem.at[k])

    copies = [fetch(0, 0, full), fetch(1, full, hid), fetch(2, full + hid, hid)]
    for copy in copies:
        copy.start()
    going = []

    def give(k, cols):
        copy = pltpu.make_async_copy(
            kept[k].at[:, cols], kept_out[k].at[:, cols], sem.at[len(going)]
        )
        copy.start()
        going.append(copy)

    every = slice(0, D)
    total = None
    for b in range(batch):
        row = lax.broadcasted_iota(jnp.int32, (rows, 1), 0) + tier * rows
        masked = jnp.where(row < at[4 + 3 * b], cot[b].astype(F32), 0.0)
        go[b * rows : (b + 1) * rows] = masked.astype(BF16)
        sums = row_sums([masked], D)
        total = sums if total is None else total + sums
    sums_out[...] = total
    give(2, every)
    copies[0].wait()
    if parts == 2:
        first = head == 0
        att = jnp.concatenate(
            [
                jnp.concatenate(
                    [
                        jnp.where(first, atts[2 * b][...], atts[2 * b + 1][...]),
                        jnp.where(first, atts[2 * b + 1][...], atts[2 * b][...]),
                    ],
                    axis=1,
                )
                for b in range(batch)
            ],
            axis=0,
        )
    else:
        att = jnp.concatenate([a[...] for a in atts], axis=0)
    h = x[...].reshape(batch * rows, D).astype(F32) + dot(att, wv[:, :full], NT)
    hidden[...] = h
    give(0, every)
    xhat, _ = standardize(h)
    n2[...] = (xhat * gain[...] + shift[...]).astype(BF16)
    give(1, every)
    copies[1].wait()
    copies[2].wait()
    c = math.sqrt(2.0 / math.pi)
    ck = c * 0.044715
    for j in range(steps):
        cols = slice(j * hb, (j + 1) * hb)
        up = wv[:, full + j * hb : full + (j + 1) * hb]
        down = wv[:, full + hid + j * hb : full + hid + (j + 1) * hb]
        pre = dot(n2[...], up, NN) + up_b[:, cols]
        g_act = dot(go[...], down, NN)
        sq = pre * pre
        half = 0.5 + 0.5 * jnp.tanh(pre * (c + ck * sq))
        a = pre * half
        slope = half + a * (1.0 - half) * (2 * c + 6 * ck * sq)
        g = (g_act * slope).astype(BF16)
        act[:, cols] = a.astype(BF16)
        gpre[:, cols] = g
        sums_up[:, cols] = row_sums([g.astype(F32)], hb)
        give(3, cols)
        give(4, cols)
    for outs_of, k, first in ((twos, 4, full), (ffns, 3, full + hid)):
        product = dot(kept[k][...], wv[:, first : first + hid], NT).astype(BF16)
        for b in range(batch):
            outs_of[b][...] = product[b * rows : (b + 1) * rows]
    for copy in going:
        copy.wait()


def feed_forward(at, atts, x, cot, w_ffn, full, gain, shift, up_b):
    batch, rows, _ = x.shape
    hidden_n = (w_ffn.shape[1] - full) // 2
    steps = hidden_n // min(512, hidden_n)
    every = batch * rows
    anywhere = pl.BlockSpec(memory_space=pl.ANY)
    kept = [(D, F32), (D, BF16), (D, BF16), (hidden_n, BF16), (hidden_n, BF16)]
    return pl.pallas_call(
        functools.partial(ffn_kernel, batch, len(atts) // batch, full),
        grid_spec=pltpu.PrefetchScalarGridSpec(
            num_scalar_prefetch=1,
            grid=(1,),
            in_specs=[whole(a.shape) for a in atts]
            + [whole(x.shape)] * 2
            + [whole((1, D)), whole((1, D)), whole((1, hidden_n)), anywhere],
            out_specs=[anywhere] * 5
            + [whole((8, hidden_n)), whole((8, D))]
            + [whole((rows, D))] * (2 * batch),
            scratch_shapes=[pltpu.VMEM((every, n), dtype) for n, dtype in kept]
            + [
                pltpu.VMEM(w_ffn.shape, BF16),
                pltpu.SemaphoreType.DMA((3,)),
                pltpu.SemaphoreType.DMA((3 + 2 * steps,)),
            ],
        ),
        out_shape=[jax.ShapeDtypeStruct((every, n), dtype) for n, dtype in kept]
        + [jax.ShapeDtypeStruct((8, hidden_n), F32), jax.ShapeDtypeStruct((8, D), F32)]
        + [jax.ShapeDtypeStruct((rows, D), BF16)] * (2 * batch),
        compiler_params=params(),
        cost_estimate=cost(50),
        name="feed_forward",
    )(at, *atts, x, cot, gain[None], shift[None], up_b[None], w_ffn)


def backward_kernel(sizes, parts, chained, at, *refs):
    twos, refs = refs[:parts], refs[parts:]
    hidden, go, gain, w = refs[:4]
    (probs, q, k_own, k_other, v_own, v_other, table, cb, pb) = refs[4:13]
    refs = refs[13:]
    if chained:
        before, refs = refs[0], refs[1:]
    ghid, gbr, sums, gq, keep, send, gtable, gbias, kf, vf, gk, gatt = refs
    tier = at[0]
    step = pl.program_id(0)
    rows, hd = q.shape[1], q.shape[2]

    @pl.when(step == 0)
    def _():
        grad = summed(twos, slice(None))
        xhat, r = standardize(hidden[...])
        g = go[...].astype(F32) + norm_back(grad, xhat, r, gain[...])
        ghid[...] = g
        low = g.astype(BF16)
        gbr[...] = low
        out = dot(low, w[...], NN).astype(BF16)
        for k in range(gatt.shape[0]):
            gatt[k] = out[:, k * hd : (k + 1) * hd]
        sums[...] = row_sums([grad * xhat, grad], D)

    @pl.when(step > 0)
    def _():
        in_order(kf, k_own, k_other, tier, sizes)
        in_order(vf, v_own, v_other, tier, sizes)
        query = q[0].astype(F32)
        content_q = (query + cb[0]).astype(BF16)
        position_q = (query + pb[0]).astype(BF16)
        scale = 1.0 / math.sqrt(hd)
        ga = gatt[step - 1]
        p_low = probs[0]
        p = p_low.astype(F32)
        gp = dot(ga, vf[...], NT)
        row_dot = jnp.sum(p * gp, axis=-1, keepdims=True)
        ds = (p * (gp - row_dot)).astype(BF16)

        def hand_out(which, value):
            gk[...] = value.astype(BF16)
            for row, pos, size in key_pieces(sizes):
                mine = pl.multiple_of(pos + tier * size, size)
                theirs = pl.multiple_of(pos + (1 - tier) * size, size)
                keep[which, row : row + size] = gk[pl.ds(mine, size)]
                send[which, row : row + size] = gk[pl.ds(theirs, size)]

        hand_out(0, dot(ds, content_q, TN) * scale)
        hand_out(1, dot(p_low, ga, TN))
        g_content = dot(ds, kf[...], NN) * scale
        r = lax.broadcasted_iota(jnp.int32, (rows, rows), 0)
        c = lax.broadcasted_iota(jnp.int32, (rows, rows), 1)
        flip = jnp.where(r + c == rows - 1, 1.0, 0.0).astype(BF16)
        ds_flip = dot(flip, ds, NN)
        skewed = pltpu.roll(ds_flip, 0, 1, stride=1, stride_axis=0).astype(BF16)
        position_flip = dot(flip, position_q, NN).astype(BF16)
        g_table = dot(position_flip, skewed, TN) * scale
        g_flip = dot(skewed, table[...], NN) * scale
        high = g_flip.astype(BF16)
        low = (g_flip - high.astype(F32)).astype(BF16)
        g_position = dot(flip, high, NN) + dot(flip, low, NN)
        gq[...] = (g_content + g_position).astype(BF16)
        gbias[0] = row_sums([g_content, g_position], hd)
        if chained:
            g_table = g_table + before[...]
        gtable[...] = g_table


def attend_back(
    b, at, twos, hidden, go, gain, w, probs, q, kv, kv_other, table, cb, pb, sizes, before
):
    _, rows, width = q.shape
    heads = cb.shape[0]
    hd = width // heads
    keys_local = kv.shape[1]
    keys = 2 * keys_local
    chained = before is not None

    def of(h):
        return jnp.maximum(h - 1, 0)

    def col(off):
        return pl.BlockSpec((1, keys_local, hd), lambda h, s: (b, 0, of(h) + off))

    def half():
        return pl.BlockSpec((2, keys_local, hd), lambda h, s: (0, 0, of(h)))

    def bias():
        return pl.BlockSpec((1, 1, hd), lambda h, s: (of(h), 0, 0))

    def turned():
        return pl.BlockSpec((hd, keys), lambda h, s: (of(h), 0))

    def own_rows():
        return pl.BlockSpec((rows, D), lambda h, s: (b, 0))

    args = [at, *twos, hidden, go, gain[None], w]
    args += [probs, q, kv, kv_other, kv, kv_other, table]
    args += [cb[:, None], pb[:, None]]
    return pl.pallas_call(
        functools.partial(backward_kernel, sizes, len(twos), chained),
        grid_spec=pltpu.PrefetchScalarGridSpec(
            num_scalar_prefetch=1,
            grid=(1 + heads,),
            in_specs=[whole((rows, D)) for _ in twos]
            + [
                own_rows(),
                own_rows(),
                whole((1, D)),
                pl.BlockSpec((D, width), lambda h, s: (0, s[1])),
                pl.BlockSpec((1, rows, keys), lambda h, s: (of(h), 0, 0)),
                pl.BlockSpec((1, rows, hd), lambda h, s: (b, 0, of(h))),
                col(0),
                col(0),
                col(heads),
                col(heads),
                pl.BlockSpec((keys, hd), lambda h, s: (0, of(h))),
                bias(),
                bias(),
            ]
            + ([turned()] if chained else []),
            out_specs=[
                whole((rows, D)),
                whole((rows, D)),
                whole((8, D)),
                pl.BlockSpec((rows, hd), lambda h, s: (0, of(h))),
                half(),
                half(),
                turned(),
                pl.BlockSpec((1, 8, hd), lambda h, s: (of(h), 0, 0)),
            ],
            scratch_shapes=[pltpu.VMEM((keys, hd), BF16)] * 3
            + [pltpu.VMEM((heads, rows, hd), BF16)],
        ),
        out_shape=[
            jax.ShapeDtypeStruct((rows, D), F32),
            jax.ShapeDtypeStruct((rows, D), BF16),
            jax.ShapeDtypeStruct((8, D), F32),
            jax.ShapeDtypeStruct((rows, width), BF16),
            jax.ShapeDtypeStruct((2, keys_local, width), BF16),
            jax.ShapeDtypeStruct((2, keys_local, width), BF16),
            jax.ShapeDtypeStruct((width, keys), F32),
            jax.ShapeDtypeStruct((heads, 8, hd), F32),
        ],
        compiler_params=params(),
        cost_estimate=cost(50),
        name="attend_back",
    )(*args, *([before] if chained else []))


def rows_kernel(sizes, keep, got, gq, normed_mem, w, gkv, part, fpart, sums, both):
    comp, fresh, mem, seg = sizes
    width = gq.shape[1]

    @pl.when(pl.program_id(0) == 0)
    def _():
        for k in range(2):
            total = keep[k].astype(F32) + got[k].astype(F32)
            both[:, k * width : (k + 1) * width] = total.astype(BF16)
        gkv[...] = both[...]

    low = comp + fresh
    split = low + mem
    grad = dot(both[...], w[:, : 2 * width], NT)
    part[:comp] = grad[:comp].astype(BF16)
    fpart[...] = grad[comp:low].astype(BF16)
    part[comp:] = (
        grad[split:] + dot(gq[...], w[:, 2 * width : 3 * width], NT)
    ).astype(BF16)
    g_mem = grad[low:split]
    sums[...] = row_sums([g_mem * normed_mem[0].astype(F32), g_mem], g_mem.shape[1])


def rows_back(b, keep, got, gq, normed_mem, w, sizes):
    width = gq.shape[1]
    local = keep.shape[1]
    comp, fresh, mem, seg = sizes
    kept = comp + seg
    db = 256
    return pl.pallas_call(
        functools.partial(rows_kernel, sizes),
        grid=(D // db,),
        in_specs=[
            whole((2, local, width)),
            whole((2, local, width)),
            whole((seg, width)),
            pl.BlockSpec((1, mem, db), lambda j: (b, 0, j)),
            pl.BlockSpec((db, 4 * width), lambda j: (j, 0)),
        ],
        out_specs=[
            whole((local, 2 * width)),
            pl.BlockSpec((kept, db), lambda j: (0, j)),
            pl.BlockSpec((fresh, db), lambda j: (0, j)),
            pl.BlockSpec((8, db), lambda j: (0, j)),
        ],
        out_shape=[
            jax.ShapeDtypeStruct((local, 2 * width), BF16),
            jax.ShapeDtypeStruct((kept, D), BF16),
            jax.ShapeDtypeStruct((fresh, D), BF16),
            jax.ShapeDtypeStruct((8, D), F32),
        ],
        scratch_shapes=[pltpu.VMEM((local, 2 * width), BF16)],
        compiler_params=params(),
        cost_estimate=cost(3),
        name="rows_back",
    )(keep, got, gq, normed_mem, w)


def summed(refs, part):
    total = refs[0][part].astype(F32)
    for other in refs[1:]:
        total = total + other[part].astype(F32)
    return total


def context_kernel(sizes, parts, chained, *refs):
    grads = refs[:parts]
    comp, seg, ghid, gain = refs[parts : parts + 4]
    gcomp, gin, sums = refs[parts + 4 + (2 if chained else 0) :]
    rows = comp.shape[1]
    total = None
    for raw, part in ((comp, slice(0, rows)), (seg, slice(rows, None))):
        grad = summed(grads, part)
        xhat, r = standardize(raw[0].astype(F32))
        g = norm_back(grad, xhat, r, gain[...])
        part_sums = row_sums([grad * xhat, grad], D)
        if total is None:
            gcomp[0] = g
            total = part_sums
        else:
            gin[0] = ghid[...] + g
            total = total + part_sums
    sums[...] = total


def context_back(b, grads, comp, seg, ghid, gain, before, sizes):
    batch = comp.shape[0]
    kept = grads[0].shape[0]
    chained = before is not None
    n_comp, _, _, n_seg = sizes
    first = len(grads) + 4
    return pl.pallas_call(
        functools.partial(context_kernel, sizes, len(grads), chained),
        grid=(1,),
        in_specs=[whole((kept, D)) for _ in grads]
        + [stream(b, n_comp), stream(b, n_seg), whole((n_seg, D)), whole((1, D))]
        + ([pl.BlockSpec(memory_space=pl.ANY)] * 2 if chained else []),
        out_specs=[stream(b, n_comp), stream(b, n_seg), whole((8, D))],
        out_shape=[
            jax.ShapeDtypeStruct((batch, n_comp, D), F32),
            jax.ShapeDtypeStruct((batch, n_seg, D), F32),
            jax.ShapeDtypeStruct((8, D), F32),
        ],
        input_output_aliases={first: 0, first + 1: 1} if chained else {},
        compiler_params=params(),
        cost_estimate=cost(3),
        name="context_back",
    )(*grads, comp, seg, ghid, gain[None], *(before if chained else ()))


def fresh_kernel(batch, *refs):
    count = len(refs) - 4
    raw, gain, gfresh, sums = refs[count:]
    per = count // batch
    total = None
    for b in range(batch):
        grad = summed(refs[b * per : (b + 1) * per], slice(None))
        xhat, r = standardize(raw[b].astype(F32))
        rows = xhat.shape[0]
        g = norm_back(grad, xhat, r, gain[...])
        gfresh[b * rows : (b + 1) * rows] = g.astype(BF16)
        part_sums = row_sums([grad * xhat, grad, g.astype(BF16).astype(F32)], D)
        total = part_sums if total is None else total + part_sums
    sums[...] = total


def fresh_back(grads, raw, gain):
    batch, rows, _ = raw.shape
    flat = [g for pair in grads for g in pair]
    return pl.pallas_call(
        functools.partial(fresh_kernel, batch),
        grid=(1,),
        in_specs=[whole((rows, D)) for _ in flat] + [whole(raw.shape), whole((1, D))],
        out_specs=[whole((batch * rows, D)), whole((8, D))],
        out_shape=[
            jax.ShapeDtypeStruct((batch * rows, D), BF16),
            jax.ShapeDtypeStruct((8, D), F32),
        ],
        compiler_params=params(),
        cost_estimate=cost(2),
        name="fresh_back",
    )(*flat, raw, gain[None])


def table_kernel(at, steps, w, out):
    out[...] = dot(steps[...], w[...], NN).astype(BF16)


def position_table(at, steps, w, seg, keys, col, width):
    return pl.pallas_call(
        table_kernel,
        grid_spec=pltpu.PrefetchScalarGridSpec(
            num_scalar_prefetch=1,
            grid=(keys // seg,),
            in_specs=[
                pl.BlockSpec((seg, D), lambda i, s: (1 - s[0] + i, 0)),
                pl.BlockSpec((D, width), lambda i, s: (0, col)),
            ],
            out_specs=pl.BlockSpec((seg, width), lambda i, s: (i, 0)),
        ),
        out_shape=jax.ShapeDtypeStruct((keys, width), BF16),
        compiler_params=params(),
        cost_estimate=cost(20),
        name="position_table",
    )(at, steps, w)


def grad_ffn_kernel(steps, n2, gpre, go, act, out):
    j = pl.program_id(0)

    @pl.when(j < steps)
    def _():
        out[...] = dot(n2[...], gpre[...], TN).astype(BF16)

    @pl.when(j >= steps)
    def _():
        out[...] = dot(go[...], act[...], TN).astype(BF16)


def grad_ffn(n2, gpre, go, act):
    rows, hidden = act.shape
    hb = min(512, hidden)
    steps = hidden // hb

    def block(first):
        return pl.BlockSpec(
            (rows, hb), lambda j: (0, jnp.clip(j - first, 0, steps - 1))
        )

    return pl.pallas_call(
        functools.partial(grad_ffn_kernel, steps),
        grid=(2 * steps,),
        in_specs=[whole((rows, D)), block(0), whole((rows, D)), block(steps)],
        out_specs=pl.BlockSpec((D, hb), lambda j: (0, j)),
        out_shape=jax.ShapeDtypeStruct((D, 2 * hidden), BF16),
        compiler_params=params(),
        cost_estimate=cost(30),
        name="grad_ffn",
    )(n2, gpre, go, act)


def fill(y, ys):
    rows = ys[0].shape[0]
    for k, part in enumerate(ys):
        y[k * rows : (k + 1) * rows] = part[...]


def grad_kv_kernel(batch, x, *refs):
    ys, (_, out, y) = refs[:batch], refs[batch:]
    fill(y, ys)
    out[...] = dot(x[...], y[...], TN).astype(BF16)


def grad_kv(x, ys, grads, col, width):
    every = x.shape[0]
    return pl.pallas_call(
        functools.partial(grad_kv_kernel, len(ys)),
        grid=(2,),
        in_specs=[whole(x.shape)]
        + [pl.BlockSpec((y.shape[0], width), lambda j: (0, j)) for y in ys]
        + [pl.BlockSpec(memory_space=pl.ANY)],
        out_specs=pl.BlockSpec((D, width), lambda j: (0, col + j)),
        scratch_shapes=[pltpu.VMEM((every, width), BF16)],
        out_shape=jax.ShapeDtypeStruct(grads.shape, BF16),
        input_output_aliases={1 + len(ys): 0},
        compiler_params=params(),
        cost_estimate=cost(8),
        name="grad_kv",
    )(x, *ys, grads)


def grad_rest_kernel(batch, at, normed, *refs):
    gq, gbr, att = (refs[k * batch : (k + 1) * batch] for k in range(3))
    steps, gtable, out, x, y = refs[3 * batch :]
    j = pl.program_id(0)
    tier = at[0]

    @pl.when(j == 0)
    def _():
        fill(x, [normed.at[k] for k in range(batch)])
        fill(y, gq)

    @pl.when(j == 1)
    def _():
        fill(x, gbr)
        fill(y, att)

    @pl.when(j < 2)
    def _():
        out[...] = dot(x[...], y[...], TN).astype(BF16)

    @pl.when(j == 2)
    def _():
        keys = gtable.shape[1]
        seg = steps.shape[0] - keys
        first = pl.multiple_of((1 - tier) * seg, seg)
        turned = dot(gtable[...].astype(BF16), steps[pl.ds(first, keys)], NN)
        out[...] = turned.astype(BF16).T


def grad_rest(at, normed, gq, gbr, att, steps, gtable, cols):
    seg, width = gq[0].shape
    batch, local, _ = normed.shape
    return pl.pallas_call(
        functools.partial(grad_rest_kernel, batch),
        grid_spec=pltpu.PrefetchScalarGridSpec(
            num_scalar_prefetch=1,
            grid=(3,),
            in_specs=[
                pl.BlockSpec((batch, seg, D), lambda j, s: (0, local // seg - 1, 0))
            ]
            + [whole((seg, width))] * batch
            + [whole((seg, D))] * batch
            + [whole((seg, width))] * batch
            + [whole(steps.shape), whole(gtable.shape)],
            out_specs=pl.BlockSpec((D, width), lambda j, s: (0, j)),
            scratch_shapes=[
                pltpu.VMEM((batch * seg, D), BF16),
                pltpu.VMEM((batch * seg, width), BF16),
            ],
        ),
        out_shape=jax.ShapeDtypeStruct((D, cols), BF16),
        compiler_params=params(),
        cost_estimate=cost(8),
        name="grad_rest",
    )(at, normed, *gq, *gbr, *att, steps, gtable)


def grad_conv_kernel(at, taps, fresh, _, out):
    out[...] = dot(taps[...], fresh[...], TN).astype(BF16)


def grad_conv(at, grouped, fresh, grads, col, wide):
    count = grouped.shape[0]
    return pl.pallas_call(
        grad_conv_kernel,
        grid_spec=pltpu.PrefetchScalarGridSpec(
            num_scalar_prefetch=1,
            grid=(KW,),
            in_specs=[
                pl.BlockSpec((count, D), lambda j, s: (0, j)),
                pl.BlockSpec((count, wide), lambda j, s: (0, s[1])),
                pl.BlockSpec(memory_space=pl.ANY),
            ],
            out_specs=pl.BlockSpec((D, wide), lambda j, s: (0, col + j)),
        ),
        out_shape=jax.ShapeDtypeStruct(grads.shape, BF16),
        input_output_aliases={3: 0},
        compiler_params=params(),
        cost_estimate=cost(4),
        name="grad_conv",
    )(at, grouped, fresh, grads)


def conv_kernel(taps, w, bias, out):
    k = pl.program_id(0)
    part = dot(taps[...], w[...], NN)

    @pl.when(k == 0)
    def _():
        out[...] = part + bias[...]

    @pl.when(k > 0)
    def _():
        out[...] += part


def compress(grouped, w, bias):
    count = grouped.shape[0]
    wide = bias.shape[0]
    return pl.pallas_call(
        conv_kernel,
        grid=(KW,),
        in_specs=[
            pl.BlockSpec((count, D), lambda j: (0, j)),
            pl.BlockSpec((D, wide), lambda j: (0, j)),
            whole((1, wide)),
        ],
        out_specs=whole((count, wide)),
        out_shape=jax.ShapeDtypeStruct((count, wide), F32),
        compiler_params=params(),
        cost_estimate=cost(3),
        name="compress",
    )(grouped, w, bias[None])


def distance_rows(first, count):
    half = D // 2
    freq = np.exp(np.arange(half) * (-2.0 * math.log(10000.0) / D))
    turned = (first - np.arange(count))[:, None] * freq[None, :]
    return np.concatenate([np.sin(turned), np.cos(turned)], axis=1).astype(
        ml_dtypes.bfloat16
    )


def col_sum(x):
    return jnp.sum(x, axis=tuple(range(x.ndim - 1)))


def ein(spec, a, b):
    return jnp.einsum(spec, a, b, preferred_element_type=F32)


def norm_rows(rows, gain, shift):
    return (standardize(rows.astype(F32))[0] * gain + shift).astype(BF16)


def shards(
    segment_input,
    memory,
    compressed,
    evicted,
    cotangent,
    seg_lengths,
    memory_fills,
    compressed_fills,
    conv_weight,
    conv_bias,
    norm1_gain,
    norm1_bias,
    query_weight,
    key_weight,
    value_weight,
    position_weight,
    content_bias,
    position_bias,
    out_weight,
    norm2_gain,
    norm2_bias,
    up_weight,
    up_bias,
    down_weight,
    down_bias,
):
    tier = lax.axis_index("tier")
    head = lax.axis_index("head")
    heads_n = lax.axis_size("head")
    batch, seg, _ = segment_input.shape
    mem = memory.shape[1]
    comp = compressed.shape[1]
    fresh = evicted.shape[1] // KW
    sizes = (comp, fresh, mem, seg)
    width = query_weight.shape[1]
    wide = conv_weight.shape[2]
    hidden = up_weight.shape[1]
    keys = 2 * (comp + fresh + mem + seg)
    streams = range(batch)
    at = jnp.concatenate(
        [
            jnp.stack([tier, head]).astype(jnp.int32),
            jnp.stack([compressed_fills, memory_fills, seg_lengths], 1).reshape(-1),
        ]
    )


    conv_z = gather_z(jnp.concatenate([conv_weight[k] for k in range(KW)], 1))
    out_t = head_gather(out_weight.T)
    full = out_t.shape[1]
    attn_pack = jnp.concatenate(
        [key_weight, value_weight, query_weight, position_weight], 1
    )
    ffn_pack = jnp.concatenate([out_t, up_weight, down_weight.T], 1)
    attn_z = gather_z(after(attn_pack, conv_z, out_t))
    ffn_w = lax.all_gather(
        after(ffn_pack, conv_z), ("dp", "tier"), axis=0, tiled=True
    )
    conv_blocks = gather_yt(conv_z)
    conv_blocks[0] = after(conv_blocks[0], out_t)
    conv_w = place(conv_blocks)

    n_comp = norm_rows(compressed, norm1_gain, norm1_bias)
    n_mem = norm_rows(memory, norm1_gain, norm1_bias)
    n_seg = norm_rows(segment_input, norm1_gain, norm1_bias)
    grouped = evicted.reshape(batch * fresh, KW * D)
    fresh_part = compress(grouped, conv_w, conv_bias).astype(BF16)
    fresh_rows = head_gather(fresh_part.reshape(batch, fresh, wide))
    n_fresh = norm_rows(fresh_rows, norm1_gain, norm1_bias)
    attn_blocks = gather_yt(attn_z)
    attn_blocks[0] = after(attn_blocks[0], fresh_part)
    attn_w = place(attn_blocks)

    normed, kv, q = project(n_comp, n_fresh, n_mem, n_seg, attn_w)
    kv_other = swap(kv, "tier")
    steps = jnp.asarray(distance_rows(keys - 1, keys + seg))
    table = position_table(at, steps, after(attn_w, kv), seg, keys, 3, width)
    atts, probs, others = [], [], []
    for b in streams:
        q_b = after(q, *(others[-2:-1] + atts[-1:])) if b else after(q, table)
        att, p = attend(
            b, at, q_b, kv, kv_other, table, content_bias, position_bias, sizes
        )
        atts.append(att)
        probs.append(p)
        if heads_n == 2:
            others.append(swap(att, "head"))
        else:
            others.append(lax.all_gather(att, "head", axis=1, tiled=True))

    def over_head(x):
        if heads_n == 2:
            return [x, swap(x, "head")]
        return [lax.psum(x, "head")]

    if heads_n == 2:
        pairs = [v for pair in zip(atts, others) for v in pair]
    else:
        pairs = others
    hid, n2, go, act, gpre, up_sums, out_sums, *halves = feed_forward(
        at,
        pairs,
        segment_input,
        cotangent,
        ffn_w,
        full,
        norm2_gain,
        norm2_bias,
        up_bias,
    )
    twos = [over_head(halves[0])]
    g_ffn = grad_ffn(n2, gpre, go, act)
    g_ffn_s = lax.psum_scatter(
        g_ffn, ("dp", "tier"), scatter_dimension=0, tiled=True
    ).astype(F32)

    ghids, gbrs, gqs, keeps, gots = [], [], [], [], []
    gkvs, parts, fparts, downs = [], [], [], []
    bias_sums, mem_sums, mid_rows = 0, 0, 0
    gtable = None
    last = g_ffn

    def rows_of(b, *others):
        gq = after(gqs[b], *others)
        gkv, part, fpart, sums = rows_back(
            b, keeps[b], gots[b], gq, n_mem, attn_w, sizes
        )
        gkvs.append(gkv)
        if b == batch - 1:
            fparts.append(over_head(fpart))
            parts.append(over_head(after(part, fparts[-1][-1])))
        else:
            parts.append(over_head(part))
            fparts.append(over_head(fpart))
        return sums[:2], part

    for b in streams:
        if b > 1:
            sums, last = rows_of(b - 2, last)
            mem_sums = mem_sums + sums
        if b < batch - 1:
            twos.append(over_head(after(halves[b + 1], twos[b][-1])))
        ghid, gbr, sums, gq, keep, send, gtable, gbias = attend_back(
            b,
            at,
            twos[b],
            hid,
            after(go, last),
            norm2_gain,
            ffn_w,
            probs[b],
            q,
            kv,
            kv_other,
            table,
            content_bias,
            position_bias,
            sizes,
            gtable,
        )
        last = gq
        ghids.append(ghid)
        gbrs.append(gbr)
        gqs.append(gq)
        keeps.append(keep)
        gots.append(swap(send, "tier"))
        if 0 < b:
            downs.append(over_head(after(halves[batch + b - 1], gq)))
        mid_rows = mid_rows + sums
        bias_sums = bias_sums + gbias
    cols = 5 * width + KW * wide
    gq_0 = after(gqs[0], last, parts[0][-1])
    grads = grad_rest(
        at, normed, [gq_0] + gqs[1:], gbrs, atts, steps, gtable, cols
    )
    last = grads
    for b in range(max(batch - 2, 0), batch):
        sums, last = rows_of(b, last)
        mem_sums = mem_sums + sums
    mem_sums = sum(over_head(mem_sums))
    grads = grad_kv(
        after(normed, mem_sums).reshape(-1, D), gkvs, grads, 3, width
    )
    fresh_grad, fresh_sums = fresh_back(
        fparts, after(fresh_rows, g_ffn_s), norm1_gain
    )
    grads = grad_conv(at, grouped, fresh_grad, grads, 5 * width // wide, wide)
    grads_s = lax.psum_scatter(
        grads, ("dp", "tier"), scatter_dimension=0, tiled=True
    ).astype(F32)
    g_q, g_out, g_pos, g_k, g_v = (
        grads_s[:, k * width : (k + 1) * width] for k in range(5)
    )
    g_conv = jnp.stack(
        [
            grads_s[:, 5 * width + k * wide : 5 * width + (k + 1) * wide]
            for k in range(KW)
        ]
    )
    downs.append(over_head(after(halves[-1], parts[-1][-1])))
    row_totals = fresh_sums[:2]
    gcomp = gin = None
    for b in streams:
        gcomp, gin, sums = context_back(
            b,
            parts[b],
            compressed,
            segment_input,
            after(ghids[b], grads if b == 0 else gin),
            norm1_gain,
            (gcomp, gin) if b else None,
            sizes,
        )
        row_totals = row_totals + sums[:2]
    grad_comp, grad_in = gcomp, gin

    outs = []
    for b in streams:
        out = hid[b * seg : (b + 1) * seg] + down_bias
        for x in downs[b]:
            out = out + x.astype(F32)
        outs.append(out.astype(BF16))
    output = jnp.stack(outs)
    mem_gain = (mem_sums[0] - norm1_bias * mem_sums[1]) / norm1_gain
    fresh_sum = lax.dynamic_slice_in_dim(fresh_sums[2], head * wide, wide, 0)
    sums = small_sum(
        [
            mid_rows[0],
            mid_rows[1],
            up_sums[0],
            out_sums[0],
            fresh_sum,
            row_totals[0] + mem_gain,
            row_totals[1] + mem_sums[1],
            bias_sums[:, 0],
            bias_sums[:, 1],
        ]
    )
    return (
        output,
        grad_in,
        grad_comp,
        g_conv,
        sums[4],
        sums[5],
        sums[6],
        g_q,
        g_k,
        g_v,
        g_pos,
        sums[7],
        sums[8],
        g_out.T,
        sums[0],
        sums[1],
        g_ffn_s[:, :hidden],
        sums[2],
        g_ffn_s[:, hidden:].T,
        sums[3],
    )


def solution(mesh):
    rows = P("dp", "tier", None)
    by_row = P(("dp", "tier"), "head")
    by_col = P("head", ("dp", "tier"))
    conv = P(None, ("dp", "tier"), "head")
    heads = P("head", None)
    placed = (
        (rows,) * 5
        + (P("dp"),) * 3
        + (conv, P("head"), P(), P())
        + (by_row,) * 4
        + (heads, heads, by_col, P(), P(), by_row, P("head"), by_col, P())
    )
    results = (
        (rows,) * 3
        + (conv, P("head"), P(), P())
        + (by_row,) * 4
        + (heads, heads, by_col, P(), P(), by_row, P("head"), by_col, P())
    )
    return jax.shard_map(
        shards, mesh=mesh, in_specs=placed, out_specs=results, check_vma=False
    )
```

time: 706 us -> 450 us (0.64)
  waiting for transfers between devices: 331 us -> 134 us
  Pallas kernels: 80 us -> 215 us
  matrix products: 90.6 us -> 0 us
  starting transfers between devices: 91.3 us -> 35.3 us
  local copies, waits for them, and re-layouts: 48.5 us -> 20.7 us
  other arithmetic: 52.4 us -> 25.4 us
  between operations: 2.61 us -> 15 us
    pallas_call x5 -> x23, Pallas kernels: 80 us -> 215 us  [the longest x3 52.8 us: attend_back(): pl.pallas_call(functools.partial(backward_kernel, sizes, len(twos), chain...]
    ppermute x69 -> x32, waiting for transfers between devices: 227 us -> 107 us  [swap(): return lax.ppermute(x, axis, [(i, i ^ step) for i in range(n)])]
    ppermute x33 -> x0, waiting for transfers between devices: 104 us -> none  [turn(): lax.ppermute(x, 'dp', [(i, (i // 2 + steps) % zn * 2 + i % 2) for i in ra...]
    dot_general x25 -> x0, matrix products: 90.6 us -> none  [ein(): return jnp.einsum(spec, a, b, preferred_element_type=F32)]
    ppermute x33 -> x0, starting transfers between devices: 49.6 us -> none  [turn(): lax.ppermute(x, 'dp', [(i, (i // 2 + steps) % zn * 2 + i % 2) for i in ra...]
    all_to_all x0 -> x2, waiting for transfers between devices: none -> 19.8 us  [z_exchange(): return lax.all_to_all(x, 'dp', 0, 0, axis_index_groups=groups, tiled=True)]
    ppermute x69 -> x32, starting transfers between devices: 41.7 us -> 25.7 us  [swap(): return lax.ppermute(x, axis, [(i, i ^ step) for i in range(n)])]
    unnamed x175 -> x116, local copies, waits for them, and re-layouts: 20 us -> 8.63 us
  transfers between devices with their start and end apart: 102 -> 37, of which waited for: 40 -> 13; matrix products, arithmetic and copies ran while one was open for 16% -> 7% of each run, Pallas kernels for 11% -> 41%
where the time goes in v2:
time: 450 us; the launch traced here: 445 us
  Pallas kernels  215 us (48%)
  waiting for transfers between devices  134 us (30%)
  starting transfers between devices  35.3 us (8%)
  other arithmetic  25.4 us (6%)
  local copies, waits for them, and re-layouts  20.7 us (5%)
  between operations  15 us (3%)
    ppermute x32, waiting for transfers between devices, swap(): return lax.ppermute(x, axis, [(i, i ^ step) for i in range(n)])  107 us
    pallas_call x3, Pallas kernels, attend_back(): pl.pallas_call(functools.partial(backward_kernel, sizes, len(twos), chain...  52.8 us
    pallas_call x3, Pallas kernels, attend(): pl.pallas_call(functools.partial(forward_kernel, b, sizes), grid_spec=plt...  26.9 us
    ppermute x32, starting transfers between devices, swap(): return lax.ppermute(x, axis, [(i, i ^ step) for i in range(n)])  25.7 us
    pallas_call x1, Pallas kernels, feed_forward(): pl.pallas_call(functools.partial(ffn_kernel, batch, len(atts) // batch, f...  24.8 us
    pallas_call x3, Pallas kernels, rows_back(): pl.pallas_call(functools.partial(rows_kernel, sizes), grid=(D // db,), in...  22.4 us
    all_to_all x2, waiting for transfers between devices, z_exchange(): return lax.all_to_all(x, 'dp', 0, 0, axis_index_groups=groups, tiled=True)  19.8 us
    pallas_call x3, Pallas kernels, context_back(): pl.pallas_call(functools.partial(context_kernel, sizes, len(grads), chain...  14.1 us
  transfers between devices with their start and end apart: 37, of which 13 were waited for; matrix products, arithmetic and copies ran while one was open for 7% of the time, Pallas kernels for 41%

profile of v2, /device:TPU:0, one launch (start us, length us, event | category | flops | bytes accessed | tf_op | source)
XLA Modules:
  0.0 444.9 jit_solution(9250775870802440070)
XLA Ops:
  12.1 5.0 %all-to-all-start = ((bf16[4,64,1536]{2,1,0:T(8,128)(2,1)}), bf16[4,64,1536]{2,1,0:T(8,128)(2,1)}, u32[]{:S(2)}, u32[]{:S(2)}) async-start(bf16[4,64,1536]{2,1,0:T(8,128)(2,1)} %broadcast_in_dim.18), calls=%async_computation | async-start | bytes 1572864 | tf_op jit(solution)/shard_map/all_to_all | solution.py:36
  21.8 15.2 %all-to-all-done.b0 = bf16[4,64,1536]{2,1,0:T(8,128)(2,1)} async-done(((bf16[4,64,1536]{2,1,0:T(8,128)(2,1)}), bf16[4,64,1536]{2,1,0:T(8,128)(2,1)}, u32[]{:S(2)}, u32[]{:S(2)}) %all-to-all-start) | async-done | bytes 786464 | tf_op jit(solution)/shard_map/all_to_all | solution.py:36
  47.9 13.4 %collective-permute-done.1.b1 = bf16[4,64,1536]{2,1,0:T(8,128)(2,1)} collective-permute-done((bf16[4,64,1536]{2,1,0:T(8,128)(2,1)}, bf16[4,64,1536]{2,1,0:T(8,128)(2,1)}, u32[]{:S(2)}, u32[]{:S(2)}) %collective-permute-start.1) | collective-permute-done | bytes 786464 | tf_op jit(solution)/shard_map/ppermute | solution.py:26
  63.0 4.6 %all-to-all-done.1.b0 = bf16[4,64,2048]{2,1,0:T(8,128)(2,1)} async-done(((bf16[4,64,2048]{2,1,0:T(8,128)(2,1)}), bf16[4,64,2048]{2,1,0:T(8,128)(2,1)}, u32[]{:S(2)}, u32[]{:S(2)}) %all-to-all-start.1) | async-done | bytes 1048608 | tf_op jit(solution)/shard_map/all_to_all | solution.py:36
  76.3 4.3 compress.1
  84.0 15.1 %collective-permute-done.5.b1 = bf16[4,64,2048]{2,1,0:T(8,128)(2,1)} collective-permute-done((bf16[4,64,2048]{2,1,0:T(8,128)(2,1)}, bf16[4,64,2048]{2,1,0:T(8,128)(2,1)}, u32[]{:S(2)}, u32[]{:S(2)}) %collective-permute-start.5) | collective-permute-done | bytes 1048608 | tf_op jit(solution)/shard_map/ppermute | solution.py:26
  102.9 6.1 %place.3 = bf16[4,2,2,64,2048]{4,3,2,1,0:T(8,128)(2,1)} custom-call(s32[2]{0:T(128)} %pad_add_fusion.2.at_ref, bf16[4,64,2048]{2,1,0:T(8,128)(2,1)} %all-to-all-done.1.b0, bf16[4,64,2048]{2,1,0:T(8,128)(2,1)} %collective-permute-done.5.b1, bf16[4,64,2048]{2,1,0:T(8,128)(2,1)} %copy-done.37, bf16[4,64,2048]{2,1,0:T(8,128)(2,1)} %copy-done.38), custom_call_target="tpu_custom_call" | custom-call | flops 3449999872 | bytes 1024 | tf_op jit(solution)/shard_map/place/pallas_call | solution.py:76
  109.0 10.1 %project.1 = (bf16[3,768,1024]{2,1,0:T(8,128)(2,1)}, bf16[3,768,1024]{2,1,0:T(8,128)(2,1)}, bf16[3,256,512]{2,1,0:T(8,128)(2,1)}) custom-call(bf16[3,192,1024]{2,1,0:T(8,128)(2,1)} %fusion.17.comp, bf16[3,64,1024]{2,1,0:T(8,128)(2,1)} %fusion.23.fresh, bf16[3,256,1024]{2,1,0:T(8,128)(2,1)} %get-tuple-element.245.mem.normed_mem, ...), custom_call_target="tpu_custom_call" | custom-call | flops 57500000256 | bytes 1024 | tf_op jit(solution)/shard_map/project/pallas_call | solution.py:181
  120.3 7.1 %position_table.1.table.refs_12_ = bf16[1536,512]{1,0:T(8,128)(2,1)} custom-call(s32[11]{0:T(128)} %pad_add_fusion.1.at, bf16[1792,1024]{1,0:T(8,128)(2,1)} %constant.54.clone.steps.refs_9_, bf16[1024,2048]{1,0:T(8,128)(2,1)} %bitcast.118), custom_call_target="tpu_custom_call" | custom-call | flops 23000000512 | bytes 1024 | tf_op jit(solution)/shard_map/position_table/pallas_call | solution.py:721
  127.5 8.9 %attend.3 = (bf16[256,512]{1,0:T(8,128)(2,1)}, bf16[4,256,1536]{2,1,0:T(8,128)(2,1)}) custom-call(s32[11]{0:T(128)} %pad_add_fusion.1.at, bf16[3,256,512]{2,1,0:T(8,128)(2,1)} %get-tuple-element.125.q.refs_7_, bf16[3,768,1024]{2,1,0:T(8,128)(2,1)} %get-tuple-element.119.k_own.v_own.refs_8_.refs_10_, ...), custom_call_target="tpu_custom_call" | custom-call | flops 23000000512 | bytes 1024 | tf_op jit(solution)/shard_map/attend/pallas_call | solution.py:241
  136.4 8.8 %attend.4 = (bf16[256,512]{1,0:T(8,128)(2,1)}, bf16[4,256,1536]{2,1,0:T(8,128)(2,1)}) custom-call(s32[11]{0:T(128)} %pad_add_fusion.1.at, bf16[3,256,512]{2,1,0:T(8,128)(2,1)} %get-tuple-element.125.q.refs_7_, bf16[3,768,1024]{2,1,0:T(8,128)(2,1)} %get-tuple-element.119.k_own.v_own.refs_8_.refs_10_, ...), custom_call_target="tpu_custom_call" | custom-call | flops 23000000512 | bytes 1024 | tf_op jit(solution)/shard_map/attend/pallas_call | solution.py:241
  147.3 9.2 %attend.5 = (bf16[256,512]{1,0:T(8,128)(2,1)}, bf16[4,256,1536]{2,1,0:T(8,128)(2,1)}) custom-call(s32[11]{0:T(128)} %pad_add_fusion.1.at, bf16[3,256,512]{2,1,0:T(8,128)(2,1)} %get-tuple-element.125.q.refs_7_, bf16[3,768,1024]{2,1,0:T(8,128)(2,1)} %get-tuple-element.119.k_own.v_own.refs_8_.refs_10_, ...), custom_call_target="tpu_custom_call" | custom-call | flops 23000000512 | bytes 1024 | tf_op jit(solution)/shard_map/attend/pallas_call | solution.py:241
  156.7 8.2 %collective-permute-done.11.refs_5_ = bf16[256,512]{1,0:T(8,128)(2,1)S(1)} collective-permute-done((bf16[256,512]{1,0:T(8,128)(2,1)}, bf16[256,512]{1,0:T(8,128)(2,1)S(1)}, u32[]{:S(2)}, u32[]{:S(2)}) %collective-permute-start.11) | collective-permute-done | bytes 262176 | tf_op jit(solution)/shard_map/ppermute | solution.py:26
  165.6 24.8 %feed_forward.1 = (f32[768,1024]{1,0:T(8,128)}, bf16[768,1024]{1,0:T(8,128)(2,1)}, bf16[768,1024]{1,0:T(8,128)(2,1)}, bf16[768,2048]{1,0:T(8,128)(2,1)}, bf16[76...) custom-call(s32[11]{0:T(128)} %pad_add_fusion.1.at, ...), custom_call_target="tpu_custom_call" | custom-call | flops 57500000256 | bytes 1024 | tf_op jit(solution)/shard_map/feed_forward/pallas_call | solution.py:394
  190.7 13.2 %grad_ffn.1 = bf16[1024,4096]{1,0:T(8,128)(2,1)} custom-call(bf16[768,1024]{1,0:T(8,128)(2,1)} %get-tuple-element.134.n2, bf16[768,2048]{1,0:T(8,128)(2,1)} %get-tuple-element.135.gpre, bf16[768,1024]{1,0:T(8,128)(2,1)} %get-tuple-element.152.go.refs_3_, bf16[768,2048]{1,0:T(8,128)(2,1)} %get-tuple-element.136.act), custom_call_target="tpu_custom_call" | custom-call | flops 34500001792 | bytes 1024 | tf_op jit(solution)/shard_map/grad_ffn/pallas_call | solution.py:761
  206.9 17.5 %attend_back.3 = (f32[256,1024]{1,0:T(8,128)}, bf16[256,1024]{1,0:T(8,128)(2,1)}, f32[8,1024]{1,0:T(8,128)}, bf16[256,512]{1,0:T(8,128)(2,1)}, bf16[2,768,512]{2...) custom-call(s32[11]{0:T(128)} %pad_add_fusion.1.at, ...), custom_call_target="tpu_custom_call" | custom-call | flops 57500000256 | bytes 1024 | tf_op jit(solution)/shard_map/attend_back/pallas_call | solution.py:521
  225.3 17.5 %attend_back.4 = (f32[256,1024]{1,0:T(8,128)}, bf16[256,1024]{1,0:T(8,128)(2,1)}, f32[8,1024]{1,0:T(8,128)}, bf16[256,512]{1,0:T(8,128)(2,1)}, bf16[2,768,512]{2...) custom-call(s32[11]{0:T(128)} %pad_add_fusion.1.at, ...), custom_call_target="tpu_custom_call" | custom-call | flops 57500000256 | bytes 1024 | tf_op jit(solution)/shard_map/attend_back/pallas_call | solution.py:521
  244.5 7.5 %rows_back.3 = (bf16[768,1024]{1,0:T(8,128)(2,1)}, bf16[448,1024]{1,0:T(8,128)(2,1)}, bf16[64,1024]{1,0:T(8,128)(2,1)}, f32[8,1024]{1,0:T(8,128)}) custom-call(bf16[2,768,512]{2,1,0:T(8,128)(2,1)} %get-tuple-element.148.keep, bf16[2,768,512]{2,1,0:T(8,128)(2,1)} %copy-done.36, bf16[256,512]{1,0:T(8,128)(2,1)} %get-tuple-element.163.gq.refs_0_, ...), custom_call_target="tpu_custom_call" | custom-call | flops 3449999872 | bytes 1024 | tf_op jit(solution)/shard_map/rows_back/pallas_call | solution.py:601
  253.1 17.8 %attend_back.5 = (f32[256,1024]{1,0:T(8,128)}, bf16[256,1024]{1,0:T(8,128)(2,1)}, f32[8,1024]{1,0:T(8,128)}, bf16[256,512]{1,0:T(8,128)(2,1)}, bf16[2,768,512]{2...) custom-call(s32[11]{0:T(128)} %pad_add_fusion.1.at, ...), custom_call_target="tpu_custom_call" | custom-call | flops 57500000256 | bytes 1024 | tf_op jit(solution)/shard_map/attend_back/pallas_call | solution.py:521
  274.5 10.4 %grad_rest.1.refs_3_ = bf16[1024,4096]{1,0:T(8,128)(2,1)} custom-call(s32[11]{0:T(128)} %pad_add_fusion.1.at, bf16[3,768,1024]{2,1,0:T(8,128)(2,1)} %get-tuple-element.185.normed, bf16[256,512]{1,0:T(8,128)(2,1)} %get-tuple-element.163.gq.refs_0_, bf16[256,512]{1,0:T(8,128)(2,1)} %get-tuple-element.168.refs_1_.gq, ...), custom_call_target="tpu_custom_call" | custom-call | flops 9200000000 | bytes 1024 | tf_op jit(solution)/shard_map/grad_rest/pallas_call | solution.py:835
  286.1 7.4 %rows_back.4 = (bf16[768,1024]{1,0:T(8,128)(2,1)}, bf16[448,1024]{1,0:T(8,128)(2,1)}, bf16[64,1024]{1,0:T(8,128)(2,1)}, f32[8,1024]{1,0:T(8,128)}) custom-call(bf16[2,768,512]{2,1,0:T(8,128)(2,1)} %get-tuple-element.160.keep, bf16[2,768,512]{2,1,0:T(8,128)(2,1)} %copy-done.34, bf16[256,512]{1,0:T(8,128)(2,1)} %get-tuple-element.168.refs_1_.gq, ...), custom_call_target="tpu_custom_call" | custom-call | flops 3449999872 | bytes 1024 | tf_op jit(solution)/shard_map/rows_back/pallas_call | solution.py:601
  294.6 7.6 %rows_back.5 = (bf16[768,1024]{1,0:T(8,128)(2,1)}, bf16[448,1024]{1,0:T(8,128)(2,1)}, bf16[64,1024]{1,0:T(8,128)(2,1)}, f32[8,1024]{1,0:T(8,128)}) custom-call(bf16[2,768,512]{2,1,0:T(8,128)(2,1)} %get-tuple-element.158.keep, bf16[2,768,512]{2,1,0:T(8,128)(2,1)} %copy-done.35, bf16[256,512]{1,0:T(8,128)(2,1)} %get-tuple-element.170.refs_2_.gq, ...), custom_call_target="tpu_custom_call" | custom-call | flops 3449999872 | bytes 1024 | tf_op jit(solution)/shard_map/rows_back/pallas_call | solution.py:601
  307.9 10.2 %grad_kv.1._ = bf16[1024,4096]{1,0:T(8,128)(2,1)} custom-call(bf16[2304,1024]{1,0:T(8,128)(2,1)} %bitcast.116, bf16[768,1024]{1,0:T(8,128)(2,1)} %get-tuple-element.186.refs_0_, bf16[768,1024]{1,0:T(8,128)(2,1)} %get-tuple-element.187.refs_1_, bf16[768,1024]{1,0:T(8,128)(2,1)} %get-tuple-element.188.refs_2_, ...), custom_call_target="tpu_custom_call", output_to_operand_aliasing={{}: (4, {})} | custom-call | flops 9200000000 | bytes 1024 | tf_op jit(solution)/shard_map/grad_kv/pallas_call | solution.py:787
  323.9 5.1 %grad_conv.1 = bf16[1024,4096]{1,0:T(8,128)(2,1)} custom-call(s32[11]{0:T(128)} %pad_add_fusion.1.at, bf16[192,3072]{1,0:T(8,128)(2,1)} %reshape.130.taps, bf16[192,1024]{1,0:T(8,128)(2,1)} %get-tuple-element.181.fresh, bf16[1024,4096]{1,0:T(8,128)(2,1)} %grad_kv.1._), custom_call_target="tpu_custom_call", output_to_operand_aliasing={{}: (3, {})} | custom-call | flops 4600000000 | bytes 1024 | tf_op jit(solution)/shard_map/grad_conv/pallas_call | solution.py:866
  335.1 41.5 %collective-permute-done.22.refs_1_ = bf16[448,1024]{1,0:T(8,128)(2,1)S(1)} collective-permute-done((bf16[448,1024]{1,0:T(8,128)(2,1)S(1)}, bf16[448,1024]{1,0:T(8,128)(2,1)S(1)}, u32[]{:S(2)}, u32[]{:S(2)}) %collective-permute-start.22) | collective-permute-done | bytes 917536 | tf_op jit(solution)/shard_map/ppermute | solution.py:26
  378.8 4.6 %context_back.3 = (f32[3,192,1024]{2,1,0:T(8,128)}, f32[3,256,1024]{2,1,0:T(8,128)}, f32[8,1024]{1,0:T(8,128)}) custom-call(bf16[448,1024]{1,0:T(8,128)(2,1)} %get-tuple-element.151.refs_0_, bf16[448,1024]{1,0:T(8,128)(2,1)} %copy-done.39, bf16[3,192,1024]{2,1,0:T(8,128)(2,1)} %refs_2_.5, bf16[3,256,1024]{2,1,0:T(8,128)(2,1)} %refs_3_.5, ...), custom_call_target="tpu_custom_call" | custom-call | flops 3449999872 | bytes 1024 | tf_op jit(solution)/shard_map/context_back/pallas_call | solution.py:663
  383.4 12.9 %collective-permute-done.24.refs_1_ = bf16[448,1024]{1,0:T(8,128)(2,1)} collective-permute-done((bf16[448,1024]{1,0:T(8,128)(2,1)S(1)}, bf16[448,1024]{1,0:T(8,128)(2,1)}, u32[]{:S(2)}, u32[]{:S(2)}) %collective-permute-start.24) | collective-permute-done | bytes 917536 | tf_op jit(solution)/shard_map/ppermute | solution.py:26
  396.3 4.7 %context_back.4 = (f32[3,192,1024]{2,1,0:T(8,128)}, f32[3,256,1024]{2,1,0:T(8,128)}, f32[8,1024]{1,0:T(8,128)}) custom-call(bf16[448,1024]{1,0:T(8,128)(2,1)} %get-tuple-element.169.refs_0_, bf16[448,1024]{1,0:T(8,128)(2,1)} %collective-permute-done.24.refs_1_, bf16[3,192,1024]{2,1,0:T(8,128)(2,1)} %refs_2_.5, ...), custom_call_target="tpu_custom_call", output_to_operand_aliasing={{0}: (6, {}), {1}: (7, {})} | custom-call | flops 3449999872 | bytes 1024 | tf_op jit(solution)/shard_map/context_back/pallas_call | solution.py:663
  401.1 4.8 %context_back.5 = (f32[3,192,1024]{2,1,0:T(8,128)}, f32[3,256,1024]{2,1,0:T(8,128)}, f32[8,1024]{1,0:T(8,128)}) custom-call(bf16[448,1024]{1,0:T(8,128)(2,1)} %get-tuple-element.173.refs_0_, bf16[448,1024]{1,0:T(8,128)(2,1)} %copy-done.42, bf16[3,192,1024]{2,1,0:T(8,128)(2,1)} %refs_2_.5, ...), custom_call_target="tpu_custom_call", output_to_operand_aliasing={{0}: (6, {}), {1}: (7, {})} | custom-call | flops 3449999872 | bytes 1024 | tf_op jit(solution)/shard_map/context_back/pallas_call | solution.py:663
  414.1 4.9 %collective-permute-done.30 = f32[72,128]{1,0:T(8,128)S(1)} collective-permute-done((f32[72,128]{1,0:T(8,128)S(1)}, f32[72,128]{1,0:T(8,128)S(1)}, u32[]{:S(2)}, u32[]{:S(2)}) %collective-permute-start.30) | collective-permute-done | bytes 36896 | tf_op jit(solution)/shard_map/ppermute | solution.py:26
  420.7 5.6 %collective-permute-done.31 = f32[72,128]{1,0:T(8,128)S(1)} collective-permute-done((f32[72,128]{1,0:T(8,128)S(1)}, f32[72,128]{1,0:T(8,128)S(1)}, u32[]{:S(2)}, u32[]{:S(2)}) %collective-permute-start.31) | collective-permute-done | bytes 36896 | tf_op jit(solution)/shard_map/ppermute | solution.py:26
  428.1 6.3 %reduce-scatter.5.cloned.1.call-done = bf16[64,4096]{1,0:T(8,128)(2,1)} async-done(((bf16[1024,4096]{1,0:T(8,128)(2,1)}), bf16[64,4096]{1,0:T(8,128)(2,1)}) %reduce-scatter.5.cloned.1.call-update) | async-done | bytes 524304 | tf_op jit(solution)/shard_map/reduce_scatter | solution.py:1127
  (251 shorter events, 89.4 us)
Async XLA Ops:
  7.2 13.8 %collective-permute-start = (bf16[64,512]{1,0:T(8,128)(2,1)}, bf16[64,512]{1,0:T(8,128)(2,1)}, u32[]{:S(2)}, u32[]{:S(2)}) collective-permute-start(bf16[64,512]{1,0:T(8,128)(2,1)} %bitcast.81), channel_id=1, source_target_pairs={{0,1},{1,0},{2,3},{3,2},{4,5},{5,4},{6,7},{7,6},{8,9},{9,8},{10,11... | collective-permute-start | bytes 196616 | tf_op jit(solution)/shard_map/ppermute | solution.py:26
  12.1 24.9 %all-to-all-start = ((bf16[4,64,1536]{2,1,0:T(8,128)(2,1)}), bf16[4,64,1536]{2,1,0:T(8,128)(2,1)}, u32[]{:S(2)}, u32[]{:S(2)}) async-start(bf16[4,64,1536]{2,1,0:T(8,128)(2,1)} %broadcast_in_dim.18), calls=%async_computation | async-start | bytes 1572864 | tf_op jit(solution)/shard_map/all_to_all | solution.py:36
  38.1 29.5 %all-to-all-start.1 = ((bf16[4,64,2048]{2,1,0:T(8,128)(2,1)}), bf16[4,64,2048]{2,1,0:T(8,128)(2,1)}, u32[]{:S(2)}, u32[]{:S(2)}) async-start(bf16[4,64,2048]{2,1,0:T(8,128)(2,1)} %broadcast_in_dim.20), calls=%async_computation.1 | async-start | bytes 2097152 | tf_op jit(solution)/shard_map/all_to_all | solution.py:36
  42.4 122.5 %all-gather.2.cloned.1.call-start = ((), (), s32[]{:S(2)}) async-start(), calls=%async_computation.4 | async-start | bytes 11141120 | tf_op jit(solution)/shard_map/all_gather | solution.py:995
  42.4 18.9 %collective-permute-start.1 = (bf16[4,64,1536]{2,1,0:T(8,128)(2,1)}, bf16[4,64,1536]{2,1,0:T(8,128)(2,1)}, u32[]{:S(2)}, u32[]{:S(2)}) collective-permute-start(bf16[4,64,1536]{2,1,0:T(8,128)(2,1)} %all-to-all-done.b0), channel_id=1, source_target_pairs={{0,4},{4,0},{8,12},{12,8},{16,20},{20,16},{24,28},{28,24},{1,5},{5... | collective-permute-start | bytes 2359304 | tf_op jit(solution)/shard_map/ppermute | solution.py:26
  47.9 23.3 %collective-permute-start.2 = (bf16[4,64,1536]{2,1,0:T(8,128)(2,1)}, bf16[4,64,1536]{2,1,0:T(8,128)(2,1)S(1)}, u32[]{:S(2)}, u32[]{:S(2)}) collective-permute-start(bf16[4,64,1536]{2,1,0:T(8,128)(2,1)} %all-to-all-done.b0), channel_id=1, source_target_pairs={{0,2},{2,0},{1,3},{3,1},{4,6},{6,4},{5,7},{7,5},{8,10},{10,8},{9,1... | collective-permute-start | bytes 2359304 | tf_op jit(solution)/shard_map/ppermute | solution.py:26
  61.3 9.9 %collective-permute-start.3 = (bf16[4,64,1536]{2,1,0:T(8,128)(2,1)}, bf16[4,64,1536]{2,1,0:T(8,128)(2,1)}, u32[]{:S(2)}, u32[]{:S(2)}) collective-permute-start(bf16[4,64,1536]{2,1,0:T(8,128)(2,1)} %collective-permute-done.1.b1), channel_id=1, source_target_pairs={{0,2},{2,0},{1,3},{3,1},{4,6},{6,4},{5,7},{7,5},{8,10},{10,8},{9,1... | collective-permute-start | bytes 2359304 | tf_op jit(solution)/shard_map/ppermute | solution.py:26
  62.2 256.0 %reduce-scatter.3.cloned.1.call-start = ((), (), s32[]{:S(2)}) async-start(), calls=%async_computation.5 | async-start | bytes 8912896 | tf_op jit(solution)/shard_map/reduce_scatter | solution.py:1052
  67.6 31.4 %collective-permute-start.5 = (bf16[4,64,2048]{2,1,0:T(8,128)(2,1)}, bf16[4,64,2048]{2,1,0:T(8,128)(2,1)}, u32[]{:S(2)}, u32[]{:S(2)}) collective-permute-start(bf16[4,64,2048]{2,1,0:T(8,128)(2,1)} %all-to-all-done.1.b0), channel_id=1, source_target_pairs={{0,4},{4,0},{8,12},{12,8},{16,20},{20,16},{24,28},{28,24},{1,5},{5... | collective-permute-start | bytes 3145736 | tf_op jit(solution)/shard_map/ppermute | solution.py:26
  81.7 17.4 %collective-permute-start.4 = (bf16[3,64,512]{2,1,0:T(8,128)(2,1)S(1)}, bf16[3,64,512]{2,1,0:T(8,128)(2,1)S(1)}, u32[]{:S(2)}, u32[]{:S(2)}) collective-permute-start(bf16[3,64,512]{2,1,0:T(8,128)(2,1)S(1)} %bitcast.74), channel_id=1, source_target_pairs={{0,1},{1,0},{2,3},{3,2},{4,5},{5,4},{6,7},{7,6},{8,9},{9,8},{10,11... | collective-permute-start | bytes 589832 | tf_op jit(solution)/shard_map/ppermute | solution.py:26
  84.0 16.8 %collective-permute-start.6 = (bf16[4,64,2048]{2,1,0:T(8,128)(2,1)}, bf16[4,64,2048]{2,1,0:T(8,128)(2,1)S(1)}, u32[]{:S(2)}, u32[]{:S(2)}) collective-permute-start(bf16[4,64,2048]{2,1,0:T(8,128)(2,1)} %all-to-all-done.1.b0), channel_id=1, source_target_pairs={{0,2},{2,0},{1,3},{3,1},{4,6},{6,4},{5,7},{7,5},{8,10},{10,8},{9,1... | collective-permute-start | bytes 3145736 | tf_op jit(solution)/shard_map/ppermute | solution.py:26
  119.2 8.3 %collective-permute-start.8 = (bf16[3,768,1024]{2,1,0:T(8,128)(2,1)}, bf16[3,768,1024]{2,1,0:T(8,128)(2,1)}, u32[]{:S(2)}, u32[]{:S(2)}) collective-permute-start(bf16[3,768,1024]{2,1,0:T(8,128)(2,1)} %get-tuple-element.119.k_own.v_own.refs_8_.refs_10_), channel_id=1, source_target_pairs={{0,2},{2,0},{1,3},{3,1},{4,6},{6,4},{5,7},{7,5},{8,10},{10,8},{9,1... | collective-permute-start | bytes 14155784 | tf_op jit(solution)/shard_map/ppermute | solution.py:26
  136.3 11.0 %collective-permute-start.9 = (bf16[256,512]{1,0:T(8,128)(2,1)}, bf16[256,512]{1,0:T(8,128)(2,1)S(1)}, u32[]{:S(2)}, u32[]{:S(2)}) collective-permute-start(bf16[256,512]{1,0:T(8,128)(2,1)} %get-tuple-element.122.refs_0_.refs_6_), channel_id=1, source_target_pairs={{0,1},{1,0},{2,3},{3,2},{4,5},{5,4},{6,7},{7,6},{8,9},{9,8},{10,11... | collective-permute-start | bytes 786440 | tf_op jit(solution)/shard_map/ppermute | solution.py:26
  145.2 11.5 %collective-permute-start.10 = (bf16[256,512]{1,0:T(8,128)(2,1)}, bf16[256,512]{1,0:T(8,128)(2,1)S(1)}, u32[]{:S(2)}, u32[]{:S(2)}) collective-permute-start(bf16[256,512]{1,0:T(8,128)(2,1)} %get-tuple-element.124.refs_2_.refs_7_), channel_id=1, source_target_pairs={{0,1},{1,0},{2,3},{3,2},{4,5},{5,4},{6,7},{7,6},{8,9},{9,8},{10,11... | collective-permute-start | bytes 786440 | tf_op jit(solution)/shard_map/ppermute | solution.py:26
  156.6 8.3 %collective-permute-start.11 = (bf16[256,512]{1,0:T(8,128)(2,1)}, bf16[256,512]{1,0:T(8,128)(2,1)S(1)}, u32[]{:S(2)}, u32[]{:S(2)}) collective-permute-start(bf16[256,512]{1,0:T(8,128)(2,1)} %get-tuple-element.126.refs_4_.refs_8_), channel_id=1, source_target_pairs={{0,1},{1,0},{2,3},{3,2},{4,5},{5,4},{6,7},{7,6},{8,9},{9,8},{10,11... | collective-permute-start | bytes 786440 | tf_op jit(solution)/shard_map/ppermute | solution.py:26
  190.4 13.7 %collective-permute-start.12 = (bf16[256,1024]{1,0:T(8,128)(2,1)}, bf16[256,1024]{1,0:T(8,128)(2,1)S(1)}, u32[]{:S(2)}, u32[]{:S(2)}) collective-permute-start(bf16[256,1024]{1,0:T(8,128)(2,1)} %get-tuple-element.131.refs_0_), channel_id=1, source_target_pairs={{0,1},{1,0},{2,3},{3,2},{4,5},{5,4},{6,7},{7,6},{8,9},{9,8},{10,11... | collective-permute-start | bytes 1572872 | tf_op jit(solution)/shard_map/ppermute | solution.py:26
  204.0 230.5 %reduce-scatter.5.cloned.1.call-start = ((), (), s32[]{:S(2)}) async-start(), calls=%async_computation.6 | async-start | bytes 8912896 | tf_op jit(solution)/shard_map/reduce_scatter | solution.py:1127
  205.1 19.3 %collective-permute-start.13 = (bf16[256,1024]{1,0:T(8,128)(2,1)S(1)}, bf16[256,1024]{1,0:T(8,128)(2,1)S(1)}, u32[]{:S(2)}, u32[]{:S(2)}) collective-permute-start(bf16[256,1024]{1,0:T(8,128)(2,1)S(1)} %copy-done.44), channel_id=1, source_target_pairs={{0,1},{1,0},{2,3},{3,2},{4,5},{5,4},{6,7},{7,6},{8,9},{9,8},{10,11... | collective-permute-start | bytes 1572872 | tf_op jit(solution)/shard_map/ppermute | solution.py:26
  224.4 19.0 %collective-permute-start.16 = (bf16[2,768,512]{2,1,0:T(8,128)(2,1)}, bf16[2,768,512]{2,1,0:T(8,128)(2,1)S(1)}, u32[]{:S(2)}, u32[]{:S(2)}) collective-permute-start(bf16[2,768,512]{2,1,0:T(8,128)(2,1)} %get-tuple-element.149), channel_id=1, source_target_pairs={{0,2},{2,0},{1,3},{3,1},{4,6},{6,4},{5,7},{7,5},{8,10},{10,8},{9,1... | collective-permute-start | bytes 4718600 | tf_op jit(solution)/shard_map/ppermute | solution.py:26
  224.5 28.6 %collective-permute-start.15 = (bf16[256,1024]{1,0:T(8,128)(2,1)}, bf16[256,1024]{1,0:T(8,128)(2,1)}, u32[]{:S(2)}, u32[]{:S(2)}) collective-permute-start(bf16[256,1024]{1,0:T(8,128)(2,1)} %get-tuple-element.147.refs_0_), channel_id=1, source_target_pairs={{0,1},{1,0},{2,3},{3,2},{4,5},{5,4},{6,7},{7,6},{8,9},{9,8},{10,11... | collective-permute-start | bytes 1572872 | tf_op jit(solution)/shard_map/ppermute | solution.py:26
  242.8 42.1 %collective-permute-start.19 = (bf16[2,768,512]{2,1,0:T(8,128)(2,1)}, bf16[2,768,512]{2,1,0:T(8,128)(2,1)S(1)}, u32[]{:S(2)}, u32[]{:S(2)}) collective-permute-start(bf16[2,768,512]{2,1,0:T(8,128)(2,1)} %get-tuple-element.161), channel_id=1, source_target_pairs={{0,2},{2,0},{1,3},{3,1},{4,6},{6,4},{5,7},{7,5},{8,10},{10,8},{9,1... | collective-permute-start | bytes 4718600 | tf_op jit(solution)/shard_map/ppermute | solution.py:26
  252.0 22.5 %collective-permute-start.20 = (bf16[448,1024]{1,0:T(8,128)(2,1)}, bf16[448,1024]{1,0:T(8,128)(2,1)S(1)}, u32[]{:S(2)}, u32[]{:S(2)}) collective-permute-start(bf16[448,1024]{1,0:T(8,128)(2,1)} %get-tuple-element.151.refs_0_), channel_id=1, source_target_pairs={{0,1},{1,0},{2,3},{3,2},{4,5},{5,4},{6,7},{7,6},{8,9},{9,8},{10,11... | collective-permute-start | bytes 2752520 | tf_op jit(solution)/shard_map/ppermute | solution.py:26
  270.9 22.6 %collective-permute-start.18 = (bf16[2,768,512]{2,1,0:T(8,128)(2,1)}, bf16[2,768,512]{2,1,0:T(8,128)(2,1)S(1)}, u32[]{:S(2)}, u32[]{:S(2)}) collective-permute-start(bf16[2,768,512]{2,1,0:T(8,128)(2,1)} %get-tuple-element.159), channel_id=1, source_target_pairs={{0,2},{2,0},{1,3},{3,1},{4,6},{6,4},{5,7},{7,5},{8,10},{10,8},{9,1... | collective-permute-start | bytes 4718600 | tf_op jit(solution)/shard_map/ppermute | solution.py:26
  305.3 15.0 %collective-permute-start.25 = (bf16[64,1024]{1,0:T(8,128)(2,1)S(1)}, bf16[64,1024]{1,0:T(8,128)(2,1)S(1)}, u32[]{:S(2)}, u32[]{:S(2)}) collective-permute-start(bf16[64,1024]{1,0:T(8,128)(2,1)S(1)} %copy-done.50), channel_id=1, source_target_pairs={{0,1},{1,0},{2,3},{3,2},{4,5},{5,4},{6,7},{7,6},{8,9},{9,8},{10,11... | collective-permute-start | bytes 393224 | tf_op jit(solution)/shard_map/ppermute | solution.py:26
  305.9 14.4 %collective-permute-start.26 = (bf16[64,1024]{1,0:T(8,128)(2,1)S(1)}, bf16[64,1024]{1,0:T(8,128)(2,1)S(1)}, u32[]{:S(2)}, u32[]{:S(2)}) collective-permute-start(bf16[64,1024]{1,0:T(8,128)(2,1)S(1)} %copy-done.51), channel_id=1, source_target_pairs={{0,1},{1,0},{2,3},{3,2},{4,5},{5,4},{6,7},{7,6},{8,9},{9,8},{10,11... | collective-permute-start | bytes 393224 | tf_op jit(solution)/shard_map/ppermute | solution.py:26
  307.4 13.0 %collective-permute-start.21 = (bf16[64,1024]{1,0:T(8,128)(2,1)}, bf16[64,1024]{1,0:T(8,128)(2,1)S(1)}, u32[]{:S(2)}, u32[]{:S(2)}) collective-permute-start(bf16[64,1024]{1,0:T(8,128)(2,1)} %get-tuple-element.172.refs_4_), channel_id=1, source_target_pairs={{0,1},{1,0},{2,3},{3,2},{4,5},{5,4},{6,7},{7,6},{8,9},{9,8},{10,11... | collective-permute-start | bytes 393224 | tf_op jit(solution)/shard_map/ppermute | solution.py:26
  330.8 79.3 %collective-permute-start.14 = (bf16[256,1024]{1,0:T(8,128)(2,1)S(1)}, bf16[256,1024]{1,0:T(8,128)(2,1)}, u32[]{:S(2)}, u32[]{:S(2)}) collective-permute-start(bf16[256,1024]{1,0:T(8,128)(2,1)S(1)} %copy-done.13), channel_id=1, source_target_pairs={{0,1},{1,0},{2,3},{3,2},{4,5},{5,4},{6,7},{7,6},{8,9},{9,8},{10,11... | collective-permute-start | bytes 1572872 | tf_op jit(solution)/shard_map/ppermute | solution.py:26
  332.3 77.8 %collective-permute-start.17 = (bf16[256,1024]{1,0:T(8,128)(2,1)}, bf16[256,1024]{1,0:T(8,128)(2,1)}, u32[]{:S(2)}, u32[]{:S(2)}) collective-permute-start(bf16[256,1024]{1,0:T(8,128)(2,1)} %get-tuple-element.156), channel_id=1, source_target_pairs={{0,1},{1,0},{2,3},{3,2},{4,5},{5,4},{6,7},{7,6},{8,9},{9,8},{10,11... | collective-permute-start | bytes 1572872 | tf_op jit(solution)/shard_map/ppermute | solution.py:26
  332.9 43.7 %collective-permute-start.22 = (bf16[448,1024]{1,0:T(8,128)(2,1)S(1)}, bf16[448,1024]{1,0:T(8,128)(2,1)S(1)}, u32[]{:S(2)}, u32[]{:S(2)}) collective-permute-start(bf16[448,1024]{1,0:T(8,128)(2,1)S(1)} %copy-done.40), channel_id=1, source_target_pairs={{0,1},{1,0},{2,3},{3,2},{4,5},{5,4},{6,7},{7,6},{8,9},{9,8},{10,11... | collective-permute-start | bytes 2752520 | tf_op jit(solution)/shard_map/ppermute | solution.py:26
  334.4 61.9 %collective-permute-start.24 = (bf16[448,1024]{1,0:T(8,128)(2,1)S(1)}, bf16[448,1024]{1,0:T(8,128)(2,1)}, u32[]{:S(2)}, u32[]{:S(2)}) collective-permute-start(bf16[448,1024]{1,0:T(8,128)(2,1)S(1)} %copy-done.41), channel_id=1, source_target_pairs={{0,1},{1,0},{2,3},{3,2},{4,5},{5,4},{6,7},{7,6},{8,9},{9,8},{10,11... | collective-permute-start | bytes 2752520 | tf_op jit(solution)/shard_map/ppermute | solution.py:26
  376.6 33.5 %collective-permute-start.23 = (bf16[256,1024]{1,0:T(8,128)(2,1)}, bf16[256,1024]{1,0:T(8,128)(2,1)}, u32[]{:S(2)}, u32[]{:S(2)}) collective-permute-start(bf16[256,1024]{1,0:T(8,128)(2,1)} %get-tuple-element.174), channel_id=1, source_target_pairs={{0,1},{1,0},{2,3},{3,2},{4,5},{5,4},{6,7},{7,6},{8,9},{9,8},{10,11... | collective-permute-start | bytes 1572872 | tf_op jit(solution)/shard_map/ppermute | solution.py:26
  419.0 7.3 %collective-permute-start.31 = (f32[72,128]{1,0:T(8,128)S(1)}, f32[72,128]{1,0:T(8,128)S(1)}, u32[]{:S(2)}, u32[]{:S(2)}) collective-permute-start(f32[72,128]{1,0:T(8,128)S(1)} %add.207), channel_id=1, source_target_pairs={{0,16},{4,20},{8,24},{12,28},{16,0},{20,4},{24,8},{28,12},{1,17},{... | collective-permute-start | bytes 110600 | tf_op jit(solution)/shard_map/ppermute | solution.py:26
  (60 other events, 371.5 us)
Sparse Core Ops, SparseCore 0:
  62.4 91.6 all-gather.1
  204.1 105.2 reduce-scatter.2
  329.2 105.2 reduce-scatter.4

commit v3 on v2

--- a/solution.py
+++ b/solution.py
@@ -88,6 +88,23 @@
         name="place",
     )(at.astype(jnp.int32), *blocks)
     return out.reshape(zn * 4 * rows, cols)
+
+
+def add_low(a, b):
+    return (a.astype(F32) + b.astype(F32)).astype(BF16)
+
+
+def halve(keep, got):
+    zn = lax.axis_size("dp") // 2
+    y = lax.axis_index("dp") % 2
+    shape = (zn, 2, keep.shape[0] // (2 * zn), keep.shape[1])
+    keep, got = keep.reshape(shape), got.reshape(shape)
+
+    def pick(k):
+        a, b = (lax.dynamic_index_in_dim(v, k, 1, keepdims=False) for v in (keep, got))
+        return add_low(a, b)
+
+    return pick(y), pick(1 - y)
 
 
 def small_sum(parts):
@@ -466,8 +483,8 @@
                 keep[which, row : row + size] = gk[pl.ds(mine, size)]
                 send[which, row : row + size] = gk[pl.ds(theirs, size)]
 
-        hand_out(0, dot(ds, content_q, TN) * scale)
-        hand_out(1, dot(p_low, ga, TN))
+        hand_out(0, (dot(content_q, ds, TN) * scale).T)
+        hand_out(1, dot(ga, p_low, TN).T)
         g_content = dot(ds, kf[...], NN) * scale
         r = lax.broadcasted_iota(jnp.int32, (rows, rows), 0)
         c = lax.broadcasted_iota(jnp.int32, (rows, rows), 1)
@@ -713,27 +730,39 @@
     )(*flat, raw, gain[None])
 
 
-def table_kernel(at, steps, w, out):
-    out[...] = dot(steps[...], w[...], NN).astype(BF16)
-
-
-def position_table(at, steps, w, seg, keys, col, width):
+def table_kernel(keys, at, steps, w, out):
+    seg = steps.shape[0] - keys
+    first = pl.multiple_of((1 - at[0]) * seg, seg)
+    out[...] = dot(steps[pl.ds(first, keys)], w[...], NN).astype(BF16)
+
+
+def position_table(at, steps, w, keys, col, width):
+    count = max(1, width // 256)
+    cb = width // count
     return pl.pallas_call(
-        table_kernel,
+        functools.partial(table_kernel, keys),
         grid_spec=pltpu.PrefetchScalarGridSpec(
             num_scalar_prefetch=1,
-            grid=(keys // seg,),
+            grid=(count,),
             in_specs=[
-                pl.BlockSpec((seg, D), lambda i, s: (1 - s[0] + i, 0)),
-                pl.BlockSpec((D, width), lambda i, s: (0, col)),
+                whole(steps.shape),
+                pl.BlockSpec((D, cb), lambda i, s: (0, col * count + i)),
             ],
-            out_specs=pl.BlockSpec((seg, width), lambda i, s: (i, 0)),
+            out_specs=pl.BlockSpec((keys, cb), lambda i, s: (0, i)),
         ),
         out_shape=jax.ShapeDtypeStruct((keys, width), BF16),
         compiler_params=params(),
         cost_estimate=cost(20),
         name="position_table",
     )(at, steps, w)
+
+
+def split_out(acc, tier, rows, keep, send):
+    v = acc.reshape(-1, 2, rows, acc.shape[1])
+    first = tier == 0
+    shape = keep.shape
+    keep[...] = jnp.where(first, v[:, 0], v[:, 1]).reshape(shape).astype(BF16)
+    send[...] = jnp.where(first, v[:, 1], v[:, 0]).reshape(shape).astype(BF16)
 
 
 def grad_ffn_kernel(steps, n2, gpre, go, act, out):
@@ -857,30 +886,28 @@
     )(at, normed, *gq, *gbr, *att, steps, gtable)
 
 
-def grad_conv_kernel(at, taps, fresh, _, out):
-    out[...] = dot(taps[...], fresh[...], TN).astype(BF16)
-
-
-def grad_conv(at, grouped, fresh, grads, col, wide):
+def grad_conv_kernel(rows, at, taps, fresh, keep, send):
+    split_out(dot(taps[...], fresh[...], TN), at[0], rows, keep, send)
+
+
+def grad_conv(at, grouped, fresh, wide, rows):
     count = grouped.shape[0]
     return pl.pallas_call(
-        grad_conv_kernel,
+        functools.partial(grad_conv_kernel, rows),
         grid_spec=pltpu.PrefetchScalarGridSpec(
             num_scalar_prefetch=1,
             grid=(KW,),
             in_specs=[
                 pl.BlockSpec((count, D), lambda j, s: (0, j)),
                 pl.BlockSpec((count, wide), lambda j, s: (0, s[1])),
-                pl.BlockSpec(memory_space=pl.ANY),
             ],
-            out_specs=pl.BlockSpec((D, wide), lambda j, s: (0, col + j)),
+            out_specs=[pl.BlockSpec((D // 2, wide), lambda j, s: (0, j))] * 2,
         ),
-        out_shape=jax.ShapeDtypeStruct(grads.shape, BF16),
-        input_output_aliases={3: 0},
+        out_shape=[jax.ShapeDtypeStruct((D // 2, KW * wide), BF16)] * 2,
         compiler_params=params(),
         cost_estimate=cost(4),
         name="grad_conv",
-    )(at, grouped, fresh, grads)
+    )(at, grouped, fresh)
 
 
 def conv_kernel(taps, w, bias, out):
@@ -975,6 +1002,7 @@
     wide = conv_weight.shape[2]
     hidden = up_weight.shape[1]
     keys = 2 * (comp + fresh + mem + seg)
+    rows = query_weight.shape[0]
     streams = range(batch)
     at = jnp.concatenate(
         [
@@ -1013,7 +1041,7 @@
     normed, kv, q = project(n_comp, n_fresh, n_mem, n_seg, attn_w)
     kv_other = swap(kv, "tier")
     steps = jnp.asarray(distance_rows(keys - 1, keys + seg))
-    table = position_table(at, steps, after(attn_w, kv), seg, keys, 3, width)
+    table = position_table(at, steps, after(attn_w, kv), keys, 3, width)
     atts, probs, others = [], [], []
     for b in streams:
         q_b = after(q, *(others[-2:-1] + atts[-1:])) if b else after(q, table)
@@ -1051,7 +1079,7 @@
     g_ffn = grad_ffn(n2, gpre, go, act)
     g_ffn_s = lax.psum_scatter(
         g_ffn, ("dp", "tier"), scatter_dimension=0, tiled=True
-    ).astype(F32)
+    )
 
     ghids, gbrs, gqs, keeps, gots = [], [], [], [], []
     gkvs, parts, fparts, downs = [], [], [], []
@@ -1065,12 +1093,8 @@
             b, keeps[b], gots[b], gq, n_mem, attn_w, sizes
         )
         gkvs.append(gkv)
-        if b == batch - 1:
-            fparts.append(over_head(fpart))
-            parts.append(over_head(after(part, fparts[-1][-1])))
-        else:
-            parts.append(over_head(part))
-            fparts.append(over_head(fpart))
+        fparts.append(over_head(fpart))
+        parts.append(over_head(part) if b == 0 else part)
         return sums[:2], part
 
     for b in streams:
@@ -1107,51 +1131,60 @@
             downs.append(over_head(after(halves[batch + b - 1], gq)))
         mid_rows = mid_rows + sums
         bias_sums = bias_sums + gbias
-    cols = 5 * width + KW * wide
-    gq_0 = after(gqs[0], last, parts[0][-1])
-    grads = grad_rest(
-        at, normed, [gq_0] + gqs[1:], gbrs, atts, steps, gtable, cols
-    )
-    last = grads
     for b in range(max(batch - 2, 0), batch):
         sums, last = rows_of(b, last)
         mem_sums = mem_sums + sums
-    mem_sums = sum(over_head(mem_sums))
-    grads = grad_kv(
-        after(normed, mem_sums).reshape(-1, D), gkvs, grads, 3, width
-    )
+    early = [pair[-1] for pair in fparts[:-1]]
+    gq_0 = after(gqs[0], last, parts[0][-1], *early)
+    grads = grad_rest(
+        at, normed, [gq_0] + gqs[1:], gbrs, atts, steps, gtable, 5 * width
+    )
+    for b in range(1, batch):
+        parts[b] = over_head(after(parts[b], fparts[-1][-1]))
     fresh_grad, fresh_sums = fresh_back(
-        fparts, after(fresh_rows, g_ffn_s), norm1_gain
-    )
-    grads = grad_conv(at, grouped, fresh_grad, grads, 5 * width // wide, wide)
+        fparts, after(fresh_rows, grads), norm1_gain
+    )
+    keep, send = grad_conv(at, grouped, fresh_grad, wide, rows)
+    grads = grad_kv(after(normed, keep, g_ffn_s).reshape(-1, D), gkvs, grads, 3, width)
     grads_s = lax.psum_scatter(
         grads, ("dp", "tier"), scatter_dimension=0, tiled=True
-    ).astype(F32)
-    g_q, g_out, g_pos, g_k, g_v = (
-        grads_s[:, k * width : (k + 1) * width] for k in range(5)
-    )
-    g_conv = jnp.stack(
-        [
-            grads_s[:, 5 * width + k * wide : 5 * width + (k + 1) * wide]
-            for k in range(KW)
-        ]
-    )
-    downs.append(over_head(after(halves[-1], parts[-1][-1])))
+    )
+    got = swap(send, "tier")
     row_totals = fresh_sums[:2]
-    gcomp = gin = None
-    for b in streams:
-        gcomp, gin, sums = context_back(
+    before = None
+
+    def context_of(b, *others):
+        return context_back(
             b,
             parts[b],
             compressed,
             segment_input,
-            after(ghids[b], grads if b == 0 else gin),
+            after(ghids[b], *others),
             norm1_gain,
-            (gcomp, gin) if b else None,
+            before,
             sizes,
         )
+
+    mine, theirs = halve(keep, after(got, grads))
+    other = swap(theirs, "dp")
+    *before, sums = context_of(0, theirs)
+    row_totals = row_totals + sums[:2]
+    added = add_low(mine, other)
+    conv_all = z_exchange(added)
+    for b in range(1, batch):
+        *before, sums = context_of(
+            b, before[1], conv_all if b == batch - 1 else added
+        )
         row_totals = row_totals + sums[:2]
-    grad_comp, grad_in = gcomp, gin
+    grad_comp, grad_in = before
+    g_conv = jnp.sum(after(conv_all, grad_in).astype(F32), axis=0)
+    g_conv = jnp.stack([g_conv[:, k * wide : (k + 1) * wide] for k in range(KW)])
+    mem_sums = sum(over_head(after(mem_sums, grad_in)))
+    downs.append(over_head(after(halves[-1], grad_in)))
+    grads_s = after(grads_s, conv_all)
+    g_q, g_out, g_pos, g_k, g_v = (
+        grads_s[:, k * width : (k + 1) * width].astype(F32) for k in range(5)
+    )
 
     outs = []
     for b in streams:
@@ -1192,9 +1225,9 @@
         g_out.T,
         sums[0],
         sums[1],
-        g_ffn_s[:, :hidden],
+        g_ffn_s[:, :hidden].astype(F32),
         sums[2],
-        g_ffn_s[:, hidden:].T,
+        g_ffn_s[:, hidden:].T.astype(F32),
         sums[3],
     )
 

time: 450 us -> 439 us (0.976)
  waiting for transfers between devices: 134 us -> 123 us
  starting transfers between devices: 35.3 us -> 40.9 us
  Pallas kernels: 215 us -> 210 us
    ppermute x32 -> x34, waiting for transfers between devices: 107 us -> 87.7 us  [swap(): return lax.ppermute(x, axis, [(i, i ^ step) for i in range(n)])]
    all_to_all x2 -> x3, waiting for transfers between devices: 19.8 us -> 35.4 us  [z_exchange(): return lax.all_to_all(x, 'dp', 0, 0, axis_index_groups=groups, tiled=True)]
    reduce_scatter x1, waiting for transfers between devices: 6.34 us -> 0.01 us  [shards(): lax.psum_scatter(grads, ('dp', 'tier'), scatter_dimension=0, tiled=True)]
    all_to_all x2 -> x3, starting transfers between devices: 9.24 us -> 13 us  [z_exchange(): return lax.all_to_all(x, 'dp', 0, 0, axis_index_groups=groups, tiled=True)]
    ppermute x32 -> x34, starting transfers between devices: 25.7 us -> 27.5 us  [swap(): return lax.ppermute(x, axis, [(i, i ^ step) for i in range(n)])]
    unnamed x116 -> x112, local copies, waits for them, and re-layouts: 8.63 us -> 9.49 us
  transfers between devices with their start and end apart: 37 -> 40, of which waited for: 13 -> 18; matrix products, arithmetic and copies ran while one was open for 7% -> 7% of each run, Pallas kernels for 41% -> 43%
where the time goes in v3:
time: 439 us; the launch traced here: 434 us
  Pallas kernels  210 us (48%)
  waiting for transfers between devices  123 us (28%)
  starting transfers between devices  40.9 us (9%)
  other arithmetic  26.1 us (6%)
  local copies, waits for them, and re-layouts  18.4 us (4%)
  between operations  15 us (3%)
    ppermute x34, waiting for transfers between devices, swap(): return lax.ppermute(x, axis, [(i, i ^ step) for i in range(n)])  87.7 us
    pallas_call x3, Pallas kernels, attend_back(): pl.pallas_call(functools.partial(backward_kernel, sizes, len(twos), chain...  50 us
    all_to_all x3, waiting for transfers between devices, z_exchange(): return lax.all_to_all(x, 'dp', 0, 0, axis_index_groups=groups, tiled=True)  35.4 us
    ppermute x34, starting transfers between devices, swap(): return lax.ppermute(x, axis, [(i, i ^ step) for i in range(n)])  27.5 us
    pallas_call x3, Pallas kernels, attend(): pl.pallas_call(functools.partial(forward_kernel, b, sizes), grid_spec=plt...  27 us
    pallas_call x1, Pallas kernels, feed_forward(): pl.pallas_call(functools.partial(ffn_kernel, batch, len(atts) // batch, f...  24.8 us
    pallas_call x3, Pallas kernels, rows_back(): pl.pallas_call(functools.partial(rows_kernel, sizes), grid=(D // db,), in...  22.7 us
    pallas_call x3, Pallas kernels, context_back(): pl.pallas_call(functools.partial(context_kernel, sizes, len(grads), chain...  13.9 us
  transfers between devices with their start and end apart: 40, of which 18 were waited for; matrix products, arithmetic and copies ran while one was open for 7% of the time, Pallas kernels for 43%

profile of v3, /device:TPU:0, one launch (start us, length us, event | category | flops | bytes accessed | tf_op | source)
XLA Modules:
  0.0 433.8 jit_solution(862413687073329492)
XLA Ops:
  12.1 5.0 %all-to-all-start = ((bf16[4,64,1536]{2,1,0:T(8,128)(2,1)}), bf16[4,64,1536]{2,1,0:T(8,128)(2,1)}, u32[]{:S(2)}, u32[]{:S(2)}) async-start(bf16[4,64,1536]{2,1,0:T(8,128)(2,1)} %broadcast_in_dim.18), calls=%async_computation | async-start | bytes 1572864 | tf_op jit(solution)/shard_map/all_to_all | solution.py:36
  21.8 15.2 %all-to-all-done.b0 = bf16[4,64,1536]{2,1,0:T(8,128)(2,1)} async-done(((bf16[4,64,1536]{2,1,0:T(8,128)(2,1)}), bf16[4,64,1536]{2,1,0:T(8,128)(2,1)}, u32[]{:S(2)}, u32[]{:S(2)}) %all-to-all-start) | async-done | bytes 786464 | tf_op jit(solution)/shard_map/all_to_all | solution.py:36
  47.9 13.4 %collective-permute-done.1.b1 = bf16[4,64,1536]{2,1,0:T(8,128)(2,1)} collective-permute-done((bf16[4,64,1536]{2,1,0:T(8,128)(2,1)}, bf16[4,64,1536]{2,1,0:T(8,128)(2,1)}, u32[]{:S(2)}, u32[]{:S(2)}) %collective-permute-start.1) | collective-permute-done | bytes 786464 | tf_op jit(solution)/shard_map/ppermute | solution.py:26
  63.0 4.6 %all-to-all-done.1.b0 = bf16[4,64,2048]{2,1,0:T(8,128)(2,1)} async-done(((bf16[4,64,2048]{2,1,0:T(8,128)(2,1)}), bf16[4,64,2048]{2,1,0:T(8,128)(2,1)}, u32[]{:S(2)}, u32[]{:S(2)}) %all-to-all-start.1) | async-done | bytes 1048608 | tf_op jit(solution)/shard_map/all_to_all | solution.py:36
  76.3 4.3 compress.1
  84.0 15.1 %collective-permute-done.5.b1 = bf16[4,64,2048]{2,1,0:T(8,128)(2,1)} collective-permute-done((bf16[4,64,2048]{2,1,0:T(8,128)(2,1)}, bf16[4,64,2048]{2,1,0:T(8,128)(2,1)}, u32[]{:S(2)}, u32[]{:S(2)}) %collective-permute-start.5) | collective-permute-done | bytes 1048608 | tf_op jit(solution)/shard_map/ppermute | solution.py:26
  102.9 6.1 %place.3 = bf16[4,2,2,64,2048]{4,3,2,1,0:T(8,128)(2,1)} custom-call(s32[2]{0:T(128)} %pad_add_fusion.2.at_ref, bf16[4,64,2048]{2,1,0:T(8,128)(2,1)} %all-to-all-done.1.b0, bf16[4,64,2048]{2,1,0:T(8,128)(2,1)} %collective-permute-done.5.b1, bf16[4,64,2048]{2,1,0:T(8,128)(2,1)} %copy-done.38, bf16[4,64,2048]{2,1,0:T(8,128)(2,1)} %copy-done.39), custom_call_target="tpu_custom_call" | custom-call | flops 3449999872 | bytes 1024 | tf_op jit(solution)/shard_map/place/pallas_call | solution.py:76
  109.1 10.1 %project.1 = (bf16[3,768,1024]{2,1,0:T(8,128)(2,1)}, bf16[3,768,1024]{2,1,0:T(8,128)(2,1)}, bf16[3,256,512]{2,1,0:T(8,128)(2,1)}) custom-call(bf16[3,192,1024]{2,1,0:T(8,128)(2,1)} %fusion.17.comp, bf16[3,64,1024]{2,1,0:T(8,128)(2,1)} %fusion.24.fresh, bf16[3,256,1024]{2,1,0:T(8,128)(2,1)} %get-tuple-element.261.mem.normed_mem, ...), custom_call_target="tpu_custom_call" | custom-call | flops 57500000256 | bytes 1024 | tf_op jit(solution)/shard_map/project/pallas_call | solution.py:198
  120.3 5.9 %position_table.1.table.refs_12_ = bf16[1536,512]{1,0:T(8,128)(2,1)} custom-call(s32[11]{0:T(128)} %pad_add_fusion.1.at, bf16[1792,1024]{1,0:T(8,128)(2,1)} %constant.69.clone.steps.refs_9_, bf16[1024,2048]{1,0:T(8,128)(2,1)} %bitcast.135), custom_call_target="tpu_custom_call" | custom-call | flops 23000000512 | bytes 1024 | tf_op jit(solution)/shard_map/position_table/pallas_call | solution.py:742
  127.4 8.9 %attend.3 = (bf16[256,512]{1,0:T(8,128)(2,1)}, bf16[4,256,1536]{2,1,0:T(8,128)(2,1)}) custom-call(s32[11]{0:T(128)} %pad_add_fusion.1.at, bf16[3,256,512]{2,1,0:T(8,128)(2,1)} %get-tuple-element.132.q.refs_7_, bf16[3,768,1024]{2,1,0:T(8,128)(2,1)} %get-tuple-element.126.k_own.v_own.refs_8_.refs_10_, ...), custom_call_target="tpu_custom_call" | custom-call | flops 23000000512 | bytes 1024 | tf_op jit(solution)/shard_map/attend/pallas_call | solution.py:258
  136.4 8.8 %attend.4 = (bf16[256,512]{1,0:T(8,128)(2,1)}, bf16[4,256,1536]{2,1,0:T(8,128)(2,1)}) custom-call(s32[11]{0:T(128)} %pad_add_fusion.1.at, bf16[3,256,512]{2,1,0:T(8,128)(2,1)} %get-tuple-element.132.q.refs_7_, bf16[3,768,1024]{2,1,0:T(8,128)(2,1)} %get-tuple-element.126.k_own.v_own.refs_8_.refs_10_, ...), custom_call_target="tpu_custom_call" | custom-call | flops 23000000512 | bytes 1024 | tf_op jit(solution)/shard_map/attend/pallas_call | solution.py:258
  147.3 9.3 %attend.5 = (bf16[256,512]{1,0:T(8,128)(2,1)}, bf16[4,256,1536]{2,1,0:T(8,128)(2,1)}) custom-call(s32[11]{0:T(128)} %pad_add_fusion.1.at, bf16[3,256,512]{2,1,0:T(8,128)(2,1)} %get-tuple-element.132.q.refs_7_, bf16[3,768,1024]{2,1,0:T(8,128)(2,1)} %get-tuple-element.126.k_own.v_own.refs_8_.refs_10_, ...), custom_call_target="tpu_custom_call" | custom-call | flops 23000000512 | bytes 1024 | tf_op jit(solution)/shard_map/attend/pallas_call | solution.py:258
  156.7 8.2 %collective-permute-done.11.refs_5_ = bf16[256,512]{1,0:T(8,128)(2,1)S(1)} collective-permute-done((bf16[256,512]{1,0:T(8,128)(2,1)}, bf16[256,512]{1,0:T(8,128)(2,1)S(1)}, u32[]{:S(2)}, u32[]{:S(2)}) %collective-permute-start.11) | collective-permute-done | bytes 262176 | tf_op jit(solution)/shard_map/ppermute | solution.py:26
  165.6 24.8 %feed_forward.1 = (f32[768,1024]{1,0:T(8,128)}, bf16[768,1024]{1,0:T(8,128)(2,1)}, bf16[768,1024]{1,0:T(8,128)(2,1)}, bf16[768,2048]{1,0:T(8,128)(2,1)}, bf16[76...) custom-call(s32[11]{0:T(128)} %pad_add_fusion.1.at, ...), custom_call_target="tpu_custom_call" | custom-call | flops 57500000256 | bytes 1024 | tf_op jit(solution)/shard_map/feed_forward/pallas_call | solution.py:411
  190.8 13.2 %grad_ffn.1 = bf16[1024,4096]{1,0:T(8,128)(2,1)} custom-call(bf16[768,1024]{1,0:T(8,128)(2,1)} %get-tuple-element.141.n2, bf16[768,2048]{1,0:T(8,128)(2,1)} %get-tuple-element.142.gpre, bf16[768,1024]{1,0:T(8,128)(2,1)} %get-tuple-element.159.go.refs_3_, bf16[768,2048]{1,0:T(8,128)(2,1)} %get-tuple-element.143.act), custom_call_target="tpu_custom_call" | custom-call | flops 34500001792 | bytes 1024 | tf_op jit(solution)/shard_map/grad_ffn/pallas_call | solution.py:790
  206.9 16.5 %attend_back.3 = (f32[256,1024]{1,0:T(8,128)}, bf16[256,1024]{1,0:T(8,128)(2,1)}, f32[8,1024]{1,0:T(8,128)}, bf16[256,512]{1,0:T(8,128)(2,1)}, bf16[2,768,512]{2...) custom-call(s32[11]{0:T(128)} %pad_add_fusion.1.at, ...), custom_call_target="tpu_custom_call" | custom-call | flops 57500000256 | bytes 1024 | tf_op jit(solution)/shard_map/attend_back/pallas_call | solution.py:538
  224.2 16.9 %attend_back.4 = (f32[256,1024]{1,0:T(8,128)}, bf16[256,1024]{1,0:T(8,128)(2,1)}, f32[8,1024]{1,0:T(8,128)}, bf16[256,512]{1,0:T(8,128)(2,1)}, bf16[2,768,512]{2...) custom-call(s32[11]{0:T(128)} %pad_add_fusion.1.at, ...), custom_call_target="tpu_custom_call" | custom-call | flops 57500000256 | bytes 1024 | tf_op jit(solution)/shard_map/attend_back/pallas_call | solution.py:538
  242.9 7.5 %rows_back.3 = (bf16[768,1024]{1,0:T(8,128)(2,1)}, bf16[448,1024]{1,0:T(8,128)(2,1)}, bf16[64,1024]{1,0:T(8,128)(2,1)}, f32[8,1024]{1,0:T(8,128)}) custom-call(bf16[2,768,512]{2,1,0:T(8,128)(2,1)} %get-tuple-element.155.keep, bf16[2,768,512]{2,1,0:T(8,128)(2,1)} %copy-done.37, bf16[256,512]{1,0:T(8,128)(2,1)} %get-tuple-element.182.gq.refs_0_, ...), custom_call_target="tpu_custom_call" | custom-call | flops 3449999872 | bytes 1024 | tf_op jit(solution)/shard_map/rows_back/pallas_call | solution.py:618
  250.4 16.6 %attend_back.5 = (f32[256,1024]{1,0:T(8,128)}, bf16[256,1024]{1,0:T(8,128)(2,1)}, f32[8,1024]{1,0:T(8,128)}, bf16[256,512]{1,0:T(8,128)(2,1)}, bf16[2,768,512]{2...) custom-call(s32[11]{0:T(128)} %pad_add_fusion.1.at, ...), custom_call_target="tpu_custom_call" | custom-call | flops 57500000256 | bytes 1024 | tf_op jit(solution)/shard_map/attend_back/pallas_call | solution.py:538
  271.1 7.7 %rows_back.4 = (bf16[768,1024]{1,0:T(8,128)(2,1)}, bf16[448,1024]{1,0:T(8,128)(2,1)}, bf16[64,1024]{1,0:T(8,128)(2,1)}, f32[8,1024]{1,0:T(8,128)}) custom-call(bf16[2,768,512]{2,1,0:T(8,128)(2,1)} %get-tuple-element.167.keep, bf16[2,768,512]{2,1,0:T(8,128)(2,1)} %copy-done.35, bf16[256,512]{1,0:T(8,128)(2,1)} %get-tuple-element.169.gq.refs_1_, ...), custom_call_target="tpu_custom_call" | custom-call | flops 3449999872 | bytes 1024 | tf_op jit(solution)/shard_map/rows_back/pallas_call | solution.py:618
  280.9 7.5 %rows_back.5 = (bf16[768,1024]{1,0:T(8,128)(2,1)}, bf16[448,1024]{1,0:T(8,128)(2,1)}, bf16[64,1024]{1,0:T(8,128)(2,1)}, f32[8,1024]{1,0:T(8,128)}) custom-call(bf16[2,768,512]{2,1,0:T(8,128)(2,1)} %get-tuple-element.165.keep, bf16[2,768,512]{2,1,0:T(8,128)(2,1)} %copy-done.36, bf16[256,512]{1,0:T(8,128)(2,1)} %get-tuple-element.171.gq.refs_2_, ...), custom_call_target="tpu_custom_call" | custom-call | flops 3449999872 | bytes 1024 | tf_op jit(solution)/shard_map/rows_back/pallas_call | solution.py:618
  288.4 4.9 %collective-permute-done.24.refs_1_ = bf16[64,1024]{1,0:T(8,128)(2,1)S(1)} collective-permute-done((bf16[64,1024]{1,0:T(8,128)(2,1)S(1)}, bf16[64,1024]{1,0:T(8,128)(2,1)S(1)}, u32[]{:S(2)}, u32[]{:S(2)}) %collective-permute-start.24) | collective-permute-done | bytes 131104 | tf_op jit(solution)/shard_map/ppermute | solution.py:26
  296.3 10.5 %grad_rest.1.refs_3_ = bf16[1024,2560]{1,0:T(8,128)(2,1)} custom-call(s32[11]{0:T(128)} %pad_add_fusion.1.at, bf16[3,768,1024]{2,1,0:T(8,128)(2,1)} %get-tuple-element.191.normed, bf16[256,512]{1,0:T(8,128)(2,1)} %get-tuple-element.182.gq.refs_0_, bf16[256,512]{1,0:T(8,128)(2,1)} %get-tuple-element.169.gq.refs_1_, ...), custom_call_target="tpu_custom_call" | custom-call | flops 9200000000 | bytes 1024 | tf_op jit(solution)/shard_map/grad_rest/pallas_call | solution.py:864
  310.4 5.0 %grad_conv.1 = (bf16[512,1536]{1,0:T(8,128)(2,1)}, bf16[512,1536]{1,0:T(8,128)(2,1)}) custom-call(s32[11]{0:T(128)} %pad_add_fusion.1.at, bf16[192,3072]{1,0:T(8,128)(2,1)} %reshape.146.taps, bf16[192,1024]{1,0:T(8,128)(2,1)} %get-tuple-element.188.fresh), custom_call_target="tpu_custom_call" | custom-call | flops 4600000000 | bytes 1024 | tf_op jit(solution)/shard_map/grad_conv/pallas_call | solution.py:895
  315.4 9.9 %grad_kv.1 = bf16[1024,2560]{1,0:T(8,128)(2,1)} custom-call(bf16[2304,1024]{1,0:T(8,128)(2,1)} %bitcast.133, bf16[768,1024]{1,0:T(8,128)(2,1)} %get-tuple-element.192.refs_0_, bf16[768,1024]{1,0:T(8,128)(2,1)} %get-tuple-element.193.refs_1_, bf16[768,1024]{1,0:T(8,128)(2,1)} %get-tuple-element.194.refs_2_, ...), custom_call_target="tpu_custom_call", output_to_operand_aliasing={{}: (4, {})} | custom-call | flops 9200000000 | bytes 1024 | tf_op jit(solution)/shard_map/grad_kv/pallas_call | solution.py:816
  332.8 16.2 %collective-permute-done.27 = bf16[4,64,1536]{2,1,0:T(8,128)(2,1)S(1)} collective-permute-done((bf16[4,64,1536]{2,1,0:T(8,128)(2,1)S(1)}, bf16[4,64,1536]{2,1,0:T(8,128)(2,1)S(1)}, u32[]{:S(2)}, u32[]{:S(2)}) %collective-permute-start.27) | collective-permute-done | bytes 786464 | tf_op jit(solution)/shard_map/ppermute | solution.py:26
  356.9 4.6 %context_back.3 = (f32[3,192,1024]{2,1,0:T(8,128)}, f32[3,256,1024]{2,1,0:T(8,128)}, f32[8,1024]{1,0:T(8,128)}) custom-call(bf16[448,1024]{1,0:T(8,128)(2,1)} %get-tuple-element.158.refs_0_, bf16[448,1024]{1,0:T(8,128)(2,1)} %collective-permute-done.23.refs_1_, bf16[3,192,1024]{2,1,0:T(8,128)(2,1)} %refs_2_.5, bf16[3,256,1024]{2,1,0:T(8,128)(2,1)} %refs_3_.5, ...), custom_call_target="tpu_custom_call" | custom-call | flops 3449999872 | bytes 1024 | tf_op jit(solution)/shard_map/context_back/pallas_call | solution.py:680
  361.5 11.5 %collective-permute-done.22.refs_1_ = bf16[448,1024]{1,0:T(8,128)(2,1)} collective-permute-done((bf16[448,1024]{1,0:T(8,128)(2,1)}, bf16[448,1024]{1,0:T(8,128)(2,1)}, u32[]{:S(2)}, u32[]{:S(2)}) %collective-permute-start.22) | collective-permute-done | bytes 917536 | tf_op jit(solution)/shard_map/ppermute | solution.py:26
  373.0 4.6 %context_back.4 = (f32[3,192,1024]{2,1,0:T(8,128)}, f32[3,256,1024]{2,1,0:T(8,128)}, f32[8,1024]{1,0:T(8,128)}) custom-call(bf16[448,1024]{1,0:T(8,128)(2,1)} %get-tuple-element.176.refs_0_, bf16[448,1024]{1,0:T(8,128)(2,1)} %collective-permute-done.22.refs_1_, bf16[3,192,1024]{2,1,0:T(8,128)(2,1)} %refs_2_.5, ...), custom_call_target="tpu_custom_call", output_to_operand_aliasing={{0}: (6, {}), {1}: (7, {})} | custom-call | flops 3449999872 | bytes 1024 | tf_op jit(solution)/shard_map/context_back/pallas_call | solution.py:680
  377.6 15.6 %all-to-all-done.2 = bf16[4,64,1536]{2,1,0:T(8,128)(2,1)S(1)} async-done(((bf16[4,64,1536]{2,1,0:T(8,128)(2,1)}), bf16[4,64,1536]{2,1,0:T(8,128)(2,1)S(1)}, u32[]{:S(2)}, u32[]{:S(2)}) %all-to-all-start.2) | async-done | bytes 786464 | tf_op jit(solution)/shard_map/all_to_all | solution.py:36
  394.1 4.7 %context_back.5 = (f32[3,192,1024]{2,1,0:T(8,128)}, f32[3,256,1024]{2,1,0:T(8,128)}, f32[8,1024]{1,0:T(8,128)}) custom-call(bf16[448,1024]{1,0:T(8,128)(2,1)} %get-tuple-element.174.refs_0_, bf16[448,1024]{1,0:T(8,128)(2,1)} %copy-done.40, bf16[3,192,1024]{2,1,0:T(8,128)(2,1)} %refs_2_.5, ...), custom_call_target="tpu_custom_call", output_to_operand_aliasing={{0}: (6, {}), {1}: (7, {})} | custom-call | flops 3449999872 | bytes 1024 | tf_op jit(solution)/shard_map/context_back/pallas_call | solution.py:680
  409.3 4.4 %collective-permute-done.32 = f32[72,128]{1,0:T(8,128)S(1)} collective-permute-done((f32[72,128]{1,0:T(8,128)S(1)}, f32[72,128]{1,0:T(8,128)S(1)}, u32[]{:S(2)}, u32[]{:S(2)}) %collective-permute-start.32) | collective-permute-done | bytes 36896 | tf_op jit(solution)/shard_map/ppermute | solution.py:26
  (253 shorter events, 101.5 us)
Async XLA Ops:
  7.2 13.8 %collective-permute-start = (bf16[64,512]{1,0:T(8,128)(2,1)}, bf16[64,512]{1,0:T(8,128)(2,1)}, u32[]{:S(2)}, u32[]{:S(2)}) collective-permute-start(bf16[64,512]{1,0:T(8,128)(2,1)} %bitcast.98), channel_id=1, source_target_pairs={{0,1},{1,0},{2,3},{3,2},{4,5},{5,4},{6,7},{7,6},{8,9},{9,8},{10,11... | collective-permute-start | bytes 196616 | tf_op jit(solution)/shard_map/ppermute | solution.py:26
  12.1 24.9 %all-to-all-start = ((bf16[4,64,1536]{2,1,0:T(8,128)(2,1)}), bf16[4,64,1536]{2,1,0:T(8,128)(2,1)}, u32[]{:S(2)}, u32[]{:S(2)}) async-start(bf16[4,64,1536]{2,1,0:T(8,128)(2,1)} %broadcast_in_dim.18), calls=%async_computation | async-start | bytes 1572864 | tf_op jit(solution)/shard_map/all_to_all | solution.py:36
  38.1 29.5 %all-to-all-start.1 = ((bf16[4,64,2048]{2,1,0:T(8,128)(2,1)}), bf16[4,64,2048]{2,1,0:T(8,128)(2,1)}, u32[]{:S(2)}, u32[]{:S(2)}) async-start(bf16[4,64,2048]{2,1,0:T(8,128)(2,1)} %broadcast_in_dim.20), calls=%async_computation.1 | async-start | bytes 2097152 | tf_op jit(solution)/shard_map/all_to_all | solution.py:36
  42.4 122.5 %all-gather.2.cloned.1.call-start = ((), (), s32[]{:S(2)}) async-start(), calls=%async_computation.5 | async-start | bytes 11141120 | tf_op jit(solution)/shard_map/all_gather | solution.py:1023
  42.4 18.9 %collective-permute-start.1 = (bf16[4,64,1536]{2,1,0:T(8,128)(2,1)}, bf16[4,64,1536]{2,1,0:T(8,128)(2,1)}, u32[]{:S(2)}, u32[]{:S(2)}) collective-permute-start(bf16[4,64,1536]{2,1,0:T(8,128)(2,1)} %all-to-all-done.b0), channel_id=1, source_target_pairs={{0,4},{4,0},{8,12},{12,8},{16,20},{20,16},{24,28},{28,24},{1,5},{5... | collective-permute-start | bytes 2359304 | tf_op jit(solution)/shard_map/ppermute | solution.py:26
  47.9 23.3 %collective-permute-start.2 = (bf16[4,64,1536]{2,1,0:T(8,128)(2,1)}, bf16[4,64,1536]{2,1,0:T(8,128)(2,1)S(1)}, u32[]{:S(2)}, u32[]{:S(2)}) collective-permute-start(bf16[4,64,1536]{2,1,0:T(8,128)(2,1)} %all-to-all-done.b0), channel_id=1, source_target_pairs={{0,2},{2,0},{1,3},{3,1},{4,6},{6,4},{5,7},{7,5},{8,10},{10,8},{9,1... | collective-permute-start | bytes 2359304 | tf_op jit(solution)/shard_map/ppermute | solution.py:26
  61.3 9.9 %collective-permute-start.3 = (bf16[4,64,1536]{2,1,0:T(8,128)(2,1)}, bf16[4,64,1536]{2,1,0:T(8,128)(2,1)}, u32[]{:S(2)}, u32[]{:S(2)}) collective-permute-start(bf16[4,64,1536]{2,1,0:T(8,128)(2,1)} %collective-permute-done.1.b1), channel_id=1, source_target_pairs={{0,2},{2,0},{1,3},{3,1},{4,6},{6,4},{5,7},{7,5},{8,10},{10,8},{9,1... | collective-permute-start | bytes 2359304 | tf_op jit(solution)/shard_map/ppermute | solution.py:26
  62.3 253.1 %reduce-scatter.3.cloned.1.call-start = ((), (), s32[]{:S(2)}) async-start(), calls=%async_computation.6 | async-start | bytes 8912896 | tf_op jit(solution)/shard_map/reduce_scatter | solution.py:1080
  67.7 31.4 %collective-permute-start.5 = (bf16[4,64,2048]{2,1,0:T(8,128)(2,1)}, bf16[4,64,2048]{2,1,0:T(8,128)(2,1)}, u32[]{:S(2)}, u32[]{:S(2)}) collective-permute-start(bf16[4,64,2048]{2,1,0:T(8,128)(2,1)} %all-to-all-done.1.b0), channel_id=1, source_target_pairs={{0,4},{4,0},{8,12},{12,8},{16,20},{20,16},{24,28},{28,24},{1,5},{5... | collective-permute-start | bytes 3145736 | tf_op jit(solution)/shard_map/ppermute | solution.py:26
  81.7 17.5 %collective-permute-start.4 = (bf16[3,64,512]{2,1,0:T(8,128)(2,1)S(1)}, bf16[3,64,512]{2,1,0:T(8,128)(2,1)S(1)}, u32[]{:S(2)}, u32[]{:S(2)}) collective-permute-start(bf16[3,64,512]{2,1,0:T(8,128)(2,1)S(1)} %bitcast.91), channel_id=1, source_target_pairs={{0,1},{1,0},{2,3},{3,2},{4,5},{5,4},{6,7},{7,6},{8,9},{9,8},{10,11... | collective-permute-start | bytes 589832 | tf_op jit(solution)/shard_map/ppermute | solution.py:26
  84.0 16.8 %collective-permute-start.6 = (bf16[4,64,2048]{2,1,0:T(8,128)(2,1)}, bf16[4,64,2048]{2,1,0:T(8,128)(2,1)S(1)}, u32[]{:S(2)}, u32[]{:S(2)}) collective-permute-start(bf16[4,64,2048]{2,1,0:T(8,128)(2,1)} %all-to-all-done.1.b0), channel_id=1, source_target_pairs={{0,2},{2,0},{1,3},{3,1},{4,6},{6,4},{5,7},{7,5},{8,10},{10,8},{9,1... | collective-permute-start | bytes 3145736 | tf_op jit(solution)/shard_map/ppermute | solution.py:26
  136.3 11.0 %collective-permute-start.9 = (bf16[256,512]{1,0:T(8,128)(2,1)}, bf16[256,512]{1,0:T(8,128)(2,1)S(1)}, u32[]{:S(2)}, u32[]{:S(2)}) collective-permute-start(bf16[256,512]{1,0:T(8,128)(2,1)} %get-tuple-element.129.refs_0_.refs_6_), channel_id=1, source_target_pairs={{0,1},{1,0},{2,3},{3,2},{4,5},{5,4},{6,7},{7,6},{8,9},{9,8},{10,11... | collective-permute-start | bytes 786440 | tf_op jit(solution)/shard_map/ppermute | solution.py:26
  145.2 11.5 %collective-permute-start.10 = (bf16[256,512]{1,0:T(8,128)(2,1)}, bf16[256,512]{1,0:T(8,128)(2,1)S(1)}, u32[]{:S(2)}, u32[]{:S(2)}) collective-permute-start(bf16[256,512]{1,0:T(8,128)(2,1)} %get-tuple-element.131.refs_2_.refs_7_), channel_id=1, source_target_pairs={{0,1},{1,0},{2,3},{3,2},{4,5},{5,4},{6,7},{7,6},{8,9},{9,8},{10,11... | collective-permute-start | bytes 786440 | tf_op jit(solution)/shard_map/ppermute | solution.py:26
  190.4 13.6 %collective-permute-start.12 = (bf16[256,1024]{1,0:T(8,128)(2,1)}, bf16[256,1024]{1,0:T(8,128)(2,1)S(1)}, u32[]{:S(2)}, u32[]{:S(2)}) collective-permute-start(bf16[256,1024]{1,0:T(8,128)(2,1)} %get-tuple-element.138.refs_0_), channel_id=1, source_target_pairs={{0,1},{1,0},{2,3},{3,2},{4,5},{5,4},{6,7},{7,6},{8,9},{9,8},{10,11... | collective-permute-start | bytes 1572872 | tf_op jit(solution)/shard_map/ppermute | solution.py:26
  204.0 221.1 %reduce-scatter.5.cloned.1.call-start = ((), (), s32[]{:S(2)}) async-start(), calls=%async_computation.7 | async-start | bytes 5570560 | tf_op jit(solution)/shard_map/reduce_scatter | solution.py:1149
  205.1 18.3 %collective-permute-start.13 = (bf16[256,1024]{1,0:T(8,128)(2,1)S(1)}, bf16[256,1024]{1,0:T(8,128)(2,1)S(1)}, u32[]{:S(2)}, u32[]{:S(2)}) collective-permute-start(bf16[256,1024]{1,0:T(8,128)(2,1)S(1)} %copy-done.43), channel_id=1, source_target_pairs={{0,1},{1,0},{2,3},{3,2},{4,5},{5,4},{6,7},{7,6},{8,9},{9,8},{10,11... | collective-permute-start | bytes 1572872 | tf_op jit(solution)/shard_map/ppermute | solution.py:26
  223.4 18.4 %collective-permute-start.16 = (bf16[2,768,512]{2,1,0:T(8,128)(2,1)}, bf16[2,768,512]{2,1,0:T(8,128)(2,1)S(1)}, u32[]{:S(2)}, u32[]{:S(2)}) collective-permute-start(bf16[2,768,512]{2,1,0:T(8,128)(2,1)} %get-tuple-element.156), channel_id=1, source_target_pairs={{0,2},{2,0},{1,3},{3,1},{4,6},{6,4},{5,7},{7,5},{8,10},{10,8},{9,1... | collective-permute-start | bytes 4718600 | tf_op jit(solution)/shard_map/ppermute | solution.py:26
  223.5 26.9 %collective-permute-start.15 = (bf16[256,1024]{1,0:T(8,128)(2,1)S(1)}, bf16[256,1024]{1,0:T(8,128)(2,1)}, u32[]{:S(2)}, u32[]{:S(2)}) collective-permute-start(bf16[256,1024]{1,0:T(8,128)(2,1)S(1)} %copy-done.42), channel_id=1, source_target_pairs={{0,1},{1,0},{2,3},{3,2},{4,5},{5,4},{6,7},{7,6},{8,9},{9,8},{10,11... | collective-permute-start | bytes 1572872 | tf_op jit(solution)/shard_map/ppermute | solution.py:26
  241.1 28.8 %collective-permute-start.19 = (bf16[2,768,512]{2,1,0:T(8,128)(2,1)}, bf16[2,768,512]{2,1,0:T(8,128)(2,1)S(1)}, u32[]{:S(2)}, u32[]{:S(2)}) collective-permute-start(bf16[2,768,512]{2,1,0:T(8,128)(2,1)} %get-tuple-element.168), channel_id=1, source_target_pairs={{0,2},{2,0},{1,3},{3,1},{4,6},{6,4},{5,7},{7,5},{8,10},{10,8},{9,1... | collective-permute-start | bytes 4718600 | tf_op jit(solution)/shard_map/ppermute | solution.py:26
  267.0 12.7 %collective-permute-start.18 = (bf16[2,768,512]{2,1,0:T(8,128)(2,1)}, bf16[2,768,512]{2,1,0:T(8,128)(2,1)S(1)}, u32[]{:S(2)}, u32[]{:S(2)}) collective-permute-start(bf16[2,768,512]{2,1,0:T(8,128)(2,1)} %get-tuple-element.166), channel_id=1, source_target_pairs={{0,2},{2,0},{1,3},{3,1},{4,6},{6,4},{5,7},{7,5},{8,10},{10,8},{9,1... | collective-permute-start | bytes 4718600 | tf_op jit(solution)/shard_map/ppermute | solution.py:26
  267.1 28.6 %collective-permute-start.23 = (bf16[448,1024]{1,0:T(8,128)(2,1)}, bf16[448,1024]{1,0:T(8,128)(2,1)}, u32[]{:S(2)}, u32[]{:S(2)}) collective-permute-start(bf16[448,1024]{1,0:T(8,128)(2,1)} %get-tuple-element.158.refs_0_), channel_id=1, source_target_pairs={{0,1},{1,0},{2,3},{3,2},{4,5},{5,4},{6,7},{7,6},{8,9},{9,8},{10,11... | collective-permute-start | bytes 2752520 | tf_op jit(solution)/shard_map/ppermute | solution.py:26
  268.8 24.6 %collective-permute-start.24 = (bf16[64,1024]{1,0:T(8,128)(2,1)S(1)}, bf16[64,1024]{1,0:T(8,128)(2,1)S(1)}, u32[]{:S(2)}, u32[]{:S(2)}) collective-permute-start(bf16[64,1024]{1,0:T(8,128)(2,1)S(1)} %copy-done.49), channel_id=1, source_target_pairs={{0,1},{1,0},{2,3},{3,2},{4,5},{5,4},{6,7},{7,6},{8,9},{9,8},{10,11... | collective-permute-start | bytes 393224 | tf_op jit(solution)/shard_map/ppermute | solution.py:26
  278.9 16.8 %collective-permute-start.25 = (bf16[64,1024]{1,0:T(8,128)(2,1)}, bf16[64,1024]{1,0:T(8,128)(2,1)S(1)}, u32[]{:S(2)}, u32[]{:S(2)}) collective-permute-start(bf16[64,1024]{1,0:T(8,128)(2,1)} %get-tuple-element.180.refs_2_), channel_id=1, source_target_pairs={{0,1},{1,0},{2,3},{3,2},{4,5},{5,4},{6,7},{7,6},{8,9},{9,8},{10,11... | collective-permute-start | bytes 393224 | tf_op jit(solution)/shard_map/ppermute | solution.py:26
  295.7 11.2 %collective-permute-start.20 = (bf16[64,1024]{1,0:T(8,128)(2,1)}, bf16[64,1024]{1,0:T(8,128)(2,1)S(1)}, u32[]{:S(2)}, u32[]{:S(2)}) collective-permute-start(bf16[64,1024]{1,0:T(8,128)(2,1)} %get-tuple-element.173.refs_4_), channel_id=1, source_target_pairs={{0,1},{1,0},{2,3},{3,2},{4,5},{5,4},{6,7},{7,6},{8,9},{9,8},{10,11... | collective-permute-start | bytes 393224 | tf_op jit(solution)/shard_map/ppermute | solution.py:26
  315.4 13.8 %collective-permute-start.26 = (bf16[512,1536]{1,0:T(8,128)(2,1)}, bf16[512,1536]{1,0:T(8,128)(2,1)S(1)}, u32[]{:S(2)}, u32[]{:S(2)}) collective-permute-start(bf16[512,1536]{1,0:T(8,128)(2,1)} %get-tuple-element.190), channel_id=1, source_target_pairs={{0,2},{2,0},{1,3},{3,1},{4,6},{6,4},{5,7},{7,5},{8,10},{10,8},{9,1... | collective-permute-start | bytes 4718600 | tf_op jit(solution)/shard_map/ppermute | solution.py:26
  327.1 93.3 %collective-permute-start.14 = (bf16[256,1024]{1,0:T(8,128)(2,1)}, bf16[256,1024]{1,0:T(8,128)(2,1)}, u32[]{:S(2)}, u32[]{:S(2)}) collective-permute-start(bf16[256,1024]{1,0:T(8,128)(2,1)} %get-tuple-element.151), channel_id=1, source_target_pairs={{0,1},{1,0},{2,3},{3,2},{4,5},{5,4},{6,7},{7,6},{8,9},{9,8},{10,11... | collective-permute-start | bytes 1572872 | tf_op jit(solution)/shard_map/ppermute | solution.py:26
  328.4 91.9 %collective-permute-start.17 = (bf16[256,1024]{1,0:T(8,128)(2,1)}, bf16[256,1024]{1,0:T(8,128)(2,1)}, u32[]{:S(2)}, u32[]{:S(2)}) collective-permute-start(bf16[256,1024]{1,0:T(8,128)(2,1)} %get-tuple-element.163), channel_id=1, source_target_pairs={{0,1},{1,0},{2,3},{3,2},{4,5},{5,4},{6,7},{7,6},{8,9},{9,8},{10,11... | collective-permute-start | bytes 1572872 | tf_op jit(solution)/shard_map/ppermute | solution.py:26
  329.4 19.6 %collective-permute-start.27 = (bf16[4,64,1536]{2,1,0:T(8,128)(2,1)S(1)}, bf16[4,64,1536]{2,1,0:T(8,128)(2,1)S(1)}, u32[]{:S(2)}, u32[]{:S(2)}) collective-permute-start(bf16[4,64,1536]{2,1,0:T(8,128)(2,1)S(1)} %fusion.25), channel_id=1, source_target_pairs={{0,4},{4,0},{8,12},{12,8},{16,20},{20,16},{24,28},{28,24},{1,5},{5... | collective-permute-start | bytes 2359304 | tf_op jit(solution)/shard_map/ppermute | solution.py:26
  331.4 41.6 %collective-permute-start.22 = (bf16[448,1024]{1,0:T(8,128)(2,1)}, bf16[448,1024]{1,0:T(8,128)(2,1)}, u32[]{:S(2)}, u32[]{:S(2)}) collective-permute-start(bf16[448,1024]{1,0:T(8,128)(2,1)} %get-tuple-element.176.refs_0_), channel_id=1, source_target_pairs={{0,1},{1,0},{2,3},{3,2},{4,5},{5,4},{6,7},{7,6},{8,9},{9,8},{10,11... | collective-permute-start | bytes 2752520 | tf_op jit(solution)/shard_map/ppermute | solution.py:26
  350.1 43.1 %all-to-all-start.2 = ((bf16[4,64,1536]{2,1,0:T(8,128)(2,1)}), bf16[4,64,1536]{2,1,0:T(8,128)(2,1)S(1)}, u32[]{:S(2)}, u32[]{:S(2)}) async-start(bf16[4,64,1536]{2,1,0:T(8,128)(2,1)} %fusion.18), calls=%async_computation.3 | async-start | bytes 1572864 | tf_op jit(solution)/shard_map/all_to_all | solution.py:36
  353.9 39.3 %collective-permute-start.21 = (bf16[448,1024]{1,0:T(8,128)(2,1)}, bf16[448,1024]{1,0:T(8,128)(2,1)S(1)}, u32[]{:S(2)}, u32[]{:S(2)}) collective-permute-start(bf16[448,1024]{1,0:T(8,128)(2,1)} %get-tuple-element.174.refs_0_), channel_id=1, source_target_pairs={{0,1},{1,0},{2,3},{3,2},{4,5},{5,4},{6,7},{7,6},{8,9},{9,8},{10,11... | collective-permute-start | bytes 2752520 | tf_op jit(solution)/shard_map/ppermute | solution.py:26
  408.1 13.6 %collective-permute-start.28 = (bf16[256,1024]{1,0:T(8,128)(2,1)S(1)}, bf16[256,1024]{1,0:T(8,128)(2,1)S(1)}, u32[]{:S(2)}, u32[]{:S(2)}) collective-permute-start(bf16[256,1024]{1,0:T(8,128)(2,1)S(1)} %copy-done.13), channel_id=1, source_target_pairs={{0,1},{1,0},{2,3},{3,2},{4,5},{5,4},{6,7},{7,6},{8,9},{9,8},{10,11... | collective-permute-start | bytes 1572872 | tf_op jit(solution)/shard_map/ppermute | solution.py:26
  (61 other events, 490.8 us)
Sparse Core Ops, SparseCore 0:
  62.4 91.6 all-gather.1
  204.1 105.0 reduce-scatter.2
  325.4 91.1 reduce-scatter.4

commit v4 on v3

--- a/solution.py
+++ b/solution.py
@@ -614,7 +614,7 @@
     local = keep.shape[1]
     comp, fresh, mem, seg = sizes
     kept = comp + seg
-    db = 256
+    db = D
     return pl.pallas_call(
         functools.partial(rows_kernel, sizes),
         grid=(D // db,),
@@ -779,7 +779,7 @@
 
 def grad_ffn(n2, gpre, go, act):
     rows, hidden = act.shape
-    hb = min(512, hidden)
+    hb = min(1024, hidden)
     steps = hidden // hb
 
     def block(first):

time: 439 us -> 436 us (level)
  transfers between devices with their start and end apart: 40 -> 40, of which waited for: 18 -> 19; matrix products, arithmetic and copies ran while one was open for 7% -> 7% of each run, Pallas kernels for 43% -> 42%
where the time goes in v4:
time: 436 us; the launch traced here: 432 us
  Pallas kernels  206 us (47%)
  waiting for transfers between devices  126 us (29%)
  starting transfers between devices  40.7 us (9%)
  other arithmetic  26.1 us (6%)
  local copies, waits for them, and re-layouts  17.7 us (4%)
  between operations  14.9 us (3%)
    ppermute x34, waiting for transfers between devices, swap(): return lax.ppermute(x, axis, [(i, i ^ step) for i in range(n)])  90.6 us
    pallas_call x3, Pallas kernels, attend_back(): pl.pallas_call(functools.partial(backward_kernel, sizes, len(twos), chain...  50.1 us
    all_to_all x3, waiting for transfers between devices, z_exchange(): return lax.all_to_all(x, 'dp', 0, 0, axis_index_groups=groups, tiled=True)  35.4 us
    ppermute x34, starting transfers between devices, swap(): return lax.ppermute(x, axis, [(i, i ^ step) for i in range(n)])  27.4 us
    pallas_call x3, Pallas kernels, attend(): pl.pallas_call(functools.partial(forward_kernel, b, sizes), grid_spec=plt...  27 us
    pallas_call x1, Pallas kernels, feed_forward(): pl.pallas_call(functools.partial(ffn_kernel, batch, len(atts) // batch, f...  24.8 us
    pallas_call x3, Pallas kernels, rows_back(): pl.pallas_call(functools.partial(rows_kernel, sizes), grid=(D // db,), in...  19.7 us
    pallas_call x3, Pallas kernels, context_back(): pl.pallas_call(functools.partial(context_kernel, sizes, len(grads), chain...  13.9 us
  transfers between devices with their start and end apart: 40, of which 19 were waited for; matrix products, arithmetic and copies ran while one was open for 7% of the time, Pallas kernels for 42%

profile of v4, /device:TPU:0, one launch (start us, length us, event | category | flops | bytes accessed | tf_op | source)
XLA Modules:
  0.0 431.7 jit_solution(15899931194036024333)
XLA Ops:
  12.1 5.0 %all-to-all-start = ((bf16[4,64,1536]{2,1,0:T(8,128)(2,1)}), bf16[4,64,1536]{2,1,0:T(8,128)(2,1)}, u32[]{:S(2)}, u32[]{:S(2)}) async-start(bf16[4,64,1536]{2,1,0:T(8,128)(2,1)} %broadcast_in_dim.18), calls=%async_computation | async-start | bytes 1572864 | tf_op jit(solution)/shard_map/all_to_all | solution.py:36
  21.8 15.2 %all-to-all-done.b0 = bf16[4,64,1536]{2,1,0:T(8,128)(2,1)} async-done(((bf16[4,64,1536]{2,1,0:T(8,128)(2,1)}), bf16[4,64,1536]{2,1,0:T(8,128)(2,1)}, u32[]{:S(2)}, u32[]{:S(2)}) %all-to-all-start) | async-done | bytes 786464 | tf_op jit(solution)/shard_map/all_to_all | solution.py:36
  47.9 13.4 %collective-permute-done.1.b1 = bf16[4,64,1536]{2,1,0:T(8,128)(2,1)} collective-permute-done((bf16[4,64,1536]{2,1,0:T(8,128)(2,1)}, bf16[4,64,1536]{2,1,0:T(8,128)(2,1)}, u32[]{:S(2)}, u32[]{:S(2)}) %collective-permute-start.1) | collective-permute-done | bytes 786464 | tf_op jit(solution)/shard_map/ppermute | solution.py:26
  63.0 4.6 %all-to-all-done.1.b0 = bf16[4,64,2048]{2,1,0:T(8,128)(2,1)} async-done(((bf16[4,64,2048]{2,1,0:T(8,128)(2,1)}), bf16[4,64,2048]{2,1,0:T(8,128)(2,1)}, u32[]{:S(2)}, u32[]{:S(2)}) %all-to-all-start.1) | async-done | bytes 1048608 | tf_op jit(solution)/shard_map/all_to_all | solution.py:36
  76.3 4.3 compress.1
  84.0 15.1 %collective-permute-done.5.b1 = bf16[4,64,2048]{2,1,0:T(8,128)(2,1)} collective-permute-done((bf16[4,64,2048]{2,1,0:T(8,128)(2,1)}, bf16[4,64,2048]{2,1,0:T(8,128)(2,1)}, u32[]{:S(2)}, u32[]{:S(2)}) %collective-permute-start.5) | collective-permute-done | bytes 1048608 | tf_op jit(solution)/shard_map/ppermute | solution.py:26
  102.9 6.1 %place.3 = bf16[4,2,2,64,2048]{4,3,2,1,0:T(8,128)(2,1)} custom-call(s32[2]{0:T(128)} %pad_add_fusion.2.at_ref, bf16[4,64,2048]{2,1,0:T(8,128)(2,1)} %all-to-all-done.1.b0, bf16[4,64,2048]{2,1,0:T(8,128)(2,1)} %collective-permute-done.5.b1, bf16[4,64,2048]{2,1,0:T(8,128)(2,1)} %copy-done.38, bf16[4,64,2048]{2,1,0:T(8,128)(2,1)} %copy-done.39), custom_call_target="tpu_custom_call" | custom-call | flops 3449999872 | bytes 1024 | tf_op jit(solution)/shard_map/place/pallas_call | solution.py:76
  109.1 10.1 %project.1 = (bf16[3,768,1024]{2,1,0:T(8,128)(2,1)}, bf16[3,768,1024]{2,1,0:T(8,128)(2,1)}, bf16[3,256,512]{2,1,0:T(8,128)(2,1)}) custom-call(bf16[3,192,1024]{2,1,0:T(8,128)(2,1)} %fusion.17.comp, bf16[3,64,1024]{2,1,0:T(8,128)(2,1)} %fusion.24.fresh, bf16[3,256,1024]{2,1,0:T(8,128)(2,1)} %get-tuple-element.261.mem.normed_mem, ...), custom_call_target="tpu_custom_call" | custom-call | flops 57500000256 | bytes 1024 | tf_op jit(solution)/shard_map/project/pallas_call | solution.py:198
  120.3 5.9 %position_table.1.table.refs_12_ = bf16[1536,512]{1,0:T(8,128)(2,1)} custom-call(s32[11]{0:T(128)} %pad_add_fusion.1.at, bf16[1792,1024]{1,0:T(8,128)(2,1)} %constant.69.clone.steps.refs_9_, bf16[1024,2048]{1,0:T(8,128)(2,1)} %bitcast.135), custom_call_target="tpu_custom_call" | custom-call | flops 23000000512 | bytes 1024 | tf_op jit(solution)/shard_map/position_table/pallas_call | solution.py:742
  127.4 8.9 %attend.3 = (bf16[256,512]{1,0:T(8,128)(2,1)}, bf16[4,256,1536]{2,1,0:T(8,128)(2,1)}) custom-call(s32[11]{0:T(128)} %pad_add_fusion.1.at, bf16[3,256,512]{2,1,0:T(8,128)(2,1)} %get-tuple-element.132.q.refs_7_, bf16[3,768,1024]{2,1,0:T(8,128)(2,1)} %get-tuple-element.126.k_own.v_own.refs_8_.refs_10_, ...), custom_call_target="tpu_custom_call" | custom-call | flops 23000000512 | bytes 1024 | tf_op jit(solution)/shard_map/attend/pallas_call | solution.py:258
  136.4 8.8 %attend.4 = (bf16[256,512]{1,0:T(8,128)(2,1)}, bf16[4,256,1536]{2,1,0:T(8,128)(2,1)}) custom-call(s32[11]{0:T(128)} %pad_add_fusion.1.at, bf16[3,256,512]{2,1,0:T(8,128)(2,1)} %get-tuple-element.132.q.refs_7_, bf16[3,768,1024]{2,1,0:T(8,128)(2,1)} %get-tuple-element.126.k_own.v_own.refs_8_.refs_10_, ...), custom_call_target="tpu_custom_call" | custom-call | flops 23000000512 | bytes 1024 | tf_op jit(solution)/shard_map/attend/pallas_call | solution.py:258
  147.3 9.3 %attend.5 = (bf16[256,512]{1,0:T(8,128)(2,1)}, bf16[4,256,1536]{2,1,0:T(8,128)(2,1)}) custom-call(s32[11]{0:T(128)} %pad_add_fusion.1.at, bf16[3,256,512]{2,1,0:T(8,128)(2,1)} %get-tuple-element.132.q.refs_7_, bf16[3,768,1024]{2,1,0:T(8,128)(2,1)} %get-tuple-element.126.k_own.v_own.refs_8_.refs_10_, ...), custom_call_target="tpu_custom_call" | custom-call | flops 23000000512 | bytes 1024 | tf_op jit(solution)/shard_map/attend/pallas_call | solution.py:258
  156.7 8.2 %collective-permute-done.11.refs_5_ = bf16[256,512]{1,0:T(8,128)(2,1)S(1)} collective-permute-done((bf16[256,512]{1,0:T(8,128)(2,1)}, bf16[256,512]{1,0:T(8,128)(2,1)S(1)}, u32[]{:S(2)}, u32[]{:S(2)}) %collective-permute-start.11) | collective-permute-done | bytes 262176 | tf_op jit(solution)/shard_map/ppermute | solution.py:26
  165.6 24.8 %feed_forward.1 = (f32[768,1024]{1,0:T(8,128)}, bf16[768,1024]{1,0:T(8,128)(2,1)}, bf16[768,1024]{1,0:T(8,128)(2,1)}, bf16[768,2048]{1,0:T(8,128)(2,1)}, bf16[76...) custom-call(s32[11]{0:T(128)} %pad_add_fusion.1.at, ...), custom_call_target="tpu_custom_call" | custom-call | flops 57500000256 | bytes 1024 | tf_op jit(solution)/shard_map/feed_forward/pallas_call | solution.py:411
  190.8 11.9 %grad_ffn.1 = bf16[1024,4096]{1,0:T(8,128)(2,1)} custom-call(bf16[768,1024]{1,0:T(8,128)(2,1)} %get-tuple-element.141.n2, bf16[768,2048]{1,0:T(8,128)(2,1)} %get-tuple-element.142.gpre, bf16[768,1024]{1,0:T(8,128)(2,1)} %get-tuple-element.159.go.refs_3_, bf16[768,2048]{1,0:T(8,128)(2,1)} %get-tuple-element.143.act), custom_call_target="tpu_custom_call" | custom-call | flops 34500001792 | bytes 1024 | tf_op jit(solution)/shard_map/grad_ffn/pallas_call | solution.py:790
  205.6 16.5 %attend_back.3 = (f32[256,1024]{1,0:T(8,128)}, bf16[256,1024]{1,0:T(8,128)(2,1)}, f32[8,1024]{1,0:T(8,128)}, bf16[256,512]{1,0:T(8,128)(2,1)}, bf16[2,768,512]{2...) custom-call(s32[11]{0:T(128)} %pad_add_fusion.1.at, ...), custom_call_target="tpu_custom_call" | custom-call | flops 57500000256 | bytes 1024 | tf_op jit(solution)/shard_map/attend_back/pallas_call | solution.py:538
  223.0 16.8 %attend_back.4 = (f32[256,1024]{1,0:T(8,128)}, bf16[256,1024]{1,0:T(8,128)(2,1)}, f32[8,1024]{1,0:T(8,128)}, bf16[256,512]{1,0:T(8,128)(2,1)}, bf16[2,768,512]{2...) custom-call(s32[11]{0:T(128)} %pad_add_fusion.1.at, ...), custom_call_target="tpu_custom_call" | custom-call | flops 57500000256 | bytes 1024 | tf_op jit(solution)/shard_map/attend_back/pallas_call | solution.py:538
  241.6 6.5 %rows_back.3 = (bf16[768,1024]{1,0:T(8,128)(2,1)}, bf16[448,1024]{1,0:T(8,128)(2,1)}, bf16[64,1024]{1,0:T(8,128)(2,1)}, f32[8,1024]{1,0:T(8,128)}) custom-call(bf16[2,768,512]{2,1,0:T(8,128)(2,1)} %get-tuple-element.155.keep, bf16[2,768,512]{2,1,0:T(8,128)(2,1)} %copy-done.37, bf16[256,512]{1,0:T(8,128)(2,1)} %get-tuple-element.182.gq.refs_0_, ...), custom_call_target="tpu_custom_call" | custom-call | flops 3449999872 | bytes 1024 | tf_op jit(solution)/shard_map/rows_back/pallas_call | solution.py:618
  248.2 16.8 %attend_back.5 = (f32[256,1024]{1,0:T(8,128)}, bf16[256,1024]{1,0:T(8,128)(2,1)}, f32[8,1024]{1,0:T(8,128)}, bf16[256,512]{1,0:T(8,128)(2,1)}, bf16[2,768,512]{2...) custom-call(s32[11]{0:T(128)} %pad_add_fusion.1.at, ...), custom_call_target="tpu_custom_call" | custom-call | flops 57500000256 | bytes 1024 | tf_op jit(solution)/shard_map/attend_back/pallas_call | solution.py:538
  269.1 6.6 %rows_back.4 = (bf16[768,1024]{1,0:T(8,128)(2,1)}, bf16[448,1024]{1,0:T(8,128)(2,1)}, bf16[64,1024]{1,0:T(8,128)(2,1)}, f32[8,1024]{1,0:T(8,128)}) custom-call(bf16[2,768,512]{2,1,0:T(8,128)(2,1)} %get-tuple-element.167.keep, bf16[2,768,512]{2,1,0:T(8,128)(2,1)} %copy-done.35, bf16[256,512]{1,0:T(8,128)(2,1)} %get-tuple-element.169.gq.refs_1_, ...), custom_call_target="tpu_custom_call" | custom-call | flops 3449999872 | bytes 1024 | tf_op jit(solution)/shard_map/rows_back/pallas_call | solution.py:618
  277.6 6.6 %rows_back.5 = (bf16[768,1024]{1,0:T(8,128)(2,1)}, bf16[448,1024]{1,0:T(8,128)(2,1)}, bf16[64,1024]{1,0:T(8,128)(2,1)}, f32[8,1024]{1,0:T(8,128)}) custom-call(bf16[2,768,512]{2,1,0:T(8,128)(2,1)} %get-tuple-element.165.keep, bf16[2,768,512]{2,1,0:T(8,128)(2,1)} %copy-done.36, bf16[256,512]{1,0:T(8,128)(2,1)} %get-tuple-element.171.gq.refs_2_, ...), custom_call_target="tpu_custom_call" | custom-call | flops 3449999872 | bytes 1024 | tf_op jit(solution)/shard_map/rows_back/pallas_call | solution.py:618
  284.3 7.0 %collective-permute-done.24.refs_1_ = bf16[64,1024]{1,0:T(8,128)(2,1)S(1)} collective-permute-done((bf16[64,1024]{1,0:T(8,128)(2,1)S(1)}, bf16[64,1024]{1,0:T(8,128)(2,1)S(1)}, u32[]{:S(2)}, u32[]{:S(2)}) %collective-permute-start.24) | collective-permute-done | bytes 131104 | tf_op jit(solution)/shard_map/ppermute | solution.py:26
  294.2 10.5 %grad_rest.1.refs_3_ = bf16[1024,2560]{1,0:T(8,128)(2,1)} custom-call(s32[11]{0:T(128)} %pad_add_fusion.1.at, bf16[3,768,1024]{2,1,0:T(8,128)(2,1)} %get-tuple-element.191.normed, bf16[256,512]{1,0:T(8,128)(2,1)} %get-tuple-element.182.gq.refs_0_, bf16[256,512]{1,0:T(8,128)(2,1)} %get-tuple-element.169.gq.refs_1_, ...), custom_call_target="tpu_custom_call" | custom-call | flops 9200000000 | bytes 1024 | tf_op jit(solution)/shard_map/grad_rest/pallas_call | solution.py:864
  308.3 5.0 %grad_conv.1 = (bf16[512,1536]{1,0:T(8,128)(2,1)}, bf16[512,1536]{1,0:T(8,128)(2,1)}) custom-call(s32[11]{0:T(128)} %pad_add_fusion.1.at, bf16[192,3072]{1,0:T(8,128)(2,1)} %reshape.146.taps, bf16[192,1024]{1,0:T(8,128)(2,1)} %get-tuple-element.188.fresh), custom_call_target="tpu_custom_call" | custom-call | flops 4600000000 | bytes 1024 | tf_op jit(solution)/shard_map/grad_conv/pallas_call | solution.py:895
  313.2 9.9 %grad_kv.1 = bf16[1024,2560]{1,0:T(8,128)(2,1)} custom-call(bf16[2304,1024]{1,0:T(8,128)(2,1)} %bitcast.133, bf16[768,1024]{1,0:T(8,128)(2,1)} %get-tuple-element.192.refs_0_, bf16[768,1024]{1,0:T(8,128)(2,1)} %get-tuple-element.193.refs_1_, bf16[768,1024]{1,0:T(8,128)(2,1)} %get-tuple-element.194.refs_2_, ...), custom_call_target="tpu_custom_call", output_to_operand_aliasing={{}: (4, {})} | custom-call | flops 9200000000 | bytes 1024 | tf_op jit(solution)/shard_map/grad_kv/pallas_call | solution.py:816
  330.7 16.2 %collective-permute-done.27 = bf16[4,64,1536]{2,1,0:T(8,128)(2,1)S(1)} collective-permute-done((bf16[4,64,1536]{2,1,0:T(8,128)(2,1)S(1)}, bf16[4,64,1536]{2,1,0:T(8,128)(2,1)S(1)}, u32[]{:S(2)}, u32[]{:S(2)}) %collective-permute-start.27) | collective-permute-done | bytes 786464 | tf_op jit(solution)/shard_map/ppermute | solution.py:26
  354.8 4.6 %context_back.3 = (f32[3,192,1024]{2,1,0:T(8,128)}, f32[3,256,1024]{2,1,0:T(8,128)}, f32[8,1024]{1,0:T(8,128)}) custom-call(bf16[448,1024]{1,0:T(8,128)(2,1)} %get-tuple-element.158.refs_0_, bf16[448,1024]{1,0:T(8,128)(2,1)} %collective-permute-done.23.refs_1_, bf16[3,192,1024]{2,1,0:T(8,128)(2,1)} %refs_2_.5, bf16[3,256,1024]{2,1,0:T(8,128)(2,1)} %refs_3_.5, ...), custom_call_target="tpu_custom_call" | custom-call | flops 3449999872 | bytes 1024 | tf_op jit(solution)/shard_map/context_back/pallas_call | solution.py:680
  359.4 11.5 %collective-permute-done.22.refs_1_ = bf16[448,1024]{1,0:T(8,128)(2,1)} collective-permute-done((bf16[448,1024]{1,0:T(8,128)(2,1)}, bf16[448,1024]{1,0:T(8,128)(2,1)}, u32[]{:S(2)}, u32[]{:S(2)}) %collective-permute-start.22) | collective-permute-done | bytes 917536 | tf_op jit(solution)/shard_map/ppermute | solution.py:26
  370.9 4.6 %context_back.4 = (f32[3,192,1024]{2,1,0:T(8,128)}, f32[3,256,1024]{2,1,0:T(8,128)}, f32[8,1024]{1,0:T(8,128)}) custom-call(bf16[448,1024]{1,0:T(8,128)(2,1)} %get-tuple-element.176.refs_0_, bf16[448,1024]{1,0:T(8,128)(2,1)} %collective-permute-done.22.refs_1_, bf16[3,192,1024]{2,1,0:T(8,128)(2,1)} %refs_2_.5, ...), custom_call_target="tpu_custom_call", output_to_operand_aliasing={{0}: (6, {}), {1}: (7, {})} | custom-call | flops 3449999872 | bytes 1024 | tf_op jit(solution)/shard_map/context_back/pallas_call | solution.py:680
  375.5 15.6 %all-to-all-done.2 = bf16[4,64,1536]{2,1,0:T(8,128)(2,1)S(1)} async-done(((bf16[4,64,1536]{2,1,0:T(8,128)(2,1)}), bf16[4,64,1536]{2,1,0:T(8,128)(2,1)S(1)}, u32[]{:S(2)}, u32[]{:S(2)}) %all-to-all-start.2) | async-done | bytes 786464 | tf_op jit(solution)/shard_map/all_to_all | solution.py:36
  392.0 4.7 %context_back.5 = (f32[3,192,1024]{2,1,0:T(8,128)}, f32[3,256,1024]{2,1,0:T(8,128)}, f32[8,1024]{1,0:T(8,128)}) custom-call(bf16[448,1024]{1,0:T(8,128)(2,1)} %get-tuple-element.174.refs_0_, bf16[448,1024]{1,0:T(8,128)(2,1)} %copy-done.40, bf16[3,192,1024]{2,1,0:T(8,128)(2,1)} %refs_2_.5, ...), custom_call_target="tpu_custom_call", output_to_operand_aliasing={{0}: (6, {}), {1}: (7, {})} | custom-call | flops 3449999872 | bytes 1024 | tf_op jit(solution)/shard_map/context_back/pallas_call | solution.py:680
  407.2 4.4 %collective-permute-done.32 = f32[72,128]{1,0:T(8,128)S(1)} collective-permute-done((f32[72,128]{1,0:T(8,128)S(1)}, f32[72,128]{1,0:T(8,128)S(1)}, u32[]{:S(2)}, u32[]{:S(2)}) %collective-permute-start.32) | collective-permute-done | bytes 36896 | tf_op jit(solution)/shard_map/ppermute | solution.py:26
  (253 shorter events, 101.4 us)
Async XLA Ops:
  7.2 13.8 %collective-permute-start = (bf16[64,512]{1,0:T(8,128)(2,1)}, bf16[64,512]{1,0:T(8,128)(2,1)}, u32[]{:S(2)}, u32[]{:S(2)}) collective-permute-start(bf16[64,512]{1,0:T(8,128)(2,1)} %bitcast.98), channel_id=1, source_target_pairs={{0,1},{1,0},{2,3},{3,2},{4,5},{5,4},{6,7},{7,6},{8,9},{9,8},{10,11... | collective-permute-start | bytes 196616 | tf_op jit(solution)/shard_map/ppermute | solution.py:26
  12.1 24.9 %all-to-all-start = ((bf16[4,64,1536]{2,1,0:T(8,128)(2,1)}), bf16[4,64,1536]{2,1,0:T(8,128)(2,1)}, u32[]{:S(2)}, u32[]{:S(2)}) async-start(bf16[4,64,1536]{2,1,0:T(8,128)(2,1)} %broadcast_in_dim.18), calls=%async_computation | async-start | bytes 1572864 | tf_op jit(solution)/shard_map/all_to_all | solution.py:36
  38.1 29.5 %all-to-all-start.1 = ((bf16[4,64,2048]{2,1,0:T(8,128)(2,1)}), bf16[4,64,2048]{2,1,0:T(8,128)(2,1)}, u32[]{:S(2)}, u32[]{:S(2)}) async-start(bf16[4,64,2048]{2,1,0:T(8,128)(2,1)} %broadcast_in_dim.20), calls=%async_computation.1 | async-start | bytes 2097152 | tf_op jit(solution)/shard_map/all_to_all | solution.py:36
  42.4 122.5 %all-gather.2.cloned.1.call-start = ((), (), s32[]{:S(2)}) async-start(), calls=%async_computation.5 | async-start | bytes 11141120 | tf_op jit(solution)/shard_map/all_gather | solution.py:1023
  42.4 18.9 %collective-permute-start.1 = (bf16[4,64,1536]{2,1,0:T(8,128)(2,1)}, bf16[4,64,1536]{2,1,0:T(8,128)(2,1)}, u32[]{:S(2)}, u32[]{:S(2)}) collective-permute-start(bf16[4,64,1536]{2,1,0:T(8,128)(2,1)} %all-to-all-done.b0), channel_id=1, source_target_pairs={{0,4},{4,0},{8,12},{12,8},{16,20},{20,16},{24,28},{28,24},{1,5},{5... | collective-permute-start | bytes 2359304 | tf_op jit(solution)/shard_map/ppermute | solution.py:26
  47.9 23.3 %collective-permute-start.2 = (bf16[4,64,1536]{2,1,0:T(8,128)(2,1)}, bf16[4,64,1536]{2,1,0:T(8,128)(2,1)S(1)}, u32[]{:S(2)}, u32[]{:S(2)}) collective-permute-start(bf16[4,64,1536]{2,1,0:T(8,128)(2,1)} %all-to-all-done.b0), channel_id=1, source_target_pairs={{0,2},{2,0},{1,3},{3,1},{4,6},{6,4},{5,7},{7,5},{8,10},{10,8},{9,1... | collective-permute-start | bytes 2359304 | tf_op jit(solution)/shard_map/ppermute | solution.py:26
  61.3 9.9 %collective-permute-start.3 = (bf16[4,64,1536]{2,1,0:T(8,128)(2,1)}, bf16[4,64,1536]{2,1,0:T(8,128)(2,1)}, u32[]{:S(2)}, u32[]{:S(2)}) collective-permute-start(bf16[4,64,1536]{2,1,0:T(8,128)(2,1)} %collective-permute-done.1.b1), channel_id=1, source_target_pairs={{0,2},{2,0},{1,3},{3,1},{4,6},{6,4},{5,7},{7,5},{8,10},{10,8},{9,1... | collective-permute-start | bytes 2359304 | tf_op jit(solution)/shard_map/ppermute | solution.py:26
  62.3 251.0 %reduce-scatter.3.cloned.1.call-start = ((), (), s32[]{:S(2)}) async-start(), calls=%async_computation.6 | async-start | bytes 8912896 | tf_op jit(solution)/shard_map/reduce_scatter | solution.py:1080
  67.7 31.4 %collective-permute-start.5 = (bf16[4,64,2048]{2,1,0:T(8,128)(2,1)}, bf16[4,64,2048]{2,1,0:T(8,128)(2,1)}, u32[]{:S(2)}, u32[]{:S(2)}) collective-permute-start(bf16[4,64,2048]{2,1,0:T(8,128)(2,1)} %all-to-all-done.1.b0), channel_id=1, source_target_pairs={{0,4},{4,0},{8,12},{12,8},{16,20},{20,16},{24,28},{28,24},{1,5},{5... | collective-permute-start | bytes 3145736 | tf_op jit(solution)/shard_map/ppermute | solution.py:26
  81.7 17.5 %collective-permute-start.4 = (bf16[3,64,512]{2,1,0:T(8,128)(2,1)S(1)}, bf16[3,64,512]{2,1,0:T(8,128)(2,1)S(1)}, u32[]{:S(2)}, u32[]{:S(2)}) collective-permute-start(bf16[3,64,512]{2,1,0:T(8,128)(2,1)S(1)} %bitcast.91), channel_id=1, source_target_pairs={{0,1},{1,0},{2,3},{3,2},{4,5},{5,4},{6,7},{7,6},{8,9},{9,8},{10,11... | collective-permute-start | bytes 589832 | tf_op jit(solution)/shard_map/ppermute | solution.py:26
  84.0 16.8 %collective-permute-start.6 = (bf16[4,64,2048]{2,1,0:T(8,128)(2,1)}, bf16[4,64,2048]{2,1,0:T(8,128)(2,1)S(1)}, u32[]{:S(2)}, u32[]{:S(2)}) collective-permute-start(bf16[4,64,2048]{2,1,0:T(8,128)(2,1)} %all-to-all-done.1.b0), channel_id=1, source_target_pairs={{0,2},{2,0},{1,3},{3,1},{4,6},{6,4},{5,7},{7,5},{8,10},{10,8},{9,1... | collective-permute-start | bytes 3145736 | tf_op jit(solution)/shard_map/ppermute | solution.py:26
  136.3 11.0 %collective-permute-start.9 = (bf16[256,512]{1,0:T(8,128)(2,1)}, bf16[256,512]{1,0:T(8,128)(2,1)S(1)}, u32[]{:S(2)}, u32[]{:S(2)}) collective-permute-start(bf16[256,512]{1,0:T(8,128)(2,1)} %get-tuple-element.129.refs_0_.refs_6_), channel_id=1, source_target_pairs={{0,1},{1,0},{2,3},{3,2},{4,5},{5,4},{6,7},{7,6},{8,9},{9,8},{10,11... | collective-permute-start | bytes 786440 | tf_op jit(solution)/shard_map/ppermute | solution.py:26
  145.2 11.5 %collective-permute-start.10 = (bf16[256,512]{1,0:T(8,128)(2,1)}, bf16[256,512]{1,0:T(8,128)(2,1)S(1)}, u32[]{:S(2)}, u32[]{:S(2)}) collective-permute-start(bf16[256,512]{1,0:T(8,128)(2,1)} %get-tuple-element.131.refs_2_.refs_7_), channel_id=1, source_target_pairs={{0,1},{1,0},{2,3},{3,2},{4,5},{5,4},{6,7},{7,6},{8,9},{9,8},{10,11... | collective-permute-start | bytes 786440 | tf_op jit(solution)/shard_map/ppermute | solution.py:26
  190.4 13.1 %collective-permute-start.12 = (bf16[256,1024]{1,0:T(8,128)(2,1)}, bf16[256,1024]{1,0:T(8,128)(2,1)S(1)}, u32[]{:S(2)}, u32[]{:S(2)}) collective-permute-start(bf16[256,1024]{1,0:T(8,128)(2,1)} %get-tuple-element.138.refs_0_), channel_id=1, source_target_pairs={{0,1},{1,0},{2,3},{3,2},{4,5},{5,4},{6,7},{7,6},{8,9},{9,8},{10,11... | collective-permute-start | bytes 1572872 | tf_op jit(solution)/shard_map/ppermute | solution.py:26
  202.7 220.2 %reduce-scatter.5.cloned.1.call-start = ((), (), s32[]{:S(2)}) async-start(), calls=%async_computation.7 | async-start | bytes 5570560 | tf_op jit(solution)/shard_map/reduce_scatter | solution.py:1149
  203.7 18.5 %collective-permute-start.13 = (bf16[256,1024]{1,0:T(8,128)(2,1)S(1)}, bf16[256,1024]{1,0:T(8,128)(2,1)S(1)}, u32[]{:S(2)}, u32[]{:S(2)}) collective-permute-start(bf16[256,1024]{1,0:T(8,128)(2,1)S(1)} %copy-done.43), channel_id=1, source_target_pairs={{0,1},{1,0},{2,3},{3,2},{4,5},{5,4},{6,7},{7,6},{8,9},{9,8},{10,11... | collective-permute-start | bytes 1572872 | tf_op jit(solution)/shard_map/ppermute | solution.py:26
  222.1 18.4 %collective-permute-start.16 = (bf16[2,768,512]{2,1,0:T(8,128)(2,1)}, bf16[2,768,512]{2,1,0:T(8,128)(2,1)S(1)}, u32[]{:S(2)}, u32[]{:S(2)}) collective-permute-start(bf16[2,768,512]{2,1,0:T(8,128)(2,1)} %get-tuple-element.156), channel_id=1, source_target_pairs={{0,2},{2,0},{1,3},{3,1},{4,6},{6,4},{5,7},{7,5},{8,10},{10,8},{9,1... | collective-permute-start | bytes 4718600 | tf_op jit(solution)/shard_map/ppermute | solution.py:26
  222.2 25.9 %collective-permute-start.15 = (bf16[256,1024]{1,0:T(8,128)(2,1)S(1)}, bf16[256,1024]{1,0:T(8,128)(2,1)}, u32[]{:S(2)}, u32[]{:S(2)}) collective-permute-start(bf16[256,1024]{1,0:T(8,128)(2,1)S(1)} %copy-done.42), channel_id=1, source_target_pairs={{0,1},{1,0},{2,3},{3,2},{4,5},{5,4},{6,7},{7,6},{8,9},{9,8},{10,11... | collective-permute-start | bytes 1572872 | tf_op jit(solution)/shard_map/ppermute | solution.py:26
  239.8 28.1 %collective-permute-start.19 = (bf16[2,768,512]{2,1,0:T(8,128)(2,1)}, bf16[2,768,512]{2,1,0:T(8,128)(2,1)S(1)}, u32[]{:S(2)}, u32[]{:S(2)}) collective-permute-start(bf16[2,768,512]{2,1,0:T(8,128)(2,1)} %get-tuple-element.168), channel_id=1, source_target_pairs={{0,2},{2,0},{1,3},{3,1},{4,6},{6,4},{5,7},{7,5},{8,10},{10,8},{9,1... | collective-permute-start | bytes 4718600 | tf_op jit(solution)/shard_map/ppermute | solution.py:26
  265.0 11.5 %collective-permute-start.18 = (bf16[2,768,512]{2,1,0:T(8,128)(2,1)}, bf16[2,768,512]{2,1,0:T(8,128)(2,1)S(1)}, u32[]{:S(2)}, u32[]{:S(2)}) collective-permute-start(bf16[2,768,512]{2,1,0:T(8,128)(2,1)} %get-tuple-element.166), channel_id=1, source_target_pairs={{0,2},{2,0},{1,3},{3,1},{4,6},{6,4},{5,7},{7,5},{8,10},{10,8},{9,1... | collective-permute-start | bytes 4718600 | tf_op jit(solution)/shard_map/ppermute | solution.py:26
  265.0 28.6 %collective-permute-start.23 = (bf16[448,1024]{1,0:T(8,128)(2,1)}, bf16[448,1024]{1,0:T(8,128)(2,1)}, u32[]{:S(2)}, u32[]{:S(2)}) collective-permute-start(bf16[448,1024]{1,0:T(8,128)(2,1)} %get-tuple-element.158.refs_0_), channel_id=1, source_target_pairs={{0,1},{1,0},{2,3},{3,2},{4,5},{5,4},{6,7},{7,6},{8,9},{9,8},{10,11... | collective-permute-start | bytes 2752520 | tf_op jit(solution)/shard_map/ppermute | solution.py:26
  266.7 24.6 %collective-permute-start.24 = (bf16[64,1024]{1,0:T(8,128)(2,1)S(1)}, bf16[64,1024]{1,0:T(8,128)(2,1)S(1)}, u32[]{:S(2)}, u32[]{:S(2)}) collective-permute-start(bf16[64,1024]{1,0:T(8,128)(2,1)S(1)} %copy-done.49), channel_id=1, source_target_pairs={{0,1},{1,0},{2,3},{3,2},{4,5},{5,4},{6,7},{7,6},{8,9},{9,8},{10,11... | collective-permute-start | bytes 393224 | tf_op jit(solution)/shard_map/ppermute | solution.py:26
  275.7 18.0 %collective-permute-start.25 = (bf16[64,1024]{1,0:T(8,128)(2,1)}, bf16[64,1024]{1,0:T(8,128)(2,1)S(1)}, u32[]{:S(2)}, u32[]{:S(2)}) collective-permute-start(bf16[64,1024]{1,0:T(8,128)(2,1)} %get-tuple-element.180.refs_2_), channel_id=1, source_target_pairs={{0,1},{1,0},{2,3},{3,2},{4,5},{5,4},{6,7},{7,6},{8,9},{9,8},{10,11... | collective-permute-start | bytes 393224 | tf_op jit(solution)/shard_map/ppermute | solution.py:26
  293.6 11.1 %collective-permute-start.20 = (bf16[64,1024]{1,0:T(8,128)(2,1)}, bf16[64,1024]{1,0:T(8,128)(2,1)S(1)}, u32[]{:S(2)}, u32[]{:S(2)}) collective-permute-start(bf16[64,1024]{1,0:T(8,128)(2,1)} %get-tuple-element.173.refs_4_), channel_id=1, source_target_pairs={{0,1},{1,0},{2,3},{3,2},{4,5},{5,4},{6,7},{7,6},{8,9},{9,8},{10,11... | collective-permute-start | bytes 393224 | tf_op jit(solution)/shard_map/ppermute | solution.py:26
  313.2 13.8 %collective-permute-start.26 = (bf16[512,1536]{1,0:T(8,128)(2,1)}, bf16[512,1536]{1,0:T(8,128)(2,1)S(1)}, u32[]{:S(2)}, u32[]{:S(2)}) collective-permute-start(bf16[512,1536]{1,0:T(8,128)(2,1)} %get-tuple-element.190), channel_id=1, source_target_pairs={{0,2},{2,0},{1,3},{3,1},{4,6},{6,4},{5,7},{7,5},{8,10},{10,8},{9,1... | collective-permute-start | bytes 4718600 | tf_op jit(solution)/shard_map/ppermute | solution.py:26
  325.0 93.3 %collective-permute-start.14 = (bf16[256,1024]{1,0:T(8,128)(2,1)}, bf16[256,1024]{1,0:T(8,128)(2,1)}, u32[]{:S(2)}, u32[]{:S(2)}) collective-permute-start(bf16[256,1024]{1,0:T(8,128)(2,1)} %get-tuple-element.151), channel_id=1, source_target_pairs={{0,1},{1,0},{2,3},{3,2},{4,5},{5,4},{6,7},{7,6},{8,9},{9,8},{10,11... | collective-permute-start | bytes 1572872 | tf_op jit(solution)/shard_map/ppermute | solution.py:26
  326.4 91.9 %collective-permute-start.17 = (bf16[256,1024]{1,0:T(8,128)(2,1)}, bf16[256,1024]{1,0:T(8,128)(2,1)}, u32[]{:S(2)}, u32[]{:S(2)}) collective-permute-start(bf16[256,1024]{1,0:T(8,128)(2,1)} %get-tuple-element.163), channel_id=1, source_target_pairs={{0,1},{1,0},{2,3},{3,2},{4,5},{5,4},{6,7},{7,6},{8,9},{9,8},{10,11... | collective-permute-start | bytes 1572872 | tf_op jit(solution)/shard_map/ppermute | solution.py:26
  327.2 19.6 %collective-permute-start.27 = (bf16[4,64,1536]{2,1,0:T(8,128)(2,1)S(1)}, bf16[4,64,1536]{2,1,0:T(8,128)(2,1)S(1)}, u32[]{:S(2)}, u32[]{:S(2)}) collective-permute-start(bf16[4,64,1536]{2,1,0:T(8,128)(2,1)S(1)} %fusion.25), channel_id=1, source_target_pairs={{0,4},{4,0},{8,12},{12,8},{16,20},{20,16},{24,28},{28,24},{1,5},{5... | collective-permute-start | bytes 2359304 | tf_op jit(solution)/shard_map/ppermute | solution.py:26
  329.3 41.6 %collective-permute-start.22 = (bf16[448,1024]{1,0:T(8,128)(2,1)}, bf16[448,1024]{1,0:T(8,128)(2,1)}, u32[]{:S(2)}, u32[]{:S(2)}) collective-permute-start(bf16[448,1024]{1,0:T(8,128)(2,1)} %get-tuple-element.176.refs_0_), channel_id=1, source_target_pairs={{0,1},{1,0},{2,3},{3,2},{4,5},{5,4},{6,7},{7,6},{8,9},{9,8},{10,11... | collective-permute-start | bytes 2752520 | tf_op jit(solution)/shard_map/ppermute | solution.py:26
  348.0 43.0 %all-to-all-start.2 = ((bf16[4,64,1536]{2,1,0:T(8,128)(2,1)}), bf16[4,64,1536]{2,1,0:T(8,128)(2,1)S(1)}, u32[]{:S(2)}, u32[]{:S(2)}) async-start(bf16[4,64,1536]{2,1,0:T(8,128)(2,1)} %fusion.18), calls=%async_computation.3 | async-start | bytes 1572864 | tf_op jit(solution)/shard_map/all_to_all | solution.py:36
  351.8 39.3 %collective-permute-start.21 = (bf16[448,1024]{1,0:T(8,128)(2,1)}, bf16[448,1024]{1,0:T(8,128)(2,1)S(1)}, u32[]{:S(2)}, u32[]{:S(2)}) collective-permute-start(bf16[448,1024]{1,0:T(8,128)(2,1)} %get-tuple-element.174.refs_0_), channel_id=1, source_target_pairs={{0,1},{1,0},{2,3},{3,2},{4,5},{5,4},{6,7},{7,6},{8,9},{9,8},{10,11... | collective-permute-start | bytes 2752520 | tf_op jit(solution)/shard_map/ppermute | solution.py:26
  405.9 13.6 %collective-permute-start.28 = (bf16[256,1024]{1,0:T(8,128)(2,1)S(1)}, bf16[256,1024]{1,0:T(8,128)(2,1)S(1)}, u32[]{:S(2)}, u32[]{:S(2)}) collective-permute-start(bf16[256,1024]{1,0:T(8,128)(2,1)S(1)} %copy-done.13), channel_id=1, source_target_pairs={{0,1},{1,0},{2,3},{3,2},{4,5},{5,4},{6,7},{7,6},{8,9},{9,8},{10,11... | collective-permute-start | bytes 1572872 | tf_op jit(solution)/shard_map/ppermute | solution.py:26
  (61 other events, 490.5 us)
Sparse Core Ops, SparseCore 0:
  62.4 91.6 all-gather.1
  202.8 105.0 reduce-scatter.2
  323.3 91.1 reduce-scatter.4
